TPU v7x, 128 devices: a whole 4x4x4 slice. The times are simulated.
128 devices in a mesh: dp: 16 (over z, y), tensor: 8 (over x, core).
Axes of the slice: x: 4, y: 4, z: 4, core: 2. Of those that a mesh axis runs over, the one named last changes fastest.
Arguments:
- attention: bfloat16 [4096, 8192], P('dp', 'tensor'), may hold values from -6 to 6
- residual: bfloat16 [4096, 8192], P('dp', 'tensor'), may hold values from -6 to 6
- out_proj: bfloat16 [8192, 8192], P(None, 'tensor'), may hold values from -0.0625 to 0.0625
- norm_gain: bfloat16 [8192], P('tensor'), may hold values from 0.25 to 1.75
- cotangent: bfloat16 [4096, 8192], P('dp', 'tensor'), may hold values from -6 to 6
- rewards: float32 [64], P('dp'), may hold values from -8 to 8
- group_ids: int32 [64], P('dp'), may hold values from 0 to 3, as said below
- kept_flags: int32 [64], P('dp'), may hold values 0 or 1
- lengths: int32 [16, 4], P('dp'), may hold values from 1 to 128, 256 in all within a row
Outputs:
- grad_attention: bfloat16 [4096, 8192], P('dp', 'tensor')
- grad_out_proj: bfloat16 [8192, 8192], P('dp', 'tensor')
- grad_residual: bfloat16 [4096, 8192], P('dp', 'tensor')
- grad_gain: float32 [8192], P('tensor')
Inputs may be any that keep to these rules, and one draw needn't show every extreme that they name: `lengths`: row d lists the sequences of dp index d; each row sums to 256. `group_ids`: every group is named by exactly 16 sequences.
All inputs are finite; a program needn't handle non-finite values. No bound on the sum of `kept_flags` on one device may be relied on, other than what follows from the above.
Results may differ from a plain program's by a relative error of at most 0.0049.
Values may be sent and summed in bfloat16 or wider, within the bound.
No kernel may reach another device: no remote copies, remote signals or barrier semaphores. Data moves between devices by JAX's collectives and lax.ppermute only.
A program may use at most 192 MiB of HBM per device.

v0:
```python
import jax
import jax.numpy as jnp
from jax import lax
from jax.sharding import PartitionSpec as P


def token_scaling(rewards, group_ids, kept_flags, lengths, rows):
    dp_count = lax.axis_size("dp")
    groups = rewards.shape[0] * dp_count // 16
    seqs_here = rewards.shape[0]
    kept = kept_flags.astype(jnp.float32)
    onehot = (group_ids[None, :] == jnp.arange(groups, dtype=jnp.int32)[:, None]).astype(
        jnp.float32
    )
    stats = jnp.stack(
        [
            jnp.sum(onehot * kept[None, :], axis=1),
            jnp.sum(onehot * (kept * rewards)[None, :], axis=1),
            jnp.sum(onehot * (kept * rewards * rewards)[None, :], axis=1),
        ]
    )
    local_tokens = jnp.sum(kept * lengths[0].astype(jnp.float32))
    stats, kept_tokens = lax.psum((stats, local_tokens), "dp")
    group_mean = stats[1] / jnp.maximum(stats[0], 1.0)
    group_var = stats[2] / jnp.maximum(stats[0], 1.0) - group_mean * group_mean
    group_scale = jnp.sqrt(jnp.maximum(group_var, 1.0))
    seq_mean = jnp.sum(onehot * group_mean[:, None], axis=0)
    seq_scale = jnp.sum(onehot * group_scale[:, None], axis=0)
    advantage = (rewards - seq_mean) / seq_scale
    seq_coef = -advantage * kept * float(rows * dp_count) / jnp.maximum(kept_tokens, 1.0)
    ends = jnp.cumsum(lengths[0])
    position = jnp.arange(rows, dtype=jnp.int32)
    segment = jnp.sum((position[:, None] >= ends[None, :]).astype(jnp.int32), axis=1)
    picks = (segment[:, None] == jnp.arange(seqs_here, dtype=jnp.int32)[None, :]).astype(
        jnp.float32
    )
    return jnp.sum(picks * seq_coef[None, :], axis=1)


def norm_backward(upstream, hidden, gain_value, square_total, inner_total, width):
    inverse = lax.rsqrt(square_total / width + 1e-06)
    scaled = upstream * gain_value[None, :]
    grad_hidden = (
        inverse[:, None] * scaled
        - hidden * (inverse * inverse * inverse * inner_total / width)[:, None]
    )
    return (grad_hidden, inverse)


def shards(
    attention, residual, out_proj, norm_gain, cotangent, rewards, group_ids, kept_flags, lengths
):
    rows = attention.shape[0]
    width = out_proj.shape[0]
    token_coef = token_scaling(rewards, group_ids, kept_flags, lengths, rows)
    projected = lax.dot_general(
        attention, out_proj, (((1,), (1,)), ((), ())), preferred_element_type=jnp.float32
    )
    upstream = token_coef[:, None] * cotangent.astype(jnp.float32)
    hidden = residual.astype(jnp.float32) + lax.psum_scatter(
        projected, "tensor", scatter_dimension=1, tiled=True
    )
    square_total = lax.psum(jnp.sum(hidden * hidden, axis=1), "tensor")
    gain_value = norm_gain.astype(jnp.float32)
    inner_total = lax.psum(jnp.sum(upstream * gain_value[None, :] * hidden, axis=1), "tensor")
    grad_hidden, inverse = norm_backward(
        upstream, hidden, gain_value, square_total, inner_total, width
    )
    grad_residual = grad_hidden.astype(jnp.bfloat16)
    gain_term = jnp.sum(upstream * hidden * inverse[:, None], axis=0)
    grad_full = lax.all_gather(grad_residual, "tensor", axis=1, tiled=True)
    grad_gain = lax.psum(gain_term, "dp")
    grad_attention = jnp.dot(grad_full, out_proj, preferred_element_type=jnp.float32).astype(
        jnp.bfloat16
    )
    summed = lax.psum_scatter(
        lax.dot_general(
            grad_full, attention, (((0,), (0,)), ((), ())), preferred_element_type=jnp.float32
        ),
        "dp",
        scatter_dimension=0,
        tiled=True,
    )
    grad_out_proj = summed.astype(jnp.bfloat16)
    return (grad_attention, grad_out_proj, grad_residual, grad_gain)


def solution(mesh):
    return jax.shard_map(
        shards,
        mesh=mesh,
        in_specs=(
            P("dp", "tensor"),
            P("dp", "tensor"),
            P(None, "tensor"),
            P("tensor"),
            P("dp", "tensor"),
            P("dp"),
            P("dp"),
            P("dp"),
            P("dp", None),
        ),
        out_specs=(P("dp", "tensor"), P("dp", "tensor"), P("dp", "tensor"), P("tensor")),
        check_vma=False,
    )
```

profile of v0, /device:TPU:1, one launch (start us, length us, event | category | flops | bytes accessed | tf_op | source)
XLA Modules:
  0.0 365.0 jit_solution(15690753474159045759)
XLA Ops:
  7.2 0.0 copy-start
  7.2 0.0 reduce-scatter.3.cloned.1.call-start
  7.2 1.0 copy-done
  8.2 18.8 %fusion.9 = f32[256,8192]{1,0:T(8,128)} fusion(bf16[256,1024]{1,0:T(8,128)(2,1)S(1)} %copy-done, bf16[8192,1024]{1,0:T(8,128)(2,1)} %param.11), kind=kOutput, calls=%fused_computation.36 | convolution fusion | flops 4294967296 | bytes 25690112 | tf_op jit(solution)/shard_map/dot_general | solution.py:56
  27.1 0.0 copy-start.6
  27.1 0.0 copy-start.7
  27.1 0.0 copy-start.8
  27.1 0.0 copy-start.5
  27.1 0.0 copy-start.4
  27.1 0.0 copy-start.2
  27.1 0.0 copy-start.3
  27.1 0.0 reduce-scatter.3.cloned.1.call-update
  27.1 0.0 all-gather.2.cloned.1.call-start
  27.2 0.5 copy-done.6
  27.7 0.0 copy-done.7
  27.7 0.0 copy-done.8
  27.7 0.6 convert_multiply_fusion.1
  28.3 0.0 copy-done.5
  28.3 0.1 select_reduce_fusion.5
  28.5 36.2 %all-reduce = (f32[3,4]{1,0:T(4,128)S(1)}, f32[]{:T(128)}) all-reduce(f32[3,4]{1,0:T(4,128)S(1)} %pad_maximum_fusion, f32[]{:T(128)} %get-tuple-element.17), channel_id=1, replica_groups=mesh['dp'=16,'tensor'=8] {'dp'}, use_global_device_ids=true, to_apply=%region_8.0 | all-reduce | flops 13 | bytes 104 | tf_op jit(solution)/shard_map/psum | solution.py:23
  64.7 0.0 copy-done.4
  64.7 0.2 reduce-window.8
  65.5 0.1 convert_reduce_fusion
  65.6 0.1 select_reduce_fusion.2
  65.7 0.1 select_reduce_fusion
  65.8 16.6 %reduce-scatter.3.cloned.1.call-done = f32[256,1024]{1,0:T(8,128)} async-done(((f32[256,8192]{1,0:T(8,128)}), f32[256,1024]{1,0:T(8,128)}) %reduce-scatter.3.cloned.1.call-update) | async-done | bytes 1048592 | tf_op jit(solution)/shard_map/reduce_scatter | solution.py:60
  82.4 0.0 copy-done.2
  82.4 1.4 multiply_reduce_fusion.2
  83.8 13.0 %psum.35 = f32[256]{0:T(256)S(1)} all-reduce(f32[256]{0:T(256)S(1)} %multiply_reduce_fusion.2), channel_id=1, replica_groups=mesh['dp'=16,'tensor'=8] {'tensor'}, use_global_device_ids=true, to_apply=%region_2.0 | all-reduce | flops 256 | bytes 2048 | tf_op jit(solution)/shard_map/psum | solution.py:63
  96.8 0.0 copy-done.3
  96.8 1.7 multiply_reduce_fusion
  98.5 12.8 %psum.38 = f32[256]{0:T(256)S(1)} all-reduce(f32[256]{0:T(256)S(1)} %get-tuple-element.5), channel_id=1, replica_groups=mesh['dp'=16,'tensor'=8] {'tensor'}, use_global_device_ids=true, to_apply=%region_15.16 | all-reduce | flops 256 | bytes 2048 | tf_op jit(solution)/shard_map/psum | solution.py:65
  111.4 2.4 subtract_convert_fusion
  113.7 0.0 all-gather.2.cloned.1.call-update
  113.8 0.0 reduce-scatter.5.cloned.1.call-start
  113.8 31.5 %all-gather.2.cloned.1.call-done = bf16[256,8192]{1,0:T(8,128)(2,1)} async-done(((bf16[256,1024]{1,0:T(8,128)(2,1)}), bf16[256,8192]{1,0:T(8,128)(2,1)}) %all-gather.2.cloned.1.call-update) | async-done | bytes 4194320 | tf_op jit(solution)/shard_map/all_gather | solution.py:71
  145.3 15.4 %fusion.10 = f32[8192,1024]{1,0:T(8,128)} fusion(bf16[256,8192]{1,0:T(8,128)(2,1)} %all-gather.2.cloned.1.call-done, bf16[256,1024]{1,0:T(8,128)(2,1)S(1)} %copy-done), kind=kOutput, calls=%fused_computation.37 | convolution fusion | flops 4294967296 | bytes 38273024 | tf_op jit(solution)/shard_map/dot_general | solution.py:77
  160.6 0.0 reduce-scatter.5.cloned.1.call-update
  160.7 34.8 %psum.39 = f32[1024]{0:T(1024)} all-reduce(f32[1024]{0:T(1024)S(1)} %get-tuple-element.4), channel_id=1, replica_groups=mesh['dp'=16,'tensor'=8] {'dp'}, use_global_device_ids=true, to_apply=%region_18.19 | all-reduce | flops 1024 | bytes 8192 | tf_op jit(solution)/shard_map/psum | solution.py:72
  195.5 0.0 copy-start.1
  195.5 12.8 %convolution_convert_fusion = bf16[256,1024]{1,0:T(8,128)(2,1)} fusion(bf16[256,8192]{1,0:T(8,128)(2,1)} %all-gather.2.cloned.1.call-done, bf16[8192,1024]{1,0:T(8,128)(2,1)} %param.11), kind=kOutput, calls=%fused_computation | convolution fusion | flops 4295229440 | bytes 21495808 | tf_op jit(solution)/shard_map/dot_general | solution.py:73
  208.4 147.3 %reduce-scatter.5.cloned.1.call-done = f32[512,1024]{1,0:T(8,128)} async-done(((f32[8192,1024]{1,0:T(8,128)}), f32[512,1024]{1,0:T(8,128)}) %reduce-scatter.5.cloned.1.call-update) | async-done | bytes 2097168 | tf_op jit(solution)/shard_map/reduce_scatter | solution.py:76
  355.7 2.7 convert_element_type.41
  358.4 0.0 copy-done.1
  (7 shorter events, 0.1 us)
Async XLA Ops:
  7.2 1.1 copy-start
  7.2 75.2 %reduce-scatter.3.cloned.1.call-start = ((), (), s32[]{:S(2)}) async-start(), calls=%async_computation.2 | async-start | bytes 9437184 | tf_op jit(solution)/shard_map/reduce_scatter | solution.py:60
  27.1 0.7 copy-start.6
  27.1 0.7 copy-start.7
  27.1 0.7 copy-start.8
  27.1 1.3 copy-start.5
  27.1 37.6 %copy-start.4 = (bf16[1024]{0:T(1024)(128)(2,1)S(1)}, bf16[1024]{0:T(1024)(128)(2,1)}, u32[]{:S(2)}) copy-start(bf16[1024]{0:T(1024)(128)(2,1)} %param.12) | copy-start | bytes 6148
  27.1 55.3 %copy-start.2 = (bf16[256,1024]{1,0:T(8,128)(2,1)S(1)}, bf16[256,1024]{1,0:T(8,128)(2,1)}, u32[]{:S(2)}) copy-start(bf16[256,1024]{1,0:T(8,128)(2,1)} %param.10) | copy-start | bytes 1572868
  27.1 69.7 %copy-start.3 = (bf16[256,1024]{1,0:T(8,128)(2,1)S(1)}, bf16[256,1024]{1,0:T(8,128)(2,1)}, u32[]{:S(2)}) copy-start(bf16[256,1024]{1,0:T(8,128)(2,1)} %param.13) | copy-start | bytes 1572868
  27.1 118.1 %all-gather.2.cloned.1.call-start = ((), (), s32[]{:S(2)}) async-start(), calls=%async_computation.3 | async-start | bytes 4718592 | tf_op jit(solution)/shard_map/all_gather | solution.py:71
  113.8 241.9 %reduce-scatter.5.cloned.1.call-start = ((), (), s32[]{:S(2)}) async-start(), calls=%async_computation.4 | async-start | bytes 35651584 | tf_op jit(solution)/shard_map/reduce_scatter | solution.py:76
  195.5 162.9 %copy-start.1 = (bf16[256,1024]{1,0:T(8,128)(2,1)S(1)}, bf16[256,1024]{1,0:T(8,128)(2,1)}, u32[]{:S(2)}) copy-start(bf16[256,1024]{1,0:T(8,128)(2,1)} %param.9) | copy-start | bytes 1572868
Sparse Core Ops, SparseCore 0:
  27.3 55.0 reduce-scatter.2
  113.9 31.3 all-gather.1
  160.8 194.8 reduce-scatter.4
where the time goes:
time: 365 us
  waiting for transfers between devices  195 us (53%)
  blocking collectives  96.8 us (27%)
  matrix products  47 us (13%)
  between operations  14.5 us (4%)
  other arithmetic  9.5 us (3%)
    reduce_scatter x1, waiting for transfers between devices, shards(): lax.psum_scatter(lax.dot_general(grad_full, attention, (((0,), (0,)), (()...  147 us
    psum x1, blocking collectives, token_scaling(): stats, kept_tokens = lax.psum((stats, local_tokens), 'dp')  36.2 us
    psum x1, blocking collectives, shards(): grad_gain = lax.psum(gain_term, 'dp')  34.8 us
    all_gather x1, waiting for transfers between devices, shards(): grad_full = lax.all_gather(grad_residual, 'tensor', axis=1, tiled=True)  31.5 us
    dot_general x1, matrix products, shards(): lax.dot_general(attention, out_proj, (((1,), (1,)), ((), ())), preferred_...  18.8 us
    reduce_scatter x1, waiting for transfers between devices, shards(): lax.psum_scatter(projected, 'tensor', scatter_dimension=1, tiled=True)  16.6 us
    dot_general x1, matrix products, shards(): lax.dot_general(grad_full, attention, (((0,), (0,)), ((), ())), preferred...  15.4 us
    psum x1, blocking collectives, shards(): square_total = lax.psum(jnp.sum(hidden * hidden, axis=1), 'tensor')  13 us
  transfers between devices with their start and end apart: 3, of which 3 were waited for; matrix products, arithmetic and copies ran while one was open for 4% of the time, Pallas kernels for 0%

commit v1 on v0

v1 whole, which is shorter than its diff:
```python
import functools

import jax
import jax.numpy as jnp
from jax import lax
from jax.experimental import pallas as pl
from jax.experimental.pallas import tpu as pltpu
from jax.sharding import PartitionSpec as P

BF = jnp.bfloat16
F32 = jnp.float32
LIMIT = 48 * 1024 * 1024
CORE_SWAP = [(t, t ^ 1) for t in range(8)]


def x_shift(k):
    return [(t, ((t // 2 + k) % 4) * 2 + t % 2) for t in range(8)]


def dp_shift(dz, dy):
    return [(d, ((d // 4 + dz) % 4) * 4 + (d % 4 + dy) % 4) for d in range(16)]


def plane_shift(stage, k):
    pairs = []
    for d in range(16):
        for t in range(8):
            z, y = d // 4, d % 4
            if (t % 2) == stage:
                z = (z + k) % 4
            else:
                y = (y + k) % 4
            pairs.append((d * 8 + t, (z * 4 + y) * 8 + t))
    return pairs


def swap(value):
    return lax.ppermute(value, "tensor", CORE_SWAP)


def params():
    return pltpu.CompilerParams(vmem_limit_bytes=LIMIT)


def partial_kernel(shifts, where, att, w, send, keep, buf, sems):
    x, c = where[2], where[3]
    step = buf.shape[1]
    count = 2 * len(shifts)

    def copy(n):
        i, own = n // 2, n % 2
        slot = i // 2
        shift = shifts[-1]
        for k in range(len(shifts) - 1):
            shift = jnp.where(slot == k, shifts[k], shift)
        piece = lax.rem(x + shift, 4) * 2 + jnp.where(own == 1, c, 1 - c)
        row = pl.multiple_of((piece * 2 + lax.rem(i, 2)) * step, step)
        return pltpu.make_async_copy(w.at[pl.ds(row, step)], buf.at[n], sems.at[n])

    @pl.loop(0, 2 * count)
    def _(n):
        copy(n).start()

    @pl.loop(0, count)
    def _(i):
        slot = i // 2
        columns = pl.ds(pl.multiple_of(lax.rem(i, 2) * step, step), step)
        dims = (((1,), (1,)), ((), ()))
        copy(2 * i).wait()
        send[slot, :, columns] = lax.dot_general(
            att[...], buf[2 * i], dims, preferred_element_type=F32
        ).astype(BF)
        copy(2 * i + 1).wait()
        keep[slot, :, columns] = lax.dot_general(
            att[...], buf[2 * i + 1], dims, preferred_element_type=F32
        )


def partial_products(where, attention, out_proj, shifts):
    rows, depth = attention.shape
    width = out_proj.shape[0] // 8
    step = width // 2
    slots = len(shifts)
    vmem = pl.BlockSpec(memory_space=pltpu.VMEM)
    return pl.pallas_call(
        functools.partial(partial_kernel, shifts),
        in_specs=[
            pl.BlockSpec(memory_space=pltpu.SMEM),
            vmem,
            pl.BlockSpec(memory_space=pl.ANY),
        ],
        out_specs=[vmem, vmem],
        out_shape=[
            jax.ShapeDtypeStruct((slots, rows, width), BF),
            jax.ShapeDtypeStruct((slots, rows, width), F32),
        ],
        scratch_shapes=[
            pltpu.VMEM((4 * slots, step, depth), BF),
            pltpu.SemaphoreType.DMA((4 * slots,)),
        ],
        compiler_params=params(),
        cost_estimate=pl.CostEstimate(
            flops=4 * slots * rows * depth * width,
            bytes_accessed=4 * slots * width * depth,
            transcendentals=0,
        ),
        name="partial",
    )(where, attention, out_proj)


def row_sums(value):
    rows, width = value.shape
    part = value[:, 0:128]
    for i in range(1, width // 128):
        part = part + value[:, i * 128 : (i + 1) * 128]
    return jnp.sum(part.T, axis=0, keepdims=True)


def hidden_kernel(keep, own, r1, r2, r3, residual, cot, gain, hidden, sums):
    h = keep[...] + own[...].astype(F32) + residual[...].astype(F32)
    h = h + r1[...].astype(F32) + r2[...].astype(F32) + r3[...].astype(F32)
    hidden[...] = h
    scaled = cot[...].astype(F32) * gain[...].astype(F32)
    first = row_sums(h * h)
    second = row_sums(scaled * h)
    sums[...] = jnp.concatenate([first, second, jnp.zeros((6, first.shape[1]), F32)], axis=0)


def hidden_call(keep, own, r1, r2, r3, residual, cot, gain):
    rows, width = keep.shape
    big = pl.BlockSpec((128, width), lambda i: (i, 0))
    return pl.pallas_call(
        hidden_kernel,
        grid=(rows // 128,),
        in_specs=[big] * 7 + [pl.BlockSpec((1, width), lambda i: (0, 0))],
        out_specs=[big, pl.BlockSpec((8, 128), lambda i: (0, i))],
        out_shape=[
            jax.ShapeDtypeStruct((rows, width), F32),
            jax.ShapeDtypeStruct((8, rows), F32),
        ],
        compiler_params=params(),
        cost_estimate=pl.CostEstimate(
            flops=12 * rows * width, bytes_accessed=20 * rows * width, transcendentals=0
        ),
        name="hidden",
    )(keep, own, r1, r2, r3, residual, cot, gain)


def column(row):
    return jnp.broadcast_to(row, (128, 128)).T


def spread(col, width):
    return jnp.concatenate([col] * (width // 128), axis=1)


def grad_kernel(features, hidden, cot, gain, s0, s1, s2, s3, coef, grad, gain_term):
    i = pl.program_id(0)
    width = hidden.shape[1]
    sums = s0[...] + s1[...] + s2[...] + s3[...]
    square, inner = sums[0:1, :], sums[1:2, :]
    inverse = lax.rsqrt(square / features + 1e-06)
    first = coef[...] * inverse
    second = coef[...] * (inverse * inverse * inverse * inner / features)
    first = spread(column(first), width)
    second = spread(column(second), width)
    h = hidden[...]
    c = cot[...].astype(F32)
    grad[...] = (first * (c * gain[...].astype(F32)) - h * second).astype(BF)
    term = jnp.sum(first * c * h, axis=0, keepdims=True)

    @pl.when(i == 0)
    def _():
        gain_term[...] = term

    @pl.when(i != 0)
    def _():
        gain_term[...] += term


def grad_call(features, hidden, cot, gain, s0, s1, s2, s3, coef):
    rows, width = hidden.shape
    big = pl.BlockSpec((128, width), lambda i: (i, 0))
    small = pl.BlockSpec((8, 128), lambda i: (0, i))
    return pl.pallas_call(
        functools.partial(grad_kernel, float(features)),
        grid=(rows // 128,),
        in_specs=[big, big, pl.BlockSpec((1, width), lambda i: (0, 0))]
        + [small] * 4
        + [pl.BlockSpec((1, 128), lambda i: (0, i))],
        out_specs=[big, pl.BlockSpec((1, width), lambda i: (0, 0))],
        out_shape=[
            jax.ShapeDtypeStruct((rows, width), BF),
            jax.ShapeDtypeStruct((1, width), F32),
        ],
        compiler_params=params(),
        cost_estimate=pl.CostEstimate(
            flops=12 * rows * width, bytes_accessed=8 * rows * width, transcendentals=0
        ),
        name="grad",
    )(hidden, cot, gain, s0, s1, s2, s3, coef)


def attention_kernel(where, *refs):
    pieces, w, out, buf, acc, sems = refs[:8], refs[8], refs[9], refs[10], refs[11], refs[12]
    x, c = where[2], where[3]
    step = buf.shape[1]
    copies = []
    for n in range(8):
        holder = (1 - c) if n % 2 else c
        piece = lax.rem(x + 4 - n // 2, 4) * 2 + holder
        row = pl.multiple_of(piece * step, step)
        copies.append(pltpu.make_async_copy(w.at[pl.ds(row, step)], buf.at[n], sems.at[n]))
        copies[-1].start()
    for n in range(8):
        copies[n].wait()
        term = jnp.dot(pieces[n][...], buf[n], preferred_element_type=F32)
        if n == 0:
            acc[...] = term
        elif n < 7:
            acc[...] += term
        else:
            out[...] = (acc[...] + term).astype(BF)


def attention_call(where, pieces, out_proj):
    rows, width = pieces[0].shape
    depth = out_proj.shape[1]
    vmem = pl.BlockSpec(memory_space=pltpu.VMEM)
    return pl.pallas_call(
        attention_kernel,
        in_specs=[pl.BlockSpec(memory_space=pltpu.SMEM)]
        + [vmem] * 8
        + [pl.BlockSpec(memory_space=pl.ANY)],
        out_specs=vmem,
        scratch_shapes=[
            pltpu.VMEM((8, width, depth), BF),
            pltpu.VMEM((rows, depth), F32),
            pltpu.SemaphoreType.DMA((8,)),
        ],
        out_shape=jax.ShapeDtypeStruct((rows, depth), BF),
        compiler_params=params(),
        cost_estimate=pl.CostEstimate(
            flops=2 * rows * depth * width * 8,
            bytes_accessed=2 * 8 * width * depth,
            transcendentals=0,
        ),
        name="attention_grad",
    )(where, *pieces, out_proj)


def first_pack_kernel(where, *refs):
    pieces, outs = refs[:8], refs[8:12]
    z, y, x, c = where[0], where[1], where[2], where[3]
    rows, half = outs[0].shape[1:]
    for k in range(4):
        big_z = lax.rem(x + 4 - k, 4)
        for other in range(2):
            holder = (1 - c) if other else c
            for h in range(2):
                big_y = 2 * holder + h
                slot = jnp.where(c == 0, lax.rem(big_z + 4 - z, 4), lax.rem(big_y + 4 - y, 4))
                j = jnp.where(c == 0, big_y, big_z)
                start = pl.multiple_of(h * 2 * half + c * half, half)
                for s in range(4):

                    @pl.when(slot == s)
                    def _(s=s, j=j, start=start, piece=pieces[k * 2 + other]):
                        @pl.loop(0, rows // 64)
                        def _(r):
                            band = pl.ds(pl.multiple_of(r * 64, 64), 64)
                            outs[s][j, band, :] = piece[band, pl.ds(start, half)]


def second_pack_kernel(where, *refs):
    parts, outs = refs[:4], refs[4:8]
    rows = outs[0].shape[1]
    mine = jnp.where(where[3] == 0, where[1], where[0])
    for u in range(4):
        j = lax.rem(mine + u, 4)
        for s in range(4):

            @pl.loop(0, rows // 64)
            def _(r, u=u, s=s, j=j):
                band = pl.ds(pl.multiple_of(r * 64, 64), 64)
                outs[u][s, band, :] = parts[s][j, band, :]


def pack_call(kernel, where, inputs, rows, half, name):
    vmem = pl.BlockSpec(memory_space=pltpu.VMEM)
    return pl.pallas_call(
        kernel,
        in_specs=[pl.BlockSpec(memory_space=pltpu.SMEM)] + [vmem] * len(inputs),
        out_specs=[vmem] * 4,
        out_shape=[jax.ShapeDtypeStruct((4, rows, half), BF)] * 4,
        compiler_params=pltpu.CompilerParams(vmem_limit_bytes=16 * 1024 * 1024),
        cost_estimate=pl.CostEstimate(
            flops=0, bytes_accessed=64 * rows * half, transcendentals=0
        ),
        name=name,
    )(where, *inputs)


def projection_kernel(members, first, last, where, *refs):
    count = len(members)
    mine, theirs = refs[:count], refs[count : 2 * count]
    refs = refs[2 * count :]
    gathered = refs[0]
    before = None if first else refs[1]
    out, buf, acc, sems = refs[1 if first else 2 :]
    z, y, c = where[0], where[1], where[3]
    rows = buf.shape[1]
    half = acc.shape[1]
    copies = []
    for m, u in enumerate(members):
        for s in range(4):
            for n in range(2):
                z_first = (c == 0) if n == 0 else (c == 1)
                dz, dy = jnp.where(z_first, s, u), jnp.where(z_first, u, s)
                row = lax.rem(z + 4 - dz, 4) * 4 + lax.rem(y + 4 - dy, 4)
                row = pl.multiple_of(row * rows, rows)
                i = len(copies)
                copies.append(
                    pltpu.make_async_copy(gathered.at[pl.ds(row, rows)], buf.at[i], sems.at[i])
                )
                copies[-1].start()
    i = 0
    for m in range(count):
        for s in range(4):
            for n, lhs in ((0, mine[m].at[s]), (1, theirs[m].at[s])):
                copies[i].wait()
                term = lax.dot_general(
                    lhs[...], buf[i], (((0,), (0,)), ((), ())), preferred_element_type=F32
                )
                if i >= 2:
                    acc[n] += term
                elif first:
                    acc[n] = term
                else:
                    acc[n] = before[n] + term
                i += 1
    if last:
        low = pl.multiple_of(c * half, half)
        high = pl.multiple_of((1 - c) * half, half)
        out[pl.ds(low, half), :] = acc[0].astype(BF)
        out[pl.ds(high, half), :] = acc[1].astype(BF)
    else:
        out[...] = acc[...]


def projection_call(where, mine, theirs, gathered, members, before, last):
    _, rows, half = mine[0].shape
    depth = gathered.shape[1]
    vmem = pl.BlockSpec(memory_space=pltpu.VMEM)
    blocks = 8 * len(members)
    picked = [mine[u] for u in members] + [theirs[u] for u in members]
    first = before is None
    return pl.pallas_call(
        functools.partial(projection_kernel, members, first, last),
        in_specs=[pl.BlockSpec(memory_space=pltpu.SMEM)]
        + [vmem] * len(picked)
        + [pl.BlockSpec(memory_space=pl.ANY)]
        + ([] if first else [vmem]),
        out_specs=vmem,
        scratch_shapes=[
            pltpu.VMEM((blocks, rows, depth), BF),
            pltpu.VMEM((2, half, depth), F32),
            pltpu.SemaphoreType.DMA((blocks,)),
        ],
        out_shape=jax.ShapeDtypeStruct((2 * half, depth), BF)
        if last
        else jax.ShapeDtypeStruct((2, half, depth), F32),
        compiler_params=params(),
        cost_estimate=pl.CostEstimate(
            flops=2 * blocks * rows * half * depth,
            bytes_accessed=2 * blocks * rows * (depth + half),
            transcendentals=0,
        ),
        name="projection_grad",
    )(where, *picked, gathered, *([] if first else [before]))


def dp_sum(value):
    total = value
    for k in range(1, 4):
        total = total + lax.ppermute(value, "dp", dp_shift(0, k))
    result = total
    for k in range(1, 4):
        result = result + lax.ppermute(total, "dp", dp_shift(k, 0))
    return result


def token_scaling(rewards, group_ids, kept_flags, lengths, rows):
    dp_count = lax.axis_size("dp")
    groups = rewards.shape[0] * dp_count // 16
    seqs_here = rewards.shape[0]
    kept = kept_flags.astype(F32)
    onehot = (group_ids[None, :] == jnp.arange(groups, dtype=jnp.int32)[:, None]).astype(F32)
    stats = jnp.stack(
        [
            jnp.sum(onehot * kept[None, :], axis=1),
            jnp.sum(onehot * (kept * rewards)[None, :], axis=1),
            jnp.sum(onehot * (kept * rewards * rewards)[None, :], axis=1),
        ]
    )
    local_tokens = jnp.sum(kept * lengths[0].astype(F32))
    packed = jnp.concatenate([stats, jnp.full((1, groups), local_tokens, F32)], axis=0)
    packed = dp_sum(packed)
    stats, kept_tokens = packed[:3], packed[3, 0]
    group_mean = stats[1] / jnp.maximum(stats[0], 1.0)
    group_var = stats[2] / jnp.maximum(stats[0], 1.0) - group_mean * group_mean
    group_scale = jnp.sqrt(jnp.maximum(group_var, 1.0))
    seq_mean = jnp.sum(onehot * group_mean[:, None], axis=0)
    seq_scale = jnp.sum(onehot * group_scale[:, None], axis=0)
    advantage = (rewards - seq_mean) / seq_scale
    seq_coef = -advantage * kept * float(rows * dp_count) / jnp.maximum(kept_tokens, 1.0)
    ends = jnp.cumsum(lengths[0])
    position = jnp.arange(rows, dtype=jnp.int32)
    segment = jnp.sum((position[:, None] >= ends[None, :]).astype(jnp.int32), axis=1)
    picks = (segment[:, None] == jnp.arange(seqs_here, dtype=jnp.int32)[None, :]).astype(F32)
    return jnp.sum(picks * seq_coef[None, :], axis=1)


def shards(
    attention, residual, out_proj, norm_gain, cotangent, rewards, group_ids, kept_flags, lengths
):
    rows = attention.shape[0]
    features = out_proj.shape[0]
    d, t = lax.axis_index("dp"), lax.axis_index("tensor")
    where = jnp.stack([d // 4, d % 4, t // 2, t % 2]).astype(jnp.int32)
    gain = norm_gain[None, :]

    gathered = lax.all_gather(attention, "dp", axis=0, tiled=True)

    arrived = {}
    send, keep = partial_products(where, attention, out_proj, (2,))
    both = (keep[0] + swap(send)[0].astype(F32)).astype(BF)
    arrived[2] = lax.ppermute(both, "tensor", x_shift(2))
    later_where, _ = lax.optimization_barrier((where, both))
    send, keep = partial_products(later_where, attention, out_proj, (1, 3, 0))
    sent = swap(send)
    for i, k in ((0, 1), (1, 3)):
        both = (keep[i] + sent[i].astype(F32)).astype(BF)
        arrived[k] = lax.ppermute(both, "tensor", x_shift(k))
    rewards, group_ids, kept_flags, lengths, _ = lax.optimization_barrier(
        (rewards, group_ids, kept_flags, lengths, both)
    )
    coef = token_scaling(rewards, group_ids, kept_flags, lengths, rows)
    residual, coef = lax.optimization_barrier((residual, coef))
    hidden, sums = hidden_call(
        keep[2], sent[2], arrived[1], arrived[2], arrived[3], residual, cotangent, gain
    )

    chip = sums + swap(sums)
    others = [lax.ppermute(chip, "tensor", x_shift(k)) for k in (1, 2, 3)]
    grad_residual, gain_term = grad_call(
        features, hidden, cotangent, gain, chip, *others, coef[None, :]
    )

    pieces = []
    for k in range(4):
        piece = grad_residual if k == 0 else lax.ppermute(grad_residual, "tensor", x_shift(k))
        pieces.extend([piece, swap(piece)])
    gain_term, _ = lax.optimization_barrier((gain_term, pieces[1]))
    grad_gain = dp_sum(gain_term)[0]

    half = features // 32
    pack_where, grad_gain = lax.optimization_barrier((where, grad_gain))
    sends = pack_call(first_pack_kernel, pack_where, pieces, rows, half, "first_pack")
    parts = [sends[0]] + [
        lax.ppermute(sends[k], ("dp", "tensor"), plane_shift(0, k)) for k in (1, 2, 3)
    ]
    late_where, _ = lax.optimization_barrier((where, sends))
    grad_attention = attention_call(late_where, pieces, out_proj)
    pack_where, _ = lax.optimization_barrier((where, grad_attention))
    sends = pack_call(second_pack_kernel, pack_where, parts, rows, half, "second_pack")
    mine = [sends[0]] + [
        lax.ppermute(sends[k], ("dp", "tensor"), plane_shift(1, k)) for k in (1, 2, 3)
    ]
    theirs = [swap(part) for part in mine]
    total = projection_call(where, mine, theirs, gathered, (0,), None, False)
    grad_out_proj = projection_call(where, mine, theirs, gathered, (1, 3, 2), total, True)
    return (grad_attention, grad_out_proj, grad_residual, grad_gain)


def solution(mesh):
    return jax.shard_map(
        shards,
        mesh=mesh,
        in_specs=(
            P("dp", "tensor"),
            P("dp", "tensor"),
            P(None, "tensor"),
            P("tensor"),
            P("dp", "tensor"),
            P("dp"),
            P("dp"),
            P("dp"),
            P("dp", None),
        ),
        out_specs=(P("dp", "tensor"), P("dp", "tensor"), P("dp", "tensor"), P("tensor")),
        check_vma=False,
    )
```

time: 365 us -> 173 us (0.47)
  waiting for transfers between devices: 195 us -> 40.5 us
  blocking collectives: 96.8 us -> 0 us
  starting transfers between devices: 0.12 us -> 68.4 us
  matrix products: 47 us -> 0 us
  Pallas kernels: 0 us -> 37.7 us
  other arithmetic: 9.5 us -> 4.42 us
  local copies, waits for them, and re-layouts: 1.58 us -> 6.32 us
    reduce_scatter x2 -> x0, waiting for transfers between devices: 164 us -> none  [the longest x1 147 us: shards(): lax.psum_scatter(lax.dot_general(grad_full, attention, (((0,), (0,)), (()...]
    psum x4 -> x0, blocking collectives: 96.8 us -> none  [the longest x1 36.2 us: token_scaling(): stats, kept_tokens = lax.psum((stats, local_tokens), 'dp')]
    ppermute x0 -> x38, starting transfers between devices: none -> 68.3 us  [the longest x11 38.6 us: swap(): return lax.ppermute(value, 'tensor', CORE_SWAP)]
    dot_general x3 -> x0, matrix products: 47 us -> none  [the longest x1 18.8 us: shards(): lax.dot_general(attention, out_proj, (((1,), (1,)), ((), ())), preferred_...]
    ppermute x0 -> x38, waiting for transfers between devices: none -> 39.8 us  [the longest x3 10.9 us: shards(): lax.ppermute(grad_residual, 'tensor', x_shift(k))]
    pallas_call x0 -> x9, Pallas kernels: none -> 37.7 us  [the longest x2 14 us: projection_call(): pl.pallas_call(functools.partial(projection_kernel, members, first, last)...]
    all_gather x1, waiting for transfers between devices: 31.5 us -> 0.01 us  [shards(): gathered = lax.all_gather(attention, 'dp', axis=0, tiled=True)]
  transfers between devices with their start and end apart: 3 -> 39, of which waited for: 3 -> 21; matrix products, arithmetic and copies ran while one was open for 4% -> 4% of each run, Pallas kernels for 0% -> 16%
where the time goes in v1:
time: 173 us; the launch traced here: 172 us
  starting transfers between devices  68.4 us (40%)
  waiting for transfers between devices  40.5 us (23%)
  Pallas kernels  37.7 us (22%)
  between operations  15 us (9%)
  local copies, waits for them, and re-layouts  6.32 us (4%)
  other arithmetic  4.42 us (3%)
    ppermute x11, starting transfers between devices, swap(): return lax.ppermute(value, 'tensor', CORE_SWAP)  38.6 us
    pallas_call x2, Pallas kernels, projection_call(): pl.pallas_call(functools.partial(projection_kernel, members, first, last)...  14 us
    pallas_call x2, Pallas kernels, partial_products(): pl.pallas_call(functools.partial(partial_kernel, shifts), in_specs=[pl.Bl...  11.3 us
    ppermute x3, waiting for transfers between devices, shards(): lax.ppermute(grad_residual, 'tensor', x_shift(k))  10.9 us
    ppermute x6, waiting for transfers between devices, dp_sum(): result = result + lax.ppermute(total, 'dp', dp_shift(k, 0))  9.29 us
    pallas_call x1, Pallas kernels, attention_call(): pl.pallas_call(attention_kernel, in_specs=[pl.BlockSpec(memory_space=pltp...  7.98 us
    ppermute x6, starting transfers between devices, dp_sum(): result = result + lax.ppermute(total, 'dp', dp_shift(k, 0))  7.87 us
    ppermute x6, starting transfers between devices, dp_sum(): total = total + lax.ppermute(value, 'dp', dp_shift(0, k))  6.8 us
  transfers between devices with their start and end apart: 39, of which 21 were waited for; matrix products, arithmetic and copies ran while one was open for 4% of the time, Pallas kernels for 16%

profile of v1, /device:TPU:1, one launch (start us, length us, event | category | flops | bytes accessed | tf_op | source)
XLA Modules:
  0.0 172.3 jit_solution(14759689338851744328)
XLA Ops:
  8.0 1.0 copy-done
  9.1 3.7 %partial.2 = (bf16[1,256,1024]{2,1,0:T(8,128)(2,1)S(1)}, f32[1,256,1024]{2,1,0:T(8,128)S(1)}) custom-call(s32[4]{0:T(128)S(1)} %pad_add_fusion.where, bf16[256,1024]{1,0:T(8,128)(2,1)S(1)} %copy-done, bf16[8192,1024]{1,0:T(8,128)(2,1)} %refs_8_.1), custom_call_target="tpu_custom_call" | custom-call | flops 1073741824 | bytes 4194304 | tf_op jit(solution)/shard_map/partial/pallas_call | solution.py:85
  12.8 1.5 collective-permute-start
  14.3 1.5 collective-permute-done
  15.8 0.9 fusion
  16.7 7.5 %partial.3 = (bf16[3,256,1024]{2,1,0:T(8,128)(2,1)S(1)}, f32[3,256,1024]{2,1,0:T(8,128)S(1)}) custom-call(s32[4]{0:T(128)S(1)} %pad_add_fusion.where, bf16[256,1024]{1,0:T(8,128)(2,1)S(1)} %copy-done, bf16[8192,1024]{1,0:T(8,128)(2,1)} %refs_8_.1), custom_call_target="tpu_custom_call" | custom-call | flops 3221225472 | bytes 12582912 | tf_op jit(solution)/shard_map/partial/pallas_call | solution.py:85
  24.8 2.9 %collective-permute-start.3 = (bf16[256,1024]{1,0:T(8,128)(2,1)}, bf16[256,1024]{1,0:T(8,128)(2,1)S(1)}, u32[]{:S(2)}, u32[]{:S(2)}) collective-permute-start(bf16[256,1024]{1,0:T(8,128)(2,1)} %fusion), channel_id=1, source_target_pairs={{0,4},{1,5},{2,6},{3,7},{4,0},{5,1},{6,2},{7,3},{8,12},{9,13},{10,... | collective-permute-start | bytes 1572872 | tf_op jit(solution)/shard_map/ppermute | solution.py:438
  27.8 1.4 fusion.2
  30.9 3.0 %collective-permute-start.6 = (f32[4,4]{1,0:T(4,128)S(1)}, f32[4,4]{1,0:T(4,128)S(1)}, u32[]{:S(2)}, u32[]{:S(2)}) collective-permute-start(f32[4,4]{1,0:T(4,128)S(1)} %maximum_maximum_fusion), channel_id=1, source_target_pairs={{0,16},{8,24},{16,0},{24,8},{32,48},{40,56},{48,32},{56,40},{64,80... | collective-permute-start | bytes 200 | tf_op jit(solution)/shard_map/ppermute | solution.py:386
  33.9 0.8 collective-permute-start.7
  35.4 2.5 %collective-permute-start.4 = (bf16[256,1024]{1,0:T(8,128)(2,1)}, bf16[256,1024]{1,0:T(8,128)(2,1)S(1)}, u32[]{:S(2)}, u32[]{:S(2)}) collective-permute-start(bf16[256,1024]{1,0:T(8,128)(2,1)} %get-tuple-element.67), channel_id=1, source_target_pairs={{0,6},{1,7},{2,0},{3,1},{4,2},{5,3},{6,4},{7,5},{8,14},{9,15},{10,... | collective-permute-start | bytes 1572872 | tf_op jit(solution)/shard_map/ppermute | solution.py:444
  38.0 1.1 slice_bitcast_fusion.1.own
  39.4 3.8 %collective-permute-start.10 = (f32[4,4]{1,0:T(4,128)S(1)}, f32[4,4]{1,0:T(4,128)S(1)}, u32[]{:S(2)}, u32[]{:S(2)}) collective-permute-start(f32[4,4]{1,0:T(4,128)S(1)} %add_add_fusion.3), channel_id=1, source_target_pairs={{0,96},{8,104},{16,112},{24,120},{32,0},{40,8},{48,16},{56,24},{64... | collective-permute-start | bytes 200 | tf_op jit(solution)/shard_map/ppermute | solution.py:389
  43.1 0.7 collective-permute-done.10
  43.9 3.1 %collective-permute-done.9 = f32[4,4]{1,0:T(4,128)S(1)} collective-permute-done((f32[4,4]{1,0:T(4,128)S(1)}, f32[4,4]{1,0:T(4,128)S(1)}, u32[]{:S(2)}, u32[]{:S(2)}) %collective-permute-start.9) | collective-permute-done | bytes 96 | tf_op jit(solution)/shard_map/ppermute | solution.py:389
  47.1 1.0 collective-permute-done.8
  49.4 3.3 %collective-permute-done.2.r1 = bf16[256,1024]{1,0:T(8,128)(2,1)S(1)} collective-permute-done((bf16[256,1024]{1,0:T(8,128)(2,1)}, bf16[256,1024]{1,0:T(8,128)(2,1)S(1)}, u32[]{:S(2)}, u32[]{:S(2)}) %collective-permute-start.2) | collective-permute-done | bytes 524320 | tf_op jit(solution)/shard_map/ppermute | solution.py:444
  52.7 0.8 hidden.1
  53.5 2.4 %collective-permute-start.11 = (f32[8,256]{1,0:T(8,128)S(1)}, f32[8,256]{1,0:T(8,128)S(1)}, u32[]{:S(2)}, u32[]{:S(2)}) collective-permute-start(f32[8,256]{1,0:T(8,128)S(1)} %get-tuple-element.43), channel_id=1, source_target_pairs={{0,1},{1,0},{2,3},{3,2},{4,5},{5,4},{6,7},{7,6},{8,9},{9,8},{10,11... | collective-permute-start | bytes 24584 | tf_op jit(solution)/shard_map/ppermute | solution.py:38
  55.9 0.8 collective-permute-done.11
  57.3 0.9 collective-permute-start.12
  58.2 1.4 collective-permute-done.14.s3
  59.6 1.7 %collective-permute-done.13.s2 = f32[8,256]{1,0:T(8,128)S(1)} collective-permute-done((f32[8,256]{1,0:T(8,128)S(1)}, f32[8,256]{1,0:T(8,128)S(1)}, u32[]{:S(2)}, u32[]{:S(2)}) %collective-permute-start.13) | collective-permute-done | bytes 8224 | tf_op jit(solution)/shard_map/ppermute | solution.py:455
  62.0 1.2 grad.1
  63.2 1.5 collective-permute-start.26
  64.7 0.9 collective-permute-start.24
  65.6 2.2 %collective-permute-start.15 = (bf16[256,1024]{1,0:T(8,128)(2,1)}, bf16[256,1024]{1,0:T(8,128)(2,1)S(1)}, u32[]{:S(2)}, u32[]{:S(2)}) collective-permute-start(bf16[256,1024]{1,0:T(8,128)(2,1)} %get-tuple-element.30.refs_0_), channel_id=1, source_target_pairs={{0,1},{1,0},{2,3},{3,2},{4,5},{5,4},{6,7},{7,6},{8,9},{9,8},{10,11... | collective-permute-start | bytes 1572872 | tf_op jit(solution)/shard_map/ppermute | solution.py:38
  67.7 7.8 %collective-permute-done.26.refs_6_ = bf16[256,1024]{1,0:T(8,128)(2,1)S(1)} collective-permute-done((bf16[256,1024]{1,0:T(8,128)(2,1)}, bf16[256,1024]{1,0:T(8,128)(2,1)S(1)}, u32[]{:S(2)}, u32[]{:S(2)}) %collective-permute-start.26) | collective-permute-done | bytes 524320 | tf_op jit(solution)/shard_map/ppermute | solution.py:462
  75.6 12.8 %collective-permute-start.27 = (bf16[256,1024]{1,0:T(8,128)(2,1)S(1)}, bf16[256,1024]{1,0:T(8,128)(2,1)S(1)}, u32[]{:S(2)}, u32[]{:S(2)}) collective-permute-start(bf16[256,1024]{1,0:T(8,128)(2,1)S(1)} %collective-permute-done.26.refs_6_), channel_id=1, source_target_pairs={{0,1},{1,0},{2,3},{3,2},{4,5},{5,4},{6,7},{7,6},{8,9},{9,8},{10,11... | collective-permute-start | bytes 1572872 | tf_op jit(solution)/shard_map/ppermute | solution.py:38
  88.4 3.1 %collective-permute-done.22.refs_2_ = bf16[256,1024]{1,0:T(8,128)(2,1)S(1)} collective-permute-done((bf16[256,1024]{1,0:T(8,128)(2,1)}, bf16[256,1024]{1,0:T(8,128)(2,1)S(1)}, u32[]{:S(2)}, u32[]{:S(2)}) %collective-permute-start.22) | collective-permute-done | bytes 524320 | tf_op jit(solution)/shard_map/ppermute | solution.py:462
  92.0 2.0 %collective-permute-start.18 = (f32[1,1024]{1,0:T(1,128)S(1)}, f32[1,1024]{1,0:T(1,128)S(1)}, u32[]{:S(2)}, u32[]{:S(2)}) collective-permute-start(f32[1,1024]{1,0:T(1,128)S(1)} %get-tuple-element.47), channel_id=1, source_target_pairs={{0,24},{8,0},{16,8},{24,16},{32,56},{40,32},{48,40},{56,48},{64,88... | collective-permute-start | bytes 12296 | tf_op jit(solution)/shard_map/ppermute | solution.py:386
  94.8 3.1 %collective-permute-done.17 = f32[1,1024]{1,0:T(1,128)S(1)} collective-permute-done((f32[1,1024]{1,0:T(1,128)S(1)}, f32[1,1024]{1,0:T(1,128)S(1)}, u32[]{:S(2)}, u32[]{:S(2)}) %collective-permute-start.17) | collective-permute-done | bytes 4128 | tf_op jit(solution)/shard_map/ppermute | solution.py:386
  97.9 1.0 collective-permute-done.16
  98.9 3.8 %collective-permute-start.21 = (f32[1,1024]{1,0:T(1,128)S(1)}, f32[1,1024]{1,0:T(1,128)S(1)}, u32[]{:S(2)}, u32[]{:S(2)}) collective-permute-start(f32[1,1024]{1,0:T(1,128)S(1)} %add_add_fusion.1), channel_id=1, source_target_pairs={{0,96},{8,104},{16,112},{24,120},{32,0},{40,8},{48,16},{56,24},{64... | collective-permute-start | bytes 12296 | tf_op jit(solution)/shard_map/ppermute | solution.py:389
  103.6 3.1 %collective-permute-done.20 = f32[1,1024]{1,0:T(1,128)S(1)} collective-permute-done((f32[1,1024]{1,0:T(1,128)S(1)}, f32[1,1024]{1,0:T(1,128)S(1)}, u32[]{:S(2)}, u32[]{:S(2)}) %collective-permute-start.20) | collective-permute-done | bytes 4128 | tf_op jit(solution)/shard_map/ppermute | solution.py:389
  108.0 1.0 copy-done.1
  109.1 1.5 first_pack.1
  110.7 2.3 %collective-permute-start.29 = (bf16[4,256,256]{2,1,0:T(8,128)(2,1)S(1)}, bf16[4,256,256]{2,1,0:T(8,128)(2,1)S(1)}, u32[]{:S(2)}, u32[]{:S(2)}) collective-permute-start(bf16[4,256,256]{2,1,0:T(8,128)(2,1)S(1)} %get-tuple-element.51), channel_id=1, source_target_pairs={{0,64},{1,17},{2,66},{3,19},{4,68},{5,21},{6,70},{7,23},{8,72},{9,... | collective-permute-start | bytes 1572872 | tf_op jit(solution)/shard_map/ppermute | solution.py:471
  113.4 8.0 %attention_grad.1 = bf16[256,1024]{1,0:T(8,128)(2,1)} custom-call(s32[4]{0:T(128)S(1)} %pad_add_fusion.where, bf16[256,1024]{1,0:T(8,128)(2,1)S(1)} %copy-done.2, bf16[256,1024]{1,0:T(8,128)(2,1)S(1)} %collective-permute-done.15.refs_1_, bf16[256,1024]{1,0:T(8,128)(2,1)S(1)} %collective-permute-done.22.refs_2_, ...), custom_call_target="tpu_custom_call" | custom-call | flops 4294967296 | bytes 16777216 | tf_op jit(solution)/shard_map/attention_grad/pallas_call | solution.py:230
  121.4 4.4 %collective-permute-done.28.refs_1_ = bf16[4,256,256]{2,1,0:T(8,128)(2,1)S(1)} collective-permute-done((bf16[4,256,256]{2,1,0:T(8,128)(2,1)S(1)}, bf16[4,256,256]{2,1,0:T(8,128)(2,1)S(1)}, u32[]{:S(2)}, u32[]{:S(2)}) %collective-permute-start.28) | collective-permute-done | bytes 524320 | tf_op jit(solution)/shard_map/ppermute | solution.py:471
  126.5 1.0 second_pack.1
  127.5 2.7 %collective-permute-start.32 = (bf16[4,256,256]{2,1,0:T(8,128)(2,1)S(1)}, bf16[4,256,256]{2,1,0:T(8,128)(2,1)S(1)}, u32[]{:S(2)}, u32[]{:S(2)}) collective-permute-start(bf16[4,256,256]{2,1,0:T(8,128)(2,1)S(1)} %get-tuple-element.56), channel_id=1, source_target_pairs={{0,24},{1,97},{2,26},{3,99},{4,28},{5,101},{6,30},{7,103},{8,0},{9... | collective-permute-start | bytes 1572872 | tf_op jit(solution)/shard_map/ppermute | solution.py:478
  130.4 6.0 %collective-permute-start.37 = (bf16[4,256,256]{2,1,0:T(8,128)(2,1)S(1)}, bf16[4,256,256]{2,1,0:T(8,128)(2,1)S(1)}, u32[]{:S(2)}, u32[]{:S(2)}) collective-permute-start(bf16[4,256,256]{2,1,0:T(8,128)(2,1)S(1)} %get-tuple-element.58.refs_0_), channel_id=1, source_target_pairs={{0,1},{1,0},{2,3},{3,2},{4,5},{5,4},{6,7},{7,6},{8,9},{9,8},{10,11... | collective-permute-start | bytes 1572872 | tf_op jit(solution)/shard_map/ppermute | solution.py:38
  136.7 12.2 %collective-permute-start.34 = (bf16[4,256,256]{2,1,0:T(8,128)(2,1)S(1)}, bf16[4,256,256]{2,1,0:T(8,128)(2,1)S(1)}, u32[]{:S(2)}, u32[]{:S(2)}) collective-permute-start(bf16[4,256,256]{2,1,0:T(8,128)(2,1)S(1)} %collective-permute-done.31.refs_0_), channel_id=1, source_target_pairs={{0,1},{1,0},{2,3},{3,2},{4,5},{5,4},{6,7},{7,6},{8,9},{9,8},{10,11... | collective-permute-start | bytes 1572872 | tf_op jit(solution)/shard_map/ppermute | solution.py:38
  149.5 0.8 copy-done.5
  150.3 1.0 copy-done.6
  151.3 4.0 %projection_grad.2.refs_7_ = f32[2,256,1024]{2,1,0:T(8,128)S(1)} custom-call(s32[4]{0:T(128)S(1)} %pad_add_fusion.where, bf16[4,256,256]{2,1,0:T(8,128)(2,1)S(1)} %get-tuple-element.58.refs_0_, bf16[4,256,256]{2,1,0:T(8,128)(2,1)S(1)} %copy-done.6, bf16[4096,1024]{1,0:T(8,128)(2,1)} %all-gather.2.cloned.1.call-done.refs_2_.refs_6_), custom_call_target="tpu_custom_call" | custom-call | flops 1073741824 | bytes 5242880 | tf_op jit(solution)/shard_map/projection_grad/pallas_call | solution.py:358
  155.3 10.1 %projection_grad.3 = bf16[512,1024]{1,0:T(8,128)(2,1)} custom-call(s32[4]{0:T(128)S(1)} %pad_add_fusion.where, bf16[4,256,256]{2,1,0:T(8,128)(2,1)S(1)} %collective-permute-done.31.refs_0_, bf16[4,256,256]{2,1,0:T(8,128)(2,1)S(1)} %collective-permute-done.32.refs_1_, bf16[4,256,256]{2,1,0:T(8,128)(2,1)S(1)} %collective-permute-done.33.refs_2_, ...), custom_call_target="tpu_custom_call" | custom-call | flops 3221225472 | bytes 15728640 | tf_op jit(solution)/shard_map/projection_grad/pallas_call | solution.py:358
  (88 shorter events, 11.9 us)
Async XLA Ops:
  7.2 143.1 %all-gather.2.cloned.1.call-start = ((), (), s32[]{:S(2)}) async-start(), calls=%async_computation | async-start | bytes 8912896 | tf_op jit(solution)/shard_map/all_gather | solution.py:433
  12.8 3.0 %collective-permute-start = (bf16[1,256,1024]{2,1,0:T(8,128)(2,1)S(1)}, bf16[1,256,1024]{2,1,0:T(8,128)(2,1)S(1)}, u32[]{:S(2)}, u32[]{:S(2)}) collective-permute-start(bf16[1,256,1024]{2,1,0:T(8,128)(2,1)S(1)} %get-tuple-element.33), channel_id=1, source_target_pairs={{0,1},{1,0},{2,3},{3,2},{4,5},{5,4},{6,7},{7,6},{8,9},{9,8},{10,11... | collective-permute-start | bytes 1572872 | tf_op jit(solution)/shard_map/ppermute | solution.py:38
  16.7 8.0 %copy-start.8 = (bf16[1024]{0:T(1024)(128)(2,1)S(1)}, bf16[1024]{0:T(1024)(128)(2,1)}, u32[]{:S(2)}) copy-start(bf16[1024]{0:T(1024)(128)(2,1)} %param.12) | copy-start | bytes 6148
  24.3 3.5 %collective-permute-start.1 = (bf16[3,256,1024]{2,1,0:T(8,128)(2,1)S(1)}, bf16[3,256,1024]{2,1,0:T(8,128)(2,1)S(1)}, u32[]{:S(2)}, u32[]{:S(2)}) collective-permute-start(bf16[3,256,1024]{2,1,0:T(8,128)(2,1)S(1)} %get-tuple-element.36), channel_id=1, source_target_pairs={{0,1},{1,0},{2,3},{3,2},{4,5},{5,4},{6,7},{7,6},{8,9},{9,8},{10,11... | collective-permute-start | bytes 4718600 | tf_op jit(solution)/shard_map/ppermute | solution.py:38
  24.8 24.7 %collective-permute-start.3 = (bf16[256,1024]{1,0:T(8,128)(2,1)}, bf16[256,1024]{1,0:T(8,128)(2,1)S(1)}, u32[]{:S(2)}, u32[]{:S(2)}) collective-permute-start(bf16[256,1024]{1,0:T(8,128)(2,1)} %fusion), channel_id=1, source_target_pairs={{0,4},{1,5},{2,6},{3,7},{4,0},{5,1},{6,2},{7,3},{8,12},{9,13},{10,... | collective-permute-start | bytes 1572872 | tf_op jit(solution)/shard_map/ppermute | solution.py:438
  27.8 1.5 copy-start.7
  27.8 1.5 copy-start.10
  27.8 1.5 copy-start.11
  27.8 1.5 copy-start.12
  27.8 2.8 %copy-start.9 = (s32[4]{0:T(128)S(1)}, s32[4]{0:T(128)}, u32[]{:S(2)}) copy-start(s32[4]{0:T(128)} %param.15) | copy-start | bytes 52
  27.8 24.9 %copy-start.3 = (bf16[256,1024]{1,0:T(8,128)(2,1)S(1)}, bf16[256,1024]{1,0:T(8,128)(2,1)}, u32[]{:S(2)}) copy-start(bf16[256,1024]{1,0:T(8,128)(2,1)} %cot.3) | copy-start | bytes 1572868
  27.8 24.9 %copy-start.4 = (bf16[256,1024]{1,0:T(8,128)(2,1)S(1)}, bf16[256,1024]{1,0:T(8,128)(2,1)}, u32[]{:S(2)}) copy-start(bf16[256,1024]{1,0:T(8,128)(2,1)} %residual) | copy-start | bytes 1572868
  30.9 8.3 %collective-permute-start.6 = (f32[4,4]{1,0:T(4,128)S(1)}, f32[4,4]{1,0:T(4,128)S(1)}, u32[]{:S(2)}, u32[]{:S(2)}) collective-permute-start(f32[4,4]{1,0:T(4,128)S(1)} %maximum_maximum_fusion), channel_id=1, source_target_pairs={{0,16},{8,24},{16,0},{24,8},{32,48},{40,56},{48,32},{56,40},{64,80... | collective-permute-start | bytes 200 | tf_op jit(solution)/shard_map/ppermute | solution.py:386
  33.9 5.4 %collective-permute-start.7 = (f32[4,4]{1,0:T(4,128)S(1)}, f32[4,4]{1,0:T(4,128)S(1)}, u32[]{:S(2)}, u32[]{:S(2)}) collective-permute-start(f32[4,4]{1,0:T(4,128)S(1)} %maximum_maximum_fusion), channel_id=1, source_target_pairs={{0,24},{8,0},{16,8},{24,16},{32,56},{40,32},{48,40},{56,48},{64,88... | collective-permute-start | bytes 200 | tf_op jit(solution)/shard_map/ppermute | solution.py:386
  34.7 4.6 %collective-permute-start.5 = (f32[4,4]{1,0:T(4,128)S(1)}, f32[4,4]{1,0:T(4,128)S(1)}, u32[]{:S(2)}, u32[]{:S(2)}) collective-permute-start(f32[4,4]{1,0:T(4,128)S(1)} %maximum_maximum_fusion), channel_id=1, source_target_pairs={{0,8},{8,16},{16,24},{24,0},{32,40},{40,48},{48,56},{56,32},{64,72... | collective-permute-start | bytes 200 | tf_op jit(solution)/shard_map/ppermute | solution.py:386
  35.4 17.3 %collective-permute-start.4 = (bf16[256,1024]{1,0:T(8,128)(2,1)}, bf16[256,1024]{1,0:T(8,128)(2,1)S(1)}, u32[]{:S(2)}, u32[]{:S(2)}) collective-permute-start(bf16[256,1024]{1,0:T(8,128)(2,1)} %get-tuple-element.67), channel_id=1, source_target_pairs={{0,6},{1,7},{2,0},{3,1},{4,2},{5,3},{6,4},{7,5},{8,14},{9,15},{10,... | collective-permute-start | bytes 1572872 | tf_op jit(solution)/shard_map/ppermute | solution.py:444
  39.2 13.5 %collective-permute-start.2 = (bf16[256,1024]{1,0:T(8,128)(2,1)}, bf16[256,1024]{1,0:T(8,128)(2,1)S(1)}, u32[]{:S(2)}, u32[]{:S(2)}) collective-permute-start(bf16[256,1024]{1,0:T(8,128)(2,1)} %get-tuple-element.68), channel_id=1, source_target_pairs={{0,2},{1,3},{2,4},{3,5},{4,6},{5,7},{6,0},{7,1},{8,10},{9,11},{10,... | collective-permute-start | bytes 1572872 | tf_op jit(solution)/shard_map/ppermute | solution.py:444
  39.4 4.5 %collective-permute-start.10 = (f32[4,4]{1,0:T(4,128)S(1)}, f32[4,4]{1,0:T(4,128)S(1)}, u32[]{:S(2)}, u32[]{:S(2)}) collective-permute-start(f32[4,4]{1,0:T(4,128)S(1)} %add_add_fusion.3), channel_id=1, source_target_pairs={{0,96},{8,104},{16,112},{24,120},{32,0},{40,8},{48,16},{56,24},{64... | collective-permute-start | bytes 200 | tf_op jit(solution)/shard_map/ppermute | solution.py:389
  43.1 3.9 %collective-permute-start.9 = (f32[4,4]{1,0:T(4,128)S(1)}, f32[4,4]{1,0:T(4,128)S(1)}, u32[]{:S(2)}, u32[]{:S(2)}) collective-permute-start(f32[4,4]{1,0:T(4,128)S(1)} %add_add_fusion.3), channel_id=1, source_target_pairs={{0,64},{8,72},{16,80},{24,88},{32,96},{40,104},{48,112},{56,120},{... | collective-permute-start | bytes 200 | tf_op jit(solution)/shard_map/ppermute | solution.py:389
  43.9 4.2 %collective-permute-start.8 = (f32[4,4]{1,0:T(4,128)S(1)}, f32[4,4]{1,0:T(4,128)S(1)}, u32[]{:S(2)}, u32[]{:S(2)}) collective-permute-start(f32[4,4]{1,0:T(4,128)S(1)} %add_add_fusion.3), channel_id=1, source_target_pairs={{0,32},{8,40},{16,48},{24,56},{32,64},{40,72},{48,80},{56,88},{64,... | collective-permute-start | bytes 200 | tf_op jit(solution)/shard_map/ppermute | solution.py:389
  53.5 3.2 %collective-permute-start.11 = (f32[8,256]{1,0:T(8,128)S(1)}, f32[8,256]{1,0:T(8,128)S(1)}, u32[]{:S(2)}, u32[]{:S(2)}) collective-permute-start(f32[8,256]{1,0:T(8,128)S(1)} %get-tuple-element.43), channel_id=1, source_target_pairs={{0,1},{1,0},{2,3},{3,2},{4,5},{5,4},{6,7},{7,6},{8,9},{9,8},{10,11... | collective-permute-start | bytes 24584 | tf_op jit(solution)/shard_map/ppermute | solution.py:38
  56.7 2.9 %collective-permute-start.14 = (f32[8,256]{1,0:T(8,128)S(1)}, f32[8,256]{1,0:T(8,128)S(1)}, u32[]{:S(2)}, u32[]{:S(2)}) collective-permute-start(f32[8,256]{1,0:T(8,128)S(1)} %add.71.s0), channel_id=1, source_target_pairs={{0,6},{1,7},{2,0},{3,1},{4,2},{5,3},{6,4},{7,5},{8,14},{9,15},{10,... | collective-permute-start | bytes 24584 | tf_op jit(solution)/shard_map/ppermute | solution.py:455
  57.3 4.1 %collective-permute-start.13 = (f32[8,256]{1,0:T(8,128)S(1)}, f32[8,256]{1,0:T(8,128)S(1)}, u32[]{:S(2)}, u32[]{:S(2)}) collective-permute-start(f32[8,256]{1,0:T(8,128)S(1)} %add.71.s0), channel_id=1, source_target_pairs={{0,4},{1,5},{2,6},{3,7},{4,0},{5,1},{6,2},{7,3},{8,12},{9,13},{10,... | collective-permute-start | bytes 24584 | tf_op jit(solution)/shard_map/ppermute | solution.py:455
  57.3 4.7 %collective-permute-start.12 = (f32[8,256]{1,0:T(8,128)S(1)}, f32[8,256]{1,0:T(8,128)S(1)}, u32[]{:S(2)}, u32[]{:S(2)}) collective-permute-start(f32[8,256]{1,0:T(8,128)S(1)} %add.71.s0), channel_id=1, source_target_pairs={{0,2},{1,3},{2,4},{3,5},{4,6},{5,7},{6,0},{7,1},{8,10},{9,11},{10,... | collective-permute-start | bytes 24584 | tf_op jit(solution)/shard_map/ppermute | solution.py:455
  63.2 12.4 %collective-permute-start.26 = (bf16[256,1024]{1,0:T(8,128)(2,1)}, bf16[256,1024]{1,0:T(8,128)(2,1)S(1)}, u32[]{:S(2)}, u32[]{:S(2)}) collective-permute-start(bf16[256,1024]{1,0:T(8,128)(2,1)} %get-tuple-element.30.refs_0_), channel_id=1, source_target_pairs={{0,6},{1,7},{2,0},{3,1},{4,2},{5,3},{6,4},{7,5},{8,14},{9,15},{10,... | collective-permute-start | bytes 1572872 | tf_op jit(solution)/shard_map/ppermute | solution.py:462
  64.7 23.7 %collective-permute-start.24 = (bf16[256,1024]{1,0:T(8,128)(2,1)}, bf16[256,1024]{1,0:T(8,128)(2,1)S(1)}, u32[]{:S(2)}, u32[]{:S(2)}) collective-permute-start(bf16[256,1024]{1,0:T(8,128)(2,1)} %get-tuple-element.30.refs_0_), channel_id=1, source_target_pairs={{0,4},{1,5},{2,6},{3,7},{4,0},{5,1},{6,2},{7,3},{8,12},{9,13},{10,... | collective-permute-start | bytes 1572872 | tf_op jit(solution)/shard_map/ppermute | solution.py:462
  65.6 25.9 %collective-permute-start.22 = (bf16[256,1024]{1,0:T(8,128)(2,1)}, bf16[256,1024]{1,0:T(8,128)(2,1)S(1)}, u32[]{:S(2)}, u32[]{:S(2)}) collective-permute-start(bf16[256,1024]{1,0:T(8,128)(2,1)} %get-tuple-element.30.refs_0_), channel_id=1, source_target_pairs={{0,2},{1,3},{2,4},{3,5},{4,6},{5,7},{6,0},{7,1},{8,10},{9,11},{10,... | collective-permute-start | bytes 1572872 | tf_op jit(solution)/shard_map/ppermute | solution.py:462
  65.6 26.4 %collective-permute-start.15 = (bf16[256,1024]{1,0:T(8,128)(2,1)}, bf16[256,1024]{1,0:T(8,128)(2,1)S(1)}, u32[]{:S(2)}, u32[]{:S(2)}) collective-permute-start(bf16[256,1024]{1,0:T(8,128)(2,1)} %get-tuple-element.30.refs_0_), channel_id=1, source_target_pairs={{0,1},{1,0},{2,3},{3,2},{4,5},{5,4},{6,7},{7,6},{8,9},{9,8},{10,11... | collective-permute-start | bytes 1572872 | tf_op jit(solution)/shard_map/ppermute | solution.py:38
  75.6 32.5 %collective-permute-start.27 = (bf16[256,1024]{1,0:T(8,128)(2,1)S(1)}, bf16[256,1024]{1,0:T(8,128)(2,1)S(1)}, u32[]{:S(2)}, u32[]{:S(2)}) collective-permute-start(bf16[256,1024]{1,0:T(8,128)(2,1)S(1)} %collective-permute-done.26.refs_6_), channel_id=1, source_target_pairs={{0,1},{1,0},{2,3},{3,2},{4,5},{5,4},{6,7},{7,6},{8,9},{9,8},{10,11... | collective-permute-start | bytes 1572872 | tf_op jit(solution)/shard_map/ppermute | solution.py:38
  88.4 19.6 %collective-permute-start.25 = (bf16[256,1024]{1,0:T(8,128)(2,1)S(1)}, bf16[256,1024]{1,0:T(8,128)(2,1)S(1)}, u32[]{:S(2)}, u32[]{:S(2)}) collective-permute-start(bf16[256,1024]{1,0:T(8,128)(2,1)S(1)} %collective-permute-done.24.refs_4_), channel_id=1, source_target_pairs={{0,1},{1,0},{2,3},{3,2},{4,5},{5,4},{6,7},{7,6},{8,9},{9,8},{10,11... | collective-permute-start | bytes 1572872 | tf_op jit(solution)/shard_map/ppermute | solution.py:38
  91.5 16.6 %collective-permute-start.23 = (bf16[256,1024]{1,0:T(8,128)(2,1)S(1)}, bf16[256,1024]{1,0:T(8,128)(2,1)S(1)}, u32[]{:S(2)}, u32[]{:S(2)}) collective-permute-start(bf16[256,1024]{1,0:T(8,128)(2,1)S(1)} %collective-permute-done.22.refs_2_), channel_id=1, source_target_pairs={{0,1},{1,0},{2,3},{3,2},{4,5},{5,4},{6,7},{7,6},{8,9},{9,8},{10,11... | collective-permute-start | bytes 1572872 | tf_op jit(solution)/shard_map/ppermute | solution.py:38
  92.0 2.7 %collective-permute-start.18 = (f32[1,1024]{1,0:T(1,128)S(1)}, f32[1,1024]{1,0:T(1,128)S(1)}, u32[]{:S(2)}, u32[]{:S(2)}) collective-permute-start(f32[1,1024]{1,0:T(1,128)S(1)} %get-tuple-element.47), channel_id=1, source_target_pairs={{0,24},{8,0},{16,8},{24,16},{32,56},{40,32},{48,40},{56,48},{64,88... | collective-permute-start | bytes 12296 | tf_op jit(solution)/shard_map/ppermute | solution.py:386
  94.0 4.0 %collective-permute-start.17 = (f32[1,1024]{1,0:T(1,128)S(1)}, f32[1,1024]{1,0:T(1,128)S(1)}, u32[]{:S(2)}, u32[]{:S(2)}) collective-permute-start(f32[1,1024]{1,0:T(1,128)S(1)} %get-tuple-element.47), channel_id=1, source_target_pairs={{0,16},{8,24},{16,0},{24,8},{32,48},{40,56},{48,32},{56,40},{64,80... | collective-permute-start | bytes 12296 | tf_op jit(solution)/shard_map/ppermute | solution.py:386
  94.7 4.2 %collective-permute-start.16 = (f32[1,1024]{1,0:T(1,128)S(1)}, f32[1,1024]{1,0:T(1,128)S(1)}, u32[]{:S(2)}, u32[]{:S(2)}) collective-permute-start(f32[1,1024]{1,0:T(1,128)S(1)} %get-tuple-element.47), channel_id=1, source_target_pairs={{0,8},{8,16},{16,24},{24,0},{32,40},{40,48},{48,56},{56,32},{64,72... | collective-permute-start | bytes 12296 | tf_op jit(solution)/shard_map/ppermute | solution.py:386
  98.9 4.6 %collective-permute-start.21 = (f32[1,1024]{1,0:T(1,128)S(1)}, f32[1,1024]{1,0:T(1,128)S(1)}, u32[]{:S(2)}, u32[]{:S(2)}) collective-permute-start(f32[1,1024]{1,0:T(1,128)S(1)} %add_add_fusion.1), channel_id=1, source_target_pairs={{0,96},{8,104},{16,112},{24,120},{32,0},{40,8},{48,16},{56,24},{64... | collective-permute-start | bytes 12296 | tf_op jit(solution)/shard_map/ppermute | solution.py:389
  102.8 4.0 %collective-permute-start.20 = (f32[1,1024]{1,0:T(1,128)S(1)}, f32[1,1024]{1,0:T(1,128)S(1)}, u32[]{:S(2)}, u32[]{:S(2)}) collective-permute-start(f32[1,1024]{1,0:T(1,128)S(1)} %add_add_fusion.1), channel_id=1, source_target_pairs={{0,64},{8,72},{16,80},{24,88},{32,96},{40,104},{48,112},{56,120},{... | collective-permute-start | bytes 12296 | tf_op jit(solution)/shard_map/ppermute | solution.py:389
  103.5 3.9 %collective-permute-start.19 = (f32[1,1024]{1,0:T(1,128)S(1)}, f32[1,1024]{1,0:T(1,128)S(1)}, u32[]{:S(2)}, u32[]{:S(2)}) collective-permute-start(f32[1,1024]{1,0:T(1,128)S(1)} %add_add_fusion.1), channel_id=1, source_target_pairs={{0,32},{8,40},{16,48},{24,56},{32,64},{40,72},{48,80},{56,88},{64,... | collective-permute-start | bytes 12296 | tf_op jit(solution)/shard_map/ppermute | solution.py:389
  109.1 4.3 %copy-start.2 = (bf16[256,1024]{1,0:T(8,128)(2,1)S(1)}, bf16[256,1024]{1,0:T(8,128)(2,1)}, u32[]{:S(2)}) copy-start(bf16[256,1024]{1,0:T(8,128)(2,1)} %get-tuple-element.30.refs_0_) | copy-start | bytes 1572868
  110.6 15.2 %collective-permute-start.28 = (bf16[4,256,256]{2,1,0:T(8,128)(2,1)S(1)}, bf16[4,256,256]{2,1,0:T(8,128)(2,1)S(1)}, u32[]{:S(2)}, u32[]{:S(2)}) collective-permute-start(bf16[4,256,256]{2,1,0:T(8,128)(2,1)S(1)} %get-tuple-element.50), channel_id=1, source_target_pairs={{0,32},{1,9},{2,34},{3,11},{4,36},{5,13},{6,38},{7,15},{8,40},{9,1... | collective-permute-start | bytes 1572872 | tf_op jit(solution)/shard_map/ppermute | solution.py:471
  110.7 15.1 %collective-permute-start.29 = (bf16[4,256,256]{2,1,0:T(8,128)(2,1)S(1)}, bf16[4,256,256]{2,1,0:T(8,128)(2,1)S(1)}, u32[]{:S(2)}, u32[]{:S(2)}) collective-permute-start(bf16[4,256,256]{2,1,0:T(8,128)(2,1)S(1)} %get-tuple-element.51), channel_id=1, source_target_pairs={{0,64},{1,17},{2,66},{3,19},{4,68},{5,21},{6,70},{7,23},{8,72},{9,... | collective-permute-start | bytes 1572872 | tf_op jit(solution)/shard_map/ppermute | solution.py:471
  113.0 13.4 %collective-permute-start.30 = (bf16[4,256,256]{2,1,0:T(8,128)(2,1)S(1)}, bf16[4,256,256]{2,1,0:T(8,128)(2,1)S(1)}, u32[]{:S(2)}, u32[]{:S(2)}) collective-permute-start(bf16[4,256,256]{2,1,0:T(8,128)(2,1)S(1)} %get-tuple-element.52), channel_id=1, source_target_pairs={{0,96},{1,25},{2,98},{3,27},{4,100},{5,29},{6,102},{7,31},{8,104},... | collective-permute-start | bytes 1572872 | tf_op jit(solution)/shard_map/ppermute | solution.py:471
  127.4 9.3 %collective-permute-start.31 = (bf16[4,256,256]{2,1,0:T(8,128)(2,1)S(1)}, bf16[4,256,256]{2,1,0:T(8,128)(2,1)S(1)}, u32[]{:S(2)}, u32[]{:S(2)}) collective-permute-start(bf16[4,256,256]{2,1,0:T(8,128)(2,1)S(1)} %get-tuple-element.55), channel_id=1, source_target_pairs={{0,8},{1,33},{2,10},{3,35},{4,12},{5,37},{6,14},{7,39},{8,16},{9,4... | collective-permute-start | bytes 1572872 | tf_op jit(solution)/shard_map/ppermute | solution.py:478
  127.5 21.5 %collective-permute-start.32 = (bf16[4,256,256]{2,1,0:T(8,128)(2,1)S(1)}, bf16[4,256,256]{2,1,0:T(8,128)(2,1)S(1)}, u32[]{:S(2)}, u32[]{:S(2)}) collective-permute-start(bf16[4,256,256]{2,1,0:T(8,128)(2,1)S(1)} %get-tuple-element.56), channel_id=1, source_target_pairs={{0,24},{1,97},{2,26},{3,99},{4,28},{5,101},{6,30},{7,103},{8,0},{9... | collective-permute-start | bytes 1572872 | tf_op jit(solution)/shard_map/ppermute | solution.py:478
  130.2 18.8 %collective-permute-start.33 = (bf16[4,256,256]{2,1,0:T(8,128)(2,1)S(1)}, bf16[4,256,256]{2,1,0:T(8,128)(2,1)S(1)}, u32[]{:S(2)}, u32[]{:S(2)}) collective-permute-start(bf16[4,256,256]{2,1,0:T(8,128)(2,1)S(1)} %get-tuple-element.57), channel_id=1, source_target_pairs={{0,16},{1,65},{2,18},{3,67},{4,20},{5,69},{6,22},{7,71},{8,24},{9,... | collective-permute-start | bytes 1572872 | tf_op jit(solution)/shard_map/ppermute | solution.py:478
  130.4 19.0 %collective-permute-start.37 = (bf16[4,256,256]{2,1,0:T(8,128)(2,1)S(1)}, bf16[4,256,256]{2,1,0:T(8,128)(2,1)S(1)}, u32[]{:S(2)}, u32[]{:S(2)}) collective-permute-start(bf16[4,256,256]{2,1,0:T(8,128)(2,1)S(1)} %get-tuple-element.58.refs_0_), channel_id=1, source_target_pairs={{0,1},{1,0},{2,3},{3,2},{4,5},{5,4},{6,7},{7,6},{8,9},{9,8},{10,11... | collective-permute-start | bytes 1572872 | tf_op jit(solution)/shard_map/ppermute | solution.py:38
  136.7 18.6 %collective-permute-start.34 = (bf16[4,256,256]{2,1,0:T(8,128)(2,1)S(1)}, bf16[4,256,256]{2,1,0:T(8,128)(2,1)S(1)}, u32[]{:S(2)}, u32[]{:S(2)}) collective-permute-start(bf16[4,256,256]{2,1,0:T(8,128)(2,1)S(1)} %collective-permute-done.31.refs_0_), channel_id=1, source_target_pairs={{0,1},{1,0},{2,3},{3,2},{4,5},{5,4},{6,7},{7,6},{8,9},{9,8},{10,11... | collective-permute-start | bytes 1572872 | tf_op jit(solution)/shard_map/ppermute | solution.py:38
  149.0 6.3 %collective-permute-start.35 = (bf16[4,256,256]{2,1,0:T(8,128)(2,1)S(1)}, bf16[4,256,256]{2,1,0:T(8,128)(2,1)S(1)}, u32[]{:S(2)}, u32[]{:S(2)}) collective-permute-start(bf16[4,256,256]{2,1,0:T(8,128)(2,1)S(1)} %collective-permute-done.32.refs_1_), channel_id=1, source_target_pairs={{0,1},{1,0},{2,3},{3,2},{4,5},{5,4},{6,7},{7,6},{8,9},{9,8},{10,11... | collective-permute-start | bytes 1572872 | tf_op jit(solution)/shard_map/ppermute | solution.py:38
  149.0 6.3 %collective-permute-start.36 = (bf16[4,256,256]{2,1,0:T(8,128)(2,1)S(1)}, bf16[4,256,256]{2,1,0:T(8,128)(2,1)}, u32[]{:S(2)}, u32[]{:S(2)}) collective-permute-start(bf16[4,256,256]{2,1,0:T(8,128)(2,1)S(1)} %collective-permute-done.33.refs_2_), channel_id=1, source_target_pairs={{0,1},{1,0},{2,3},{3,2},{4,5},{5,4},{6,7},{7,6},{8,9},{9,8},{10,11... | collective-permute-start | bytes 1572872 | tf_op jit(solution)/shard_map/ppermute | solution.py:38
  (4 other events, 3.9 us)
Sparse Core Ops, SparseCore 0:
  10.1 74.1 all-gather.1

commit v2 on v1

v2 whole, which is shorter than its diff:
```python
import functools

import jax
import jax.numpy as jnp
from jax import lax
from jax.experimental import pallas as pl
from jax.experimental.pallas import tpu as pltpu
from jax.sharding import PartitionSpec as P

BF = jnp.bfloat16
F32 = jnp.float32
LIMIT = 48 * 1024 * 1024
EXTRA = 16
GROUPS = 4
CORE_SWAP = [(t, t ^ 1) for t in range(8)]


def x_shift(k):
    return [(t, ((t // 2 + k) % 4) * 2 + t % 2) for t in range(8)]


def plane_shift(stage, k):
    pairs = []
    for d in range(16):
        for t in range(8):
            z, y = d // 4, d % 4
            if (t % 2) == stage:
                z = (z + k) % 4
            else:
                y = (y + k) % 4
            pairs.append((d * 8 + t, (z * 4 + y) * 8 + t))
    return pairs


def scattered(step):
    return [(d * 8 + t, ((d + 2 * t + step) % 16) * 8 + t) for d in range(16) for t in range(8)]


def swap(value):
    return lax.ppermute(value, "tensor", CORE_SWAP)


def params():
    return pltpu.CompilerParams(vmem_limit_bytes=LIMIT)


def partial_kernel(jobs, where, attention, w, *refs):
    ins = sum(1 for job in jobs if job[2])
    got, outs = refs[:ins], refs[ins:-3]
    att, buf, sems = refs[-3:]
    x, c = where[2], where[3]
    step = buf.shape[1]
    copies = []
    for shift, other, _, _ in jobs:
        piece = lax.rem(x + shift, 4) * 2 + (1 - c if other else c)
        for h in range(2):
            row = pl.multiple_of((piece * 2 + h) * step, step)
            n = len(copies)
            copies.append(pltpu.make_async_copy(w.at[pl.ds(row, step)], buf.at[n], sems.at[n]))
    left = pltpu.make_async_copy(attention, att, sems.at[len(copies)])
    left.start()
    for copy in copies:
        copy.start()
    left.wait()
    used = 0
    for n, (_, _, add, _) in enumerate(jobs):
        if add:
            used += 1

        for h in range(2):
            copies[2 * n + h].wait()

        @pl.loop(0, 2)
        def _(h, n=n, add=add, used=used):
            columns = pl.ds(pl.multiple_of(h * step, step), step)
            term = lax.dot_general(
                att[...], buf[2 * n + h], (((1,), (1,)), ((), ())), preferred_element_type=F32
            )
            if add:
                term += got[used - 1][:, columns].astype(F32)
            outs[n][:, columns] = term.astype(outs[n].dtype)


def partial_products(where, attention, out_proj, jobs, got=()):
    rows, depth = attention.shape
    width = out_proj.shape[0] // 8
    step = width // 2
    count = 2 * len(jobs)
    vmem = pl.BlockSpec(memory_space=pltpu.VMEM)
    far = pl.BlockSpec(memory_space=pltpu.HBM)
    return pl.pallas_call(
        functools.partial(partial_kernel, jobs),
        in_specs=[pl.BlockSpec(memory_space=pltpu.SMEM), far, far] + [vmem] * len(got),
        out_specs=[vmem] * len(jobs),
        out_shape=[jax.ShapeDtypeStruct((rows, width), job[3]) for job in jobs],
        scratch_shapes=[
            pltpu.VMEM((rows, depth), BF),
            pltpu.VMEM((count, step, depth), BF),
            pltpu.SemaphoreType.DMA((count + 1,)),
        ],
        compiler_params=params(),
        cost_estimate=pl.CostEstimate(
            flops=count * rows * depth * width,
            bytes_accessed=count * width * depth,
            transcendentals=0,
        ),
        name="partial",
    )(where, attention, out_proj, *got)


def row_sums(value):
    rows, width = value.shape
    part = value[:, 0:128]
    for i in range(1, width // 128):
        part = part + value[:, i * 128 : (i + 1) * 128]
    return jnp.sum(part.T, axis=0, keepdims=True)


def hidden_kernel(own, sent, r1, r2, r3, residual, cot, gain, stats, hidden, sums):
    h = own[...] + sent[...].astype(F32) + residual[...].astype(F32)
    h = h + r1[...].astype(F32) + r2[...].astype(F32) + r3[...].astype(F32)
    hidden[...] = h
    scaled = cot[...].astype(F32) * gain[...].astype(F32)
    first = row_sums(h * h)
    second = row_sums(scaled * h)
    sums[...] = jnp.concatenate([first, second, stats[...], jnp.zeros((5, 128), F32)], axis=0)


def hidden_call(own, sent, r1, r2, r3, residual, cot, gain, stats):
    rows, width = own.shape
    big = pl.BlockSpec((128, width), lambda i: (i, 0))
    return pl.pallas_call(
        hidden_kernel,
        grid=(rows // 128,),
        in_specs=[big] * 7
        + [pl.BlockSpec((1, width), lambda i: (0, 0)), pl.BlockSpec((1, 128), lambda i: (0, 0))],
        out_specs=[big, pl.BlockSpec((8, 128), lambda i: (0, i))],
        out_shape=[
            jax.ShapeDtypeStruct((rows, width), F32),
            jax.ShapeDtypeStruct((8, rows), F32),
        ],
        compiler_params=params(),
        cost_estimate=pl.CostEstimate(
            flops=12 * rows * width, bytes_accessed=20 * rows * width, transcendentals=0
        ),
        name="hidden",
    )(own, sent, r1, r2, r3, residual, cot, gain, stats)


def column(row):
    return jnp.broadcast_to(row, (128, 128)).T


def spread(col, width):
    return jnp.concatenate([col] * (width // 128), axis=1)


def split_rows(value):
    high = value.astype(BF)
    rest = value - high.astype(F32)
    middle = rest.astype(BF)
    low = (rest - middle.astype(F32)).astype(BF)
    empty = jnp.zeros((EXTRA - 3, value.shape[1]), F32)
    parts = [high.astype(F32), middle.astype(F32), low.astype(F32), empty]
    return jnp.concatenate(parts, axis=0).astype(BF)


def joined(block):
    return jnp.sum(block.astype(F32), axis=0, keepdims=True)


def grad_kernel(
    features, tokens, hidden, cot, gain, s0, s1, s2, s3, info, grad, total
):
    i = pl.program_id(0)
    width = hidden.shape[1]
    sums = s0[...] + s1[...] + s2[...] + s3[...]
    square, inner = sums[0:1, :], sums[1:2, :]
    inverse = lax.rsqrt(square / features + 1e-06)
    reward, kept, group = info[0:1, :], info[1:2, :], info[2:3, :]

    def picked(offset):
        value = jnp.zeros_like(reward)
        for g in range(GROUPS):
            stat = jnp.broadcast_to(sums[2:3, offset + g : offset + g + 1], value.shape)
            value = jnp.where(group == float(g), stat, value)
        return value

    count = jnp.maximum(picked(0), 1.0)
    mean = picked(GROUPS) / count
    variance = picked(2 * GROUPS) / count - mean * mean
    advantage = (reward - mean) / jnp.sqrt(jnp.maximum(variance, 1.0))
    kept_tokens = jnp.broadcast_to(sums[2:3, 3 * GROUPS : 3 * GROUPS + 1], reward.shape)
    coef = -advantage * kept * tokens / jnp.maximum(kept_tokens, 1.0)
    first = coef * inverse
    second = coef * (inverse * inverse * inverse * inner / features)
    first = spread(column(first), width)
    second = spread(column(second), width)
    h = hidden[...]
    c = cot[...].astype(F32)
    grad[...] = (first * (c * gain[...].astype(F32)) - h * second).astype(BF)
    term = jnp.sum(first * c * h, axis=0, keepdims=True)
    @pl.when(i == 0)
    def _():
        total[...] = term

    @pl.when(i != 0)
    def _():
        total[...] += term


def grad_call(features, tokens, hidden, cot, gain, s0, s1, s2, s3, info):
    rows, width = hidden.shape
    big = pl.BlockSpec((128, width), lambda i: (i, 0))
    small = pl.BlockSpec((8, 128), lambda i: (0, i))
    return pl.pallas_call(
        functools.partial(grad_kernel, float(features), float(tokens)),
        grid=(rows // 128,),
        in_specs=[
            big,
            big,
            pl.BlockSpec((1, width), lambda i: (0, 0)),
        ]
        + [small] * 5,
        out_specs=[big, pl.BlockSpec((1, width), lambda i: (0, 0))],
        out_shape=[
            jax.ShapeDtypeStruct((rows, width), BF),
            jax.ShapeDtypeStruct((1, width), F32),
        ],
        compiler_params=params(),
        cost_estimate=pl.CostEstimate(
            flops=12 * rows * width, bytes_accessed=10 * rows * width, transcendentals=0
        ),
        name="grad",
    )(hidden, cot, gain, s0, s1, s2, s3, info)


def attention_kernel(where, *refs):
    pieces, w, out, buf, acc, sems = refs[:8], refs[8], refs[9], refs[10], refs[11], refs[12]
    x, c = where[2], where[3]
    step = buf.shape[1]
    copies = []
    for n in range(8):
        holder = (1 - c) if n % 2 else c
        piece = lax.rem(x + 4 - n // 2, 4) * 2 + holder
        row = pl.multiple_of(piece * step, step)
        copies.append(pltpu.make_async_copy(w.at[pl.ds(row, step)], buf.at[n], sems.at[n]))
        copies[-1].start()
    for n in range(8):
        copies[n].wait()
        term = jnp.dot(pieces[n][...], buf[n], preferred_element_type=F32)
        if n == 0:
            acc[...] = term
        elif n < 7:
            acc[...] += term
        else:
            out[...] = (acc[...] + term).astype(BF)


def attention_call(where, pieces, out_proj):
    rows, width = pieces[0].shape
    depth = out_proj.shape[1]
    vmem = pl.BlockSpec(memory_space=pltpu.VMEM)
    return pl.pallas_call(
        attention_kernel,
        in_specs=[pl.BlockSpec(memory_space=pltpu.SMEM)]
        + [vmem] * 8
        + [pl.BlockSpec(memory_space=pltpu.HBM)],
        out_specs=vmem,
        scratch_shapes=[
            pltpu.VMEM((8, width, depth), BF),
            pltpu.VMEM((rows, depth), F32),
            pltpu.SemaphoreType.DMA((8,)),
        ],
        out_shape=jax.ShapeDtypeStruct((rows, depth), BF),
        compiler_params=params(),
        cost_estimate=pl.CostEstimate(
            flops=2 * rows * depth * width * 8,
            bytes_accessed=2 * 8 * width * depth,
            transcendentals=0,
        ),
        name="attention_grad",
    )(where, *pieces, out_proj)


def first_pack_kernel(where, *refs):
    pieces, gain, outs = refs[:8], refs[8], refs[9:13]
    z, y, x, c = where[0], where[1], where[2], where[3]
    half = outs[0].shape[2]
    rows = outs[0].shape[1] - EXTRA
    for j in range(4):
        block = split_rows(gain[:, j * half : (j + 1) * half])
        for s in range(4):
            outs[s][j, rows : rows + EXTRA, :] = block
    for k in range(4):
        big_z = lax.rem(x + 4 - k, 4)
        for other in range(2):
            holder = (1 - c) if other else c
            for h in range(2):
                big_y = 2 * holder + h
                slot = jnp.where(c == 0, lax.rem(big_z + 4 - z, 4), lax.rem(big_y + 4 - y, 4))
                j = jnp.where(c == 0, big_y, big_z)
                start = pl.multiple_of(h * 2 * half + c * half, half)
                for s in range(4):

                    @pl.when(slot == s)
                    def _(s=s, j=j, start=start, piece=pieces[k * 2 + other]):
                        @pl.loop(0, rows // 64)
                        def _(r):
                            band = pl.ds(pl.multiple_of(r * 64, 64), 64)
                            outs[s][j, band, :] = piece[band, pl.ds(start, half)]


def second_pack_kernel(where, *refs):
    parts, outs = refs[:4], refs[4:8]
    rows = outs[0].shape[1] - EXTRA
    mine = jnp.where(where[3] == 0, where[1], where[0])
    tail = pl.ds(rows, EXTRA)
    for j in range(4):
        block = split_rows(sum(joined(part[j, tail, :]) for part in parts))
        for u in range(4):
            outs[u][j, tail, :] = block
    for u in range(4):
        j = lax.rem(mine + u, 4)
        for s in range(4):

            @pl.loop(0, rows // 64)
            def _(r, u=u, s=s, j=j):
                band = pl.ds(pl.multiple_of(r * 64, 64), 64)
                outs[u][s, band, :] = parts[s][j, band, :]


def pack_call(kernel, where, inputs, rows, half, name):
    vmem = pl.BlockSpec(memory_space=pltpu.VMEM)
    return pl.pallas_call(
        kernel,
        in_specs=[pl.BlockSpec(memory_space=pltpu.SMEM)] + [vmem] * len(inputs),
        out_specs=[vmem] * 4,
        out_shape=[jax.ShapeDtypeStruct((4, rows + EXTRA, half), BF)] * 4,
        compiler_params=pltpu.CompilerParams(vmem_limit_bytes=16 * 1024 * 1024),
        cost_estimate=pl.CostEstimate(
            flops=0, bytes_accessed=64 * rows * half, transcendentals=0
        ),
        name=name,
    )(where, *inputs)


def projection_kernel(members, first, last, where, gathered, *refs):
    count = len(members)
    mine, theirs = refs[:count], refs[count : 2 * count]
    refs = refs[2 * count :]
    before = None if first else refs[0]
    out = refs[0 if first else 1]
    z, y, c = where[0], where[1], where[3]
    half = out.shape[-2] // (2 if last else 1)
    rows = mine[0].shape[1] - EXTRA
    for n, parts in ((0, mine), (1, theirs)):
        z_first = (c == 0) if n == 0 else (c == 1)
        total = None if first else before[n]
        for m, u in enumerate(members):
            for s in range(4):
                dz, dy = jnp.where(z_first, s, u), jnp.where(z_first, u, s)
                row = lax.rem(z + 4 - dz, 4) * 4 + lax.rem(y + 4 - dy, 4)
                row = pl.multiple_of(row * rows, rows)
                term = lax.dot_general(
                    parts[m][s, 0:rows, :],
                    gathered[pl.ds(row, rows), :],
                    (((0,), (0,)), ((), ())),
                    preferred_element_type=F32,
                )
                total = term if total is None else total + term
        if last:
            holder = c if n == 0 else 1 - c
            start = pl.multiple_of(holder * half, half)
            out[pl.ds(start, half), :] = total.astype(BF)
        else:
            out[n] = total


def projection_call(where, mine, theirs, gathered, members, before, last):
    rows, half = mine[0].shape[1] - EXTRA, mine[0].shape[2]
    depth = gathered.shape[1]
    vmem = pl.BlockSpec(memory_space=pltpu.VMEM)
    blocks = 8 * len(members)
    picked = [mine[u] for u in members] + [theirs[u] for u in members]
    first = before is None
    return pl.pallas_call(
        functools.partial(projection_kernel, members, first, last),
        in_specs=[pl.BlockSpec(memory_space=pltpu.SMEM), vmem]
        + [vmem] * len(picked)
        + ([] if first else [vmem]),
        out_specs=vmem,
        out_shape=jax.ShapeDtypeStruct((2 * half, depth), BF)
        if last
        else jax.ShapeDtypeStruct((2, half, depth), F32),
        compiler_params=pltpu.CompilerParams(vmem_limit_bytes=24 * 1024 * 1024),
        cost_estimate=pl.CostEstimate(
            flops=2 * blocks * rows * half * depth,
            bytes_accessed=2 * blocks * rows * (depth + half),
            transcendentals=0,
        ),
        name="projection_grad",
    )(where, gathered, *picked, *([] if first else [before]))


def local_stats(rewards, group_ids, kept_flags, lengths):
    kept = kept_flags.astype(F32)
    onehot = (group_ids[None, :] == jnp.arange(GROUPS, dtype=jnp.int32)[:, None]).astype(F32)
    values = [
        jnp.sum(onehot * kept[None, :], axis=1),
        jnp.sum(onehot * (kept * rewards)[None, :], axis=1),
        jnp.sum(onehot * (kept * rewards * rewards)[None, :], axis=1),
        jnp.sum(kept * lengths[0].astype(F32))[None],
        jnp.zeros((128 - 3 * GROUPS - 1,), F32),
    ]
    return jnp.concatenate(values)[None, :]


def token_info(rewards, group_ids, kept_flags, lengths, rows):
    ends = jnp.cumsum(lengths[0])
    position = jnp.arange(rows, dtype=jnp.int32)
    segment = jnp.sum((position[None, :] >= ends[:, None]).astype(jnp.int32), axis=0)
    picks = (segment[None, :] == jnp.arange(rewards.shape[0], dtype=jnp.int32)[:, None]).astype(F32)
    values = [rewards, kept_flags.astype(F32), group_ids.astype(F32)]
    found = [jnp.sum(picks * value[:, None], axis=0, keepdims=True) for value in values]
    return jnp.concatenate(found + [jnp.zeros((5, rows), F32)], axis=0)


def shards(
    attention, residual, out_proj, norm_gain, cotangent, rewards, group_ids, kept_flags, lengths
):
    rows = attention.shape[0]
    features = out_proj.shape[0]
    d, t = lax.axis_index("dp"), lax.axis_index("tensor")
    where = jnp.stack([d // 4, d % 4, t // 2, t % 2]).astype(jnp.int32)
    gain = norm_gain[None, :]

    gathered = lax.all_gather(attention, "dp", axis=0, tiled=True)

    arrived = {}
    send2, keep2, send1, send3 = partial_products(
        where,
        attention,
        out_proj,
        [(2, True, False, BF), (2, False, False, F32), (1, True, False, BF), (3, True, False, BF)],
    )
    both = (keep2 + swap(send2).astype(F32)).astype(BF)
    arrived[2] = lax.ppermute(both, "tensor", x_shift(2))
    late_where, _ = lax.optimization_barrier((where, both))
    first, third, send0, keep0 = partial_products(
        late_where,
        attention,
        out_proj,
        [(1, False, True, BF), (3, False, True, BF), (0, True, False, BF), (0, False, False, F32)],
        [swap(send1), swap(send3)],
    )
    arrived[1] = lax.ppermute(first, "tensor", x_shift(1))
    arrived[3] = lax.ppermute(third, "tensor", x_shift(3))
    sent0 = swap(send0)
    stats = local_stats(rewards, group_ids, kept_flags, lengths)
    info = token_info(rewards, group_ids, kept_flags, lengths, rows)
    stats, info, arrived[2], _ = lax.optimization_barrier((stats, info, arrived[2], sent0))
    stats = sum(lax.ppermute(stats, ("dp", "tensor"), scattered(step)) for step in (0, 1))
    residual, info = lax.optimization_barrier((residual, info))
    hidden, sums = hidden_call(
        keep0, sent0, arrived[1], arrived[2], arrived[3], residual, cotangent, gain, stats
    )

    chip = sums + swap(sums)
    others = [lax.ppermute(chip, "tensor", x_shift(k)) for k in (1, 2, 3)]
    tokens = rows * lax.axis_size("dp")
    grad_residual, gain_term = grad_call(
        features, tokens, hidden, cotangent, gain, chip, *others, info
    )

    pieces = []
    for k in range(4):
        piece = grad_residual if k == 0 else lax.ppermute(grad_residual, "tensor", x_shift(k))
        pieces.extend([piece, swap(piece)])

    half = features // 32
    sends = pack_call(first_pack_kernel, where, pieces + [gain_term], rows, half, "first_pack")
    parts = [sends[0]] + [
        lax.ppermute(sends[k], ("dp", "tensor"), plane_shift(0, k)) for k in (1, 2, 3)
    ]
    late_where, _ = lax.optimization_barrier((where, sends))
    grad_attention = attention_call(late_where, pieces, out_proj)
    pack_where, _ = lax.optimization_barrier((where, grad_attention))
    sends = pack_call(second_pack_kernel, pack_where, parts, rows, half, "second_pack")
    mine = [sends[0]] + [
        lax.ppermute(sends[k], ("dp", "tensor"), plane_shift(1, k)) for k in (1, 2, 3)
    ]
    theirs = [swap(mine[0]), None, None, None]
    total = projection_call(where, mine, theirs, gathered, (0,), None, False)
    for k in (1, 3, 2):
        mine[k], total = lax.optimization_barrier((mine[k], total))
        theirs[k] = swap(mine[k])
    total = projection_call(where, mine, theirs, gathered, (1, 3, 2), total, True)
    tails = [part[:, rows:, :].astype(F32) for part in mine]
    grad_gain = jnp.sum(sum(tails), axis=1).reshape(-1)
    return (grad_attention, total, grad_residual, grad_gain)


def solution(mesh):
    return jax.shard_map(
        shards,
        mesh=mesh,
        in_specs=(
            P("dp", "tensor"),
            P("dp", "tensor"),
            P(None, "tensor"),
            P("tensor"),
            P("dp", "tensor"),
            P("dp"),
            P("dp"),
            P("dp"),
            P("dp", None),
        ),
        out_specs=(P("dp", "tensor"), P("dp", "tensor"), P("dp", "tensor"), P("tensor")),
        check_vma=False,
    )
```

time: 173 us -> 147 us (0.85)
  starting transfers between devices: 68.4 us -> 44.5 us
  local copies, waits for them, and re-layouts: 6.32 us -> 9.81 us
  other arithmetic: 4.42 us -> 2.31 us
  Pallas kernels: 37.7 us -> 35.6 us
    ppermute x11 -> x13, starting transfers between devices: 38.6 us -> 17.6 us  [swap(): return lax.ppermute(value, 'tensor', CORE_SWAP)]
    ppermute x14 -> x4, waiting for transfers between devices: 17.2 us -> 4.75 us  [the longest x2 4.22 us: shards(): lax.ppermute(stats, ('dp', 'tensor'), scattered(step))]
    ppermute x14 -> x4, starting transfers between devices: 17.2 us -> 9.09 us  [the longest x2 6.4 us: shards(): lax.ppermute(stats, ('dp', 'tensor'), scattered(step))]
    pallas_call x2, Pallas kernels: 14 us -> 6.75 us  [projection_call(): pl.pallas_call(functools.partial(projection_kernel, members, first, last)...]
    ppermute x3, waiting for transfers between devices: 0.27 us -> 7.47 us  [shards(): lax.ppermute(sends[k], ('dp', 'tensor'), plane_shift(1, k))]
    unnamed x26 -> x31, local copies, waits for them, and re-layouts: 3.99 us -> 9 us
    ppermute x3, waiting for transfers between devices: 10.9 us -> 15.9 us  [shards(): lax.ppermute(grad_residual, 'tensor', x_shift(k))]
    pallas_call x3, Pallas kernels: 12.5 us -> 15.4 us  [the longest x2 14 us: partial_products(): pl.pallas_call(functools.partial(partial_kernel, jobs), in_specs=[pl.Bloc...]
  transfers between devices with their start and end apart: 39 -> 31, of which waited for: 21 -> 15; matrix products, arithmetic and copies ran while one was open for 4% -> 3% of each run, Pallas kernels for 16% -> 21%
where the time goes in v2:
time: 147 us; the launch traced here: 146 us
  starting transfers between devices  44.5 us (30%)
  waiting for transfers between devices  39.7 us (27%)
  Pallas kernels  35.6 us (24%)
  between operations  14.2 us (10%)
  local copies, waits for them, and re-layouts  9.81 us (7%)
  other arithmetic  2.31 us (2%)
    ppermute x13, starting transfers between devices, swap(): return lax.ppermute(value, 'tensor', CORE_SWAP)  17.6 us
    ppermute x3, waiting for transfers between devices, shards(): lax.ppermute(grad_residual, 'tensor', x_shift(k))  15.9 us
    pallas_call x2, Pallas kernels, partial_products(): pl.pallas_call(functools.partial(partial_kernel, jobs), in_specs=[pl.Bloc...  14 us
    unnamed x31, local copies, waits for them, and re-layouts  9 us
    pallas_call x1, Pallas kernels, attention_call(): pl.pallas_call(attention_kernel, in_specs=[pl.BlockSpec(memory_space=pltp...  7.98 us
    ppermute x3, waiting for transfers between devices, shards(): lax.ppermute(sends[k], ('dp', 'tensor'), plane_shift(1, k))  7.47 us
    pallas_call x2, Pallas kernels, projection_call(): pl.pallas_call(functools.partial(projection_kernel, members, first, last)...  6.75 us
    ppermute x2, starting transfers between devices, shards(): lax.ppermute(stats, ('dp', 'tensor'), scattered(step))  6.4 us
  transfers between devices with their start and end apart: 31, of which 15 were waited for; matrix products, arithmetic and copies ran while one was open for 3% of the time, Pallas kernels for 21%

profile of v2, /device:TPU:1, one launch (start us, length us, event | category | flops | bytes accessed | tf_op | source)
XLA Modules:
  0.0 146.1 jit_solution(11863156523010173290)
XLA Ops:
  8.0 1.0 copy-done.2
  9.1 6.8 %partial.2 = (bf16[256,1024]{1,0:T(8,128)(2,1)S(1)}, f32[256,1024]{1,0:T(8,128)S(1)}, bf16[256,1024]{1,0:T(8,128)(2,1)}, bf16[256,1024]{1,0:T(8,128)(2,1)}) custom-call(s32[4]{0:T(128)S(1)} %pad_add_fusion.where, bf16[256,1024]{1,0:T(8,128)(2,1)S(1)} %copy-done.2, bf16[8192,1024]{1,0:T(8,128)(2,1)} %refs_8_.1), custom_call_target="tpu_custom_call" | custom-call | flops 2147483648 | bytes 8388608 | tf_op jit(solution)/shard_map/partial/pallas_call | solution.py:91
  15.9 1.5 %collective-permute-start = (bf16[256,1024]{1,0:T(8,128)(2,1)S(1)}, bf16[256,1024]{1,0:T(8,128)(2,1)S(1)}, u32[]{:S(2)}, u32[]{:S(2)}) collective-permute-start(bf16[256,1024]{1,0:T(8,128)(2,1)S(1)} %get-tuple-element.39), channel_id=1, source_target_pairs={{0,1},{1,0},{2,3},{3,2},{4,5},{5,4},{6,7},{7,6},{8,9},{9,8},{10,11... | collective-permute-start | bytes 1572872 | tf_op jit(solution)/shard_map/ppermute | solution.py:40
  18.9 1.0 add_convert_fusion
  19.9 2.8 %collective-permute-start.5 = (bf16[256,1024]{1,0:T(8,128)(2,1)}, bf16[256,1024]{1,0:T(8,128)(2,1)S(1)}, u32[]{:S(2)}, u32[]{:S(2)}) collective-permute-start(bf16[256,1024]{1,0:T(8,128)(2,1)} %add_convert_fusion), channel_id=1, source_target_pairs={{0,4},{1,5},{2,6},{3,7},{4,0},{5,1},{6,2},{7,3},{8,12},{9,13},{10,... | collective-permute-start | bytes 1572872 | tf_op jit(solution)/shard_map/ppermute | solution.py:448
  22.8 0.8 copy-done.8
  23.6 1.1 copy-done.9
  24.6 7.2 %partial.3 = (bf16[256,1024]{1,0:T(8,128)(2,1)}, bf16[256,1024]{1,0:T(8,128)(2,1)}, bf16[256,1024]{1,0:T(8,128)(2,1)}, f32[256,1024]{1,0:T(8,128)S(1)}) custom-call(s32[4]{0:T(128)S(1)} %pad_add_fusion.where, bf16[256,1024]{1,0:T(8,128)(2,1)S(1)} %copy-done.3, bf16[8192,1024]{1,0:T(8,128)(2,1)} %refs_8_.1, bf16[256,1024]{1,0:T(8,128)(2,1)S(1)} %copy-done.9, ...), custom_call_target="tpu_custom_call" | custom-call | flops 2147483648 | bytes 8388608 | tf_op jit(solution)/shard_map/partial/pallas_call | solution.py:91
  32.9 2.3 %collective-permute-start.6 = (bf16[256,1024]{1,0:T(8,128)(2,1)}, bf16[256,1024]{1,0:T(8,128)(2,1)}, u32[]{:S(2)}, u32[]{:S(2)}) collective-permute-start(bf16[256,1024]{1,0:T(8,128)(2,1)} %get-tuple-element.47), channel_id=1, source_target_pairs={{0,6},{1,7},{2,0},{3,1},{4,2},{5,3},{6,4},{7,5},{8,14},{9,15},{10,... | collective-permute-start | bytes 1572872 | tf_op jit(solution)/shard_map/ppermute | solution.py:458
  36.4 2.8 %collective-permute-start.8 = (f32[1,128]{1,0:T(1,128)S(1)}, f32[1,128]{1,0:T(1,128)S(1)}, u32[]{:S(2)}, u32[]{:S(2)}) collective-permute-start(f32[1,128]{1,0:T(1,128)S(1)} %bitcast.23), channel_id=1, source_target_pairs={{0,8},{1,25},{2,42},{3,59},{4,76},{5,93},{6,110},{7,127},{8,16},{9... | collective-permute-start | bytes 1544 | tf_op jit(solution)/shard_map/ppermute | solution.py:463
  39.2 3.6 %collective-permute-start.7 = (f32[1,128]{1,0:T(1,128)S(1)}, f32[1,128]{1,0:T(1,128)S(1)}, u32[]{:S(2)}, u32[]{:S(2)}) collective-permute-start(f32[1,128]{1,0:T(1,128)S(1)} %bitcast.24), channel_id=1, source_target_pairs={{0,0},{1,17},{2,34},{3,51},{4,68},{5,85},{6,102},{7,119},{8,8},{9,... | collective-permute-start | bytes 1544 | tf_op jit(solution)/shard_map/ppermute | solution.py:463
  42.8 4.2 %collective-permute-done.7 = f32[1,128]{1,0:T(1,128)S(1)} collective-permute-done((f32[1,128]{1,0:T(1,128)S(1)}, f32[1,128]{1,0:T(1,128)S(1)}, u32[]{:S(2)}, u32[]{:S(2)}) %collective-permute-start.7) | collective-permute-done | bytes 544 | tf_op jit(solution)/shard_map/ppermute | solution.py:463
  47.6 1.8 %hidden.1 = (f32[256,1024]{1,0:T(8,128)S(1)}, f32[8,256]{1,0:T(8,128)S(1)}) custom-call(f32[256,1024]{1,0:T(8,128)S(1)} %get-tuple-element.43.own, bf16[256,1024]{1,0:T(8,128)(2,1)S(1)} %collective-permute-done.3.sent, bf16[256,1024]{1,0:T(8,128)(2,1)} %collective-permute-done.4.r1, bf16[256,1024]{1,0:T(8,128)(2,1)S(1)} %collective-permute-done.5.r2, ...), custom_call_target="tpu_custom_call" | custom-call | flops 3145728 | bytes 5242880 | tf_op jit(solution)/shard_map/hidden/pallas_call | solution.py:132
  49.4 0.9 collective-permute-start.9
  50.3 0.8 collective-permute-done.9
  51.2 2.7 %collective-permute-start.12 = (f32[8,256]{1,0:T(8,128)S(1)}, f32[8,256]{1,0:T(8,128)S(1)}, u32[]{:S(2)}, u32[]{:S(2)}) collective-permute-start(f32[8,256]{1,0:T(8,128)S(1)} %add.31.s0), channel_id=1, source_target_pairs={{0,6},{1,7},{2,0},{3,1},{4,2},{5,3},{6,4},{7,5},{8,14},{9,15},{10,... | collective-permute-start | bytes 24584 | tf_op jit(solution)/shard_map/ppermute | solution.py:470
  54.2 0.9 collective-permute-start.10
  55.0 2.8 %collective-permute-done.11.s2 = f32[8,256]{1,0:T(8,128)S(1)} collective-permute-done((f32[8,256]{1,0:T(8,128)S(1)}, f32[8,256]{1,0:T(8,128)S(1)}, u32[]{:S(2)}, u32[]{:S(2)}) %collective-permute-start.11) | collective-permute-done | bytes 8224 | tf_op jit(solution)/shard_map/ppermute | solution.py:470
  58.3 1.4 grad.1
  60.0 1.2 collective-permute-start.16
  61.2 0.8 collective-permute-start.14
  62.0 2.5 %collective-permute-start.13 = (bf16[256,1024]{1,0:T(8,128)(2,1)}, bf16[256,1024]{1,0:T(8,128)(2,1)S(1)}, u32[]{:S(2)}, u32[]{:S(2)}) collective-permute-start(bf16[256,1024]{1,0:T(8,128)(2,1)} %get-tuple-element.36.refs_0_), channel_id=1, source_target_pairs={{0,1},{1,0},{2,3},{3,2},{4,5},{5,4},{6,7},{7,6},{8,9},{9,8},{10,11... | collective-permute-start | bytes 1572872 | tf_op jit(solution)/shard_map/ppermute | solution.py:40
  64.5 7.6 %collective-permute-done.18.refs_6_ = bf16[256,1024]{1,0:T(8,128)(2,1)S(1)} collective-permute-done((bf16[256,1024]{1,0:T(8,128)(2,1)}, bf16[256,1024]{1,0:T(8,128)(2,1)S(1)}, u32[]{:S(2)}, u32[]{:S(2)}) %collective-permute-start.18) | collective-permute-done | bytes 524320 | tf_op jit(solution)/shard_map/ppermute | solution.py:478
  72.1 4.1 %collective-permute-start.19 = (bf16[256,1024]{1,0:T(8,128)(2,1)S(1)}, bf16[256,1024]{1,0:T(8,128)(2,1)S(1)}, u32[]{:S(2)}, u32[]{:S(2)}) collective-permute-start(bf16[256,1024]{1,0:T(8,128)(2,1)S(1)} %collective-permute-done.18.refs_6_), channel_id=1, source_target_pairs={{0,1},{1,0},{2,3},{3,2},{4,5},{5,4},{6,7},{7,6},{8,9},{9,8},{10,11... | collective-permute-start | bytes 1572872 | tf_op jit(solution)/shard_map/ppermute | solution.py:40
  76.2 2.4 %collective-permute-start.17 = (bf16[256,1024]{1,0:T(8,128)(2,1)S(1)}, bf16[256,1024]{1,0:T(8,128)(2,1)S(1)}, u32[]{:S(2)}, u32[]{:S(2)}) collective-permute-start(bf16[256,1024]{1,0:T(8,128)(2,1)S(1)} %collective-permute-done.16.refs_4_), channel_id=1, source_target_pairs={{0,1},{1,0},{2,3},{3,2},{4,5},{5,4},{6,7},{7,6},{8,9},{9,8},{10,11... | collective-permute-start | bytes 1572872 | tf_op jit(solution)/shard_map/ppermute | solution.py:40
  78.5 8.3 %collective-permute-done.14.refs_2_ = bf16[256,1024]{1,0:T(8,128)(2,1)S(1)} collective-permute-done((bf16[256,1024]{1,0:T(8,128)(2,1)}, bf16[256,1024]{1,0:T(8,128)(2,1)S(1)}, u32[]{:S(2)}, u32[]{:S(2)}) %collective-permute-start.14) | collective-permute-done | bytes 524320 | tf_op jit(solution)/shard_map/ppermute | solution.py:478
  87.3 1.5 %collective-permute-done.15.refs_3_ = bf16[256,1024]{1,0:T(8,128)(2,1)S(1)} collective-permute-done((bf16[256,1024]{1,0:T(8,128)(2,1)S(1)}, bf16[256,1024]{1,0:T(8,128)(2,1)S(1)}, u32[]{:S(2)}, u32[]{:S(2)}) %collective-permute-start.15) | collective-permute-done | bytes 524320 | tf_op jit(solution)/shard_map/ppermute | solution.py:40
  88.8 1.0 copy-done.5
  89.9 1.5 %first_pack.1 = (bf16[4,272,256]{2,1,0:T(8,128)(2,1)S(1)}, bf16[4,272,256]{2,1,0:T(8,128)(2,1)S(1)}, bf16[4,272,256]{2,1,0:T(8,128)(2,1)S(1)}, bf16[4,272,256]{2,1,0:T(8,128)(2,1)S(1)}) custom-call(s32[4]{0:T(128)S(1)} %pad_add_fusion.where, bf16[256,1024]{1,0:T(8,128)(2,1)S(1)} %copy-done.5, bf16[256,1024]{1,0:T(8,128)(2,1)S(1)} %collective-permute-done.13.refs_1_, ...), custom_call_target="tpu_custom_call" | custom-call | bytes 4194304 | tf_op jit(solution)/shard_map/first_pack/pallas_call | solution.py:335
  91.4 1.4 collective-permute-start.20
  92.7 2.6 %collective-permute-start.21 = (bf16[4,272,256]{2,1,0:T(8,128)(2,1)S(1)}, bf16[4,272,256]{2,1,0:T(8,128)(2,1)S(1)}, u32[]{:S(2)}, u32[]{:S(2)}) collective-permute-start(bf16[4,272,256]{2,1,0:T(8,128)(2,1)S(1)} %get-tuple-element.58), channel_id=1, source_target_pairs={{0,64},{1,17},{2,66},{3,19},{4,68},{5,21},{6,70},{7,23},{8,72},{9,... | collective-permute-start | bytes 1671176 | tf_op jit(solution)/shard_map/ppermute | solution.py:484
  95.3 1.1 collective-permute-start.22
  96.4 1.0 copy-done.6
  97.5 8.0 %attention_grad.1 = bf16[256,1024]{1,0:T(8,128)(2,1)} custom-call(s32[4]{0:T(128)S(1)} %pad_add_fusion.where, bf16[256,1024]{1,0:T(8,128)(2,1)S(1)} %copy-done.6, bf16[256,1024]{1,0:T(8,128)(2,1)S(1)} %collective-permute-done.13.refs_1_, bf16[256,1024]{1,0:T(8,128)(2,1)S(1)} %collective-permute-done.14.refs_2_, ...), custom_call_target="tpu_custom_call" | custom-call | flops 4294967296 | bytes 16777216 | tf_op jit(solution)/shard_map/attention_grad/pallas_call | solution.py:264
  105.5 3.1 %collective-permute-done.21.refs_2_ = bf16[4,272,256]{2,1,0:T(8,128)(2,1)S(1)} collective-permute-done((bf16[4,272,256]{2,1,0:T(8,128)(2,1)S(1)}, bf16[4,272,256]{2,1,0:T(8,128)(2,1)S(1)}, u32[]{:S(2)}, u32[]{:S(2)}) %collective-permute-start.21) | collective-permute-done | bytes 557088 | tf_op jit(solution)/shard_map/ppermute | solution.py:484
  108.5 2.2 %second_pack.1 = (bf16[4,272,256]{2,1,0:T(8,128)(2,1)S(1)}, bf16[4,272,256]{2,1,0:T(8,128)(2,1)}, bf16[4,272,256]{2,1,0:T(8,128)(2,1)}, bf16[4,272,256]{2,1,0:T(8,128)(2,1)}) custom-call(s32[4]{0:T(128)S(1)} %pad_add_fusion.where, bf16[4,272,256]{2,1,0:T(8,128)(2,1)S(1)} %get-tuple-element.56.refs_0_, ...), custom_call_target="tpu_custom_call" | custom-call | bytes 4194304 | tf_op jit(solution)/shard_map/second_pack/pallas_call | solution.py:335
  110.7 2.2 %collective-permute-start.24 = (bf16[4,272,256]{2,1,0:T(8,128)(2,1)S(1)}, bf16[4,272,256]{2,1,0:T(8,128)(2,1)S(1)}, u32[]{:S(2)}, u32[]{:S(2)}) collective-permute-start(bf16[4,272,256]{2,1,0:T(8,128)(2,1)S(1)} %get-tuple-element.63.refs_0_), channel_id=1, source_target_pairs={{0,1},{1,0},{2,3},{3,2},{4,5},{5,4},{6,7},{7,6},{8,9},{9,8},{10,11... | collective-permute-start | bytes 1671176 | tf_op jit(solution)/shard_map/ppermute | solution.py:40
  112.9 1.2 collective-permute-start.23
  114.2 1.4 collective-permute-start.25
  115.6 1.1 collective-permute-start.26
  116.7 3.4 %copy-done = bf16[4096,1024]{1,0:T(8,128)(2,1)S(1)} copy-done((bf16[4096,1024]{1,0:T(8,128)(2,1)S(1)}, bf16[4096,1024]{1,0:T(8,128)(2,1)}, u32[]{:S(2)}) %copy-start) | copy-done | bytes 8388632
  120.1 1.8 %projection_grad.2.refs_6_ = f32[2,256,1024]{2,1,0:T(8,128)S(1)} custom-call(s32[4]{0:T(128)S(1)} %pad_add_fusion.where, bf16[4096,1024]{1,0:T(8,128)(2,1)S(1)} %copy-done, bf16[4,272,256]{2,1,0:T(8,128)(2,1)S(1)} %get-tuple-element.63.refs_0_, bf16[4,272,256]{2,1,0:T(8,128)(2,1)S(1)} %collective-permute-done.24.refs_1_), custom_call_target="tpu_custom_call" | custom-call | flops 1073741824 | bytes 5242880 | tf_op jit(solution)/shard_map/projection_grad/pallas_call | solution.py:387
  121.9 1.1 collective-permute-done.23.refs_0_
  123.1 6.3 %collective-permute-done.26.refs_2_ = bf16[4,272,256]{2,1,0:T(8,128)(2,1)S(1)} collective-permute-done((bf16[4,272,256]{2,1,0:T(8,128)(2,1)}, bf16[4,272,256]{2,1,0:T(8,128)(2,1)S(1)}, u32[]{:S(2)}, u32[]{:S(2)}) %collective-permute-start.26) | collective-permute-done | bytes 557088 | tf_op jit(solution)/shard_map/ppermute | solution.py:491
  129.4 1.8 %collective-permute-start.29 = (bf16[4,272,256]{2,1,0:T(8,128)(2,1)S(1)}, bf16[4,272,256]{2,1,0:T(8,128)(2,1)S(1)}, u32[]{:S(2)}, u32[]{:S(2)}) collective-permute-start(bf16[4,272,256]{2,1,0:T(8,128)(2,1)S(1)} %collective-permute-done.26.refs_2_), channel_id=1, source_target_pairs={{0,1},{1,0},{2,3},{3,2},{4,5},{5,4},{6,7},{7,6},{8,9},{9,8},{10,11... | collective-permute-start | bytes 1671176 | tf_op jit(solution)/shard_map/ppermute | solution.py:40
  132.7 0.8 collective-permute-done.28.refs_4_
  133.5 0.8 collective-permute-done.27.refs_3_
  134.3 4.9 %projection_grad.3 = bf16[512,1024]{1,0:T(8,128)(2,1)} custom-call(s32[4]{0:T(128)S(1)} %pad_add_fusion.where, bf16[4096,1024]{1,0:T(8,128)(2,1)S(1)} %copy-done.1, bf16[4,272,256]{2,1,0:T(8,128)(2,1)S(1)} %collective-permute-done.23.refs_0_, bf16[4,272,256]{2,1,0:T(8,128)(2,1)S(1)} %collective-permute-done.25.refs_1_, ...), custom_call_target="tpu_custom_call" | custom-call | flops 3221225472 | bytes 15728640 | tf_op jit(solution)/shard_map/projection_grad/pallas_call | solution.py:387
  (73 shorter events, 8.3 us)
Async XLA Ops:
  7.2 109.6 %all-gather.2.cloned.1.call-start = ((), (), s32[]{:S(2)}) async-start(), calls=%async_computation | async-start | bytes 8912896 | tf_op jit(solution)/shard_map/all_gather | solution.py:438
  8.0 1.0 copy-start.2
  9.1 8.8 %copy-start.13 = (s32[4]{0:T(128)S(1)}, s32[4]{0:T(128)}, u32[]{:S(2)}) copy-start(s32[4]{0:T(128)} %param.16) | copy-start | bytes 52
  9.1 8.8 %copy-start.14 = (s32[1,4]{1,0:T(1,128)S(1)}, s32[1,4]{1,0:T(1,128)}, u32[]{:S(2)}) copy-start(s32[1,4]{1,0:T(1,128)} %param.17) | copy-start | bytes 52
  9.1 9.0 %copy-start.12 = (s32[4]{0:T(128)S(1)}, s32[4]{0:T(128)}, u32[]{:S(2)}) copy-start(s32[4]{0:T(128)} %param.15) | copy-start | bytes 52
  9.1 9.1 %copy-start.11 = (f32[4]{0:T(128)S(1)}, f32[4]{0:T(128)}, u32[]{:S(2)}) copy-start(f32[4]{0:T(128)} %param.14) | copy-start | bytes 52
  9.1 14.5 %copy-start.3 = (bf16[256,1024]{1,0:T(8,128)(2,1)S(1)}, bf16[256,1024]{1,0:T(8,128)(2,1)}, u32[]{:S(2)}) copy-start(bf16[256,1024]{1,0:T(8,128)(2,1)} %attention.3) | copy-start | bytes 1572868
  15.9 3.0 %collective-permute-start = (bf16[256,1024]{1,0:T(8,128)(2,1)S(1)}, bf16[256,1024]{1,0:T(8,128)(2,1)S(1)}, u32[]{:S(2)}, u32[]{:S(2)}) collective-permute-start(bf16[256,1024]{1,0:T(8,128)(2,1)S(1)} %get-tuple-element.39), channel_id=1, source_target_pairs={{0,1},{1,0},{2,3},{3,2},{4,5},{5,4},{6,7},{7,6},{8,9},{9,8},{10,11... | collective-permute-start | bytes 1572872 | tf_op jit(solution)/shard_map/ppermute | solution.py:40
  17.4 5.4 %collective-permute-start.1 = (bf16[256,1024]{1,0:T(8,128)(2,1)}, bf16[256,1024]{1,0:T(8,128)(2,1)S(1)}, u32[]{:S(2)}, u32[]{:S(2)}) collective-permute-start(bf16[256,1024]{1,0:T(8,128)(2,1)} %get-tuple-element.41), channel_id=1, source_target_pairs={{0,1},{1,0},{2,3},{3,2},{4,5},{5,4},{6,7},{7,6},{8,9},{9,8},{10,11... | collective-permute-start | bytes 1572872 | tf_op jit(solution)/shard_map/ppermute | solution.py:40
  17.5 6.1 %collective-permute-start.2 = (bf16[256,1024]{1,0:T(8,128)(2,1)}, bf16[256,1024]{1,0:T(8,128)(2,1)}, u32[]{:S(2)}, u32[]{:S(2)}) collective-permute-start(bf16[256,1024]{1,0:T(8,128)(2,1)} %get-tuple-element.42), channel_id=1, source_target_pairs={{0,1},{1,0},{2,3},{3,2},{4,5},{5,4},{6,7},{7,6},{8,9},{9,8},{10,11... | collective-permute-start | bytes 1572872 | tf_op jit(solution)/shard_map/ppermute | solution.py:40
  18.9 23.9 %copy-start.10 = (bf16[1024]{0:T(1024)(128)(2,1)S(1)}, bf16[1024]{0:T(1024)(128)(2,1)}, u32[]{:S(2)}) copy-start(bf16[1024]{0:T(1024)(128)(2,1)} %param.12) | copy-start | bytes 6148
  19.9 27.7 %copy-start.4 = (bf16[256,1024]{1,0:T(8,128)(2,1)S(1)}, bf16[256,1024]{1,0:T(8,128)(2,1)}, u32[]{:S(2)}) copy-start(bf16[256,1024]{1,0:T(8,128)(2,1)} %cot.3) | copy-start | bytes 1572868
  19.9 27.7 %copy-start.7 = (bf16[256,1024]{1,0:T(8,128)(2,1)S(1)}, bf16[256,1024]{1,0:T(8,128)(2,1)}, u32[]{:S(2)}) copy-start(bf16[256,1024]{1,0:T(8,128)(2,1)} %residual) | copy-start | bytes 1572868
  19.9 16.5 %collective-permute-start.5 = (bf16[256,1024]{1,0:T(8,128)(2,1)}, bf16[256,1024]{1,0:T(8,128)(2,1)S(1)}, u32[]{:S(2)}, u32[]{:S(2)}) collective-permute-start(bf16[256,1024]{1,0:T(8,128)(2,1)} %add_convert_fusion), channel_id=1, source_target_pairs={{0,4},{1,5},{2,6},{3,7},{4,0},{5,1},{6,2},{7,3},{8,12},{9,13},{10,... | collective-permute-start | bytes 1572872 | tf_op jit(solution)/shard_map/ppermute | solution.py:448
  22.8 0.8 copy-start.8
  23.6 1.1 copy-start.9
  31.8 4.5 %collective-permute-start.3 = (bf16[256,1024]{1,0:T(8,128)(2,1)}, bf16[256,1024]{1,0:T(8,128)(2,1)S(1)}, u32[]{:S(2)}, u32[]{:S(2)}) collective-permute-start(bf16[256,1024]{1,0:T(8,128)(2,1)} %get-tuple-element.44), channel_id=1, source_target_pairs={{0,1},{1,0},{2,3},{3,2},{4,5},{5,4},{6,7},{7,6},{8,9},{9,8},{10,11... | collective-permute-start | bytes 1572872 | tf_op jit(solution)/shard_map/ppermute | solution.py:40
  32.6 15.0 %collective-permute-start.4 = (bf16[256,1024]{1,0:T(8,128)(2,1)}, bf16[256,1024]{1,0:T(8,128)(2,1)}, u32[]{:S(2)}, u32[]{:S(2)}) collective-permute-start(bf16[256,1024]{1,0:T(8,128)(2,1)} %get-tuple-element.45), channel_id=1, source_target_pairs={{0,2},{1,3},{2,4},{3,5},{4,6},{5,7},{6,0},{7,1},{8,10},{9,11},{10,... | collective-permute-start | bytes 1572872 | tf_op jit(solution)/shard_map/ppermute | solution.py:457
  32.9 14.7 %collective-permute-start.6 = (bf16[256,1024]{1,0:T(8,128)(2,1)}, bf16[256,1024]{1,0:T(8,128)(2,1)}, u32[]{:S(2)}, u32[]{:S(2)}) collective-permute-start(bf16[256,1024]{1,0:T(8,128)(2,1)} %get-tuple-element.47), channel_id=1, source_target_pairs={{0,6},{1,7},{2,0},{3,1},{4,2},{5,3},{6,4},{7,5},{8,14},{9,15},{10,... | collective-permute-start | bytes 1572872 | tf_op jit(solution)/shard_map/ppermute | solution.py:458
  36.4 6.4 %collective-permute-start.8 = (f32[1,128]{1,0:T(1,128)S(1)}, f32[1,128]{1,0:T(1,128)S(1)}, u32[]{:S(2)}, u32[]{:S(2)}) collective-permute-start(f32[1,128]{1,0:T(1,128)S(1)} %bitcast.23), channel_id=1, source_target_pairs={{0,8},{1,25},{2,42},{3,59},{4,76},{5,93},{6,110},{7,127},{8,16},{9... | collective-permute-start | bytes 1544 | tf_op jit(solution)/shard_map/ppermute | solution.py:463
  39.2 7.9 %collective-permute-start.7 = (f32[1,128]{1,0:T(1,128)S(1)}, f32[1,128]{1,0:T(1,128)S(1)}, u32[]{:S(2)}, u32[]{:S(2)}) collective-permute-start(f32[1,128]{1,0:T(1,128)S(1)} %bitcast.24), channel_id=1, source_target_pairs={{0,0},{1,17},{2,34},{3,51},{4,68},{5,85},{6,102},{7,119},{8,8},{9,... | collective-permute-start | bytes 1544 | tf_op jit(solution)/shard_map/ppermute | solution.py:463
  49.4 1.7 %collective-permute-start.9 = (f32[8,256]{1,0:T(8,128)S(1)}, f32[8,256]{1,0:T(8,128)S(1)}, u32[]{:S(2)}, u32[]{:S(2)}) collective-permute-start(f32[8,256]{1,0:T(8,128)S(1)} %get-tuple-element.52), channel_id=1, source_target_pairs={{0,1},{1,0},{2,3},{3,2},{4,5},{5,4},{6,7},{7,6},{8,9},{9,8},{10,11... | collective-permute-start | bytes 24584 | tf_op jit(solution)/shard_map/ppermute | solution.py:40
  51.2 3.9 %collective-permute-start.12 = (f32[8,256]{1,0:T(8,128)S(1)}, f32[8,256]{1,0:T(8,128)S(1)}, u32[]{:S(2)}, u32[]{:S(2)}) collective-permute-start(f32[8,256]{1,0:T(8,128)S(1)} %add.31.s0), channel_id=1, source_target_pairs={{0,6},{1,7},{2,0},{3,1},{4,2},{5,3},{6,4},{7,5},{8,14},{9,15},{10,... | collective-permute-start | bytes 24584 | tf_op jit(solution)/shard_map/ppermute | solution.py:470
  53.8 4.1 %collective-permute-start.11 = (f32[8,256]{1,0:T(8,128)S(1)}, f32[8,256]{1,0:T(8,128)S(1)}, u32[]{:S(2)}, u32[]{:S(2)}) collective-permute-start(f32[8,256]{1,0:T(8,128)S(1)} %add.31.s0), channel_id=1, source_target_pairs={{0,4},{1,5},{2,6},{3,7},{4,0},{5,1},{6,2},{7,3},{8,12},{9,13},{10,... | collective-permute-start | bytes 24584 | tf_op jit(solution)/shard_map/ppermute | solution.py:470
  54.2 4.1 %collective-permute-start.10 = (f32[8,256]{1,0:T(8,128)S(1)}, f32[8,256]{1,0:T(8,128)S(1)}, u32[]{:S(2)}, u32[]{:S(2)}) collective-permute-start(f32[8,256]{1,0:T(8,128)S(1)} %add.31.s0), channel_id=1, source_target_pairs={{0,2},{1,3},{2,4},{3,5},{4,6},{5,7},{6,0},{7,1},{8,10},{9,11},{10,... | collective-permute-start | bytes 24584 | tf_op jit(solution)/shard_map/ppermute | solution.py:470
  59.7 12.4 %collective-permute-start.18 = (bf16[256,1024]{1,0:T(8,128)(2,1)}, bf16[256,1024]{1,0:T(8,128)(2,1)S(1)}, u32[]{:S(2)}, u32[]{:S(2)}) collective-permute-start(bf16[256,1024]{1,0:T(8,128)(2,1)} %get-tuple-element.36.refs_0_), channel_id=1, source_target_pairs={{0,6},{1,7},{2,0},{3,1},{4,2},{5,3},{6,4},{7,5},{8,14},{9,15},{10,... | collective-permute-start | bytes 1572872 | tf_op jit(solution)/shard_map/ppermute | solution.py:478
  60.0 16.2 %collective-permute-start.16 = (bf16[256,1024]{1,0:T(8,128)(2,1)}, bf16[256,1024]{1,0:T(8,128)(2,1)S(1)}, u32[]{:S(2)}, u32[]{:S(2)}) collective-permute-start(bf16[256,1024]{1,0:T(8,128)(2,1)} %get-tuple-element.36.refs_0_), channel_id=1, source_target_pairs={{0,4},{1,5},{2,6},{3,7},{4,0},{5,1},{6,2},{7,3},{8,12},{9,13},{10,... | collective-permute-start | bytes 1572872 | tf_op jit(solution)/shard_map/ppermute | solution.py:478
  61.2 25.6 %collective-permute-start.14 = (bf16[256,1024]{1,0:T(8,128)(2,1)}, bf16[256,1024]{1,0:T(8,128)(2,1)S(1)}, u32[]{:S(2)}, u32[]{:S(2)}) collective-permute-start(bf16[256,1024]{1,0:T(8,128)(2,1)} %get-tuple-element.36.refs_0_), channel_id=1, source_target_pairs={{0,2},{1,3},{2,4},{3,5},{4,6},{5,7},{6,0},{7,1},{8,10},{9,11},{10,... | collective-permute-start | bytes 1572872 | tf_op jit(solution)/shard_map/ppermute | solution.py:478
  62.0 25.3 %collective-permute-start.13 = (bf16[256,1024]{1,0:T(8,128)(2,1)}, bf16[256,1024]{1,0:T(8,128)(2,1)S(1)}, u32[]{:S(2)}, u32[]{:S(2)}) collective-permute-start(bf16[256,1024]{1,0:T(8,128)(2,1)} %get-tuple-element.36.refs_0_), channel_id=1, source_target_pairs={{0,1},{1,0},{2,3},{3,2},{4,5},{5,4},{6,7},{7,6},{8,9},{9,8},{10,11... | collective-permute-start | bytes 1572872 | tf_op jit(solution)/shard_map/ppermute | solution.py:40
  72.1 15.2 %collective-permute-start.19 = (bf16[256,1024]{1,0:T(8,128)(2,1)S(1)}, bf16[256,1024]{1,0:T(8,128)(2,1)S(1)}, u32[]{:S(2)}, u32[]{:S(2)}) collective-permute-start(bf16[256,1024]{1,0:T(8,128)(2,1)S(1)} %collective-permute-done.18.refs_6_), channel_id=1, source_target_pairs={{0,1},{1,0},{2,3},{3,2},{4,5},{5,4},{6,7},{7,6},{8,9},{9,8},{10,11... | collective-permute-start | bytes 1572872 | tf_op jit(solution)/shard_map/ppermute | solution.py:40
  76.2 11.1 %collective-permute-start.17 = (bf16[256,1024]{1,0:T(8,128)(2,1)S(1)}, bf16[256,1024]{1,0:T(8,128)(2,1)S(1)}, u32[]{:S(2)}, u32[]{:S(2)}) collective-permute-start(bf16[256,1024]{1,0:T(8,128)(2,1)S(1)} %collective-permute-done.16.refs_4_), channel_id=1, source_target_pairs={{0,1},{1,0},{2,3},{3,2},{4,5},{5,4},{6,7},{7,6},{8,9},{9,8},{10,11... | collective-permute-start | bytes 1572872 | tf_op jit(solution)/shard_map/ppermute | solution.py:40
  86.8 2.0 %collective-permute-start.15 = (bf16[256,1024]{1,0:T(8,128)(2,1)S(1)}, bf16[256,1024]{1,0:T(8,128)(2,1)S(1)}, u32[]{:S(2)}, u32[]{:S(2)}) collective-permute-start(bf16[256,1024]{1,0:T(8,128)(2,1)S(1)} %collective-permute-done.14.refs_2_), channel_id=1, source_target_pairs={{0,1},{1,0},{2,3},{3,2},{4,5},{5,4},{6,7},{7,6},{8,9},{9,8},{10,11... | collective-permute-start | bytes 1572872 | tf_op jit(solution)/shard_map/ppermute | solution.py:40
  88.8 1.0 copy-start.5
  91.4 14.1 %collective-permute-start.20 = (bf16[4,272,256]{2,1,0:T(8,128)(2,1)S(1)}, bf16[4,272,256]{2,1,0:T(8,128)(2,1)S(1)}, u32[]{:S(2)}, u32[]{:S(2)}) collective-permute-start(bf16[4,272,256]{2,1,0:T(8,128)(2,1)S(1)} %get-tuple-element.57), channel_id=1, source_target_pairs={{0,32},{1,9},{2,34},{3,11},{4,36},{5,13},{6,38},{7,15},{8,40},{9,1... | collective-permute-start | bytes 1671176 | tf_op jit(solution)/shard_map/ppermute | solution.py:484
  92.7 15.8 %collective-permute-start.21 = (bf16[4,272,256]{2,1,0:T(8,128)(2,1)S(1)}, bf16[4,272,256]{2,1,0:T(8,128)(2,1)S(1)}, u32[]{:S(2)}, u32[]{:S(2)}) collective-permute-start(bf16[4,272,256]{2,1,0:T(8,128)(2,1)S(1)} %get-tuple-element.58), channel_id=1, source_target_pairs={{0,64},{1,17},{2,66},{3,19},{4,68},{5,21},{6,70},{7,23},{8,72},{9,... | collective-permute-start | bytes 1671176 | tf_op jit(solution)/shard_map/ppermute | solution.py:484
  95.3 13.2 %collective-permute-start.22 = (bf16[4,272,256]{2,1,0:T(8,128)(2,1)S(1)}, bf16[4,272,256]{2,1,0:T(8,128)(2,1)S(1)}, u32[]{:S(2)}, u32[]{:S(2)}) collective-permute-start(bf16[4,272,256]{2,1,0:T(8,128)(2,1)S(1)} %get-tuple-element.59), channel_id=1, source_target_pairs={{0,96},{1,25},{2,98},{3,27},{4,100},{5,29},{6,102},{7,31},{8,104},... | collective-permute-start | bytes 1671176 | tf_op jit(solution)/shard_map/ppermute | solution.py:484
  96.4 1.0 copy-start.6
  110.7 6.0 %collective-permute-start.24 = (bf16[4,272,256]{2,1,0:T(8,128)(2,1)S(1)}, bf16[4,272,256]{2,1,0:T(8,128)(2,1)S(1)}, u32[]{:S(2)}, u32[]{:S(2)}) collective-permute-start(bf16[4,272,256]{2,1,0:T(8,128)(2,1)S(1)} %get-tuple-element.63.refs_0_), channel_id=1, source_target_pairs={{0,1},{1,0},{2,3},{3,2},{4,5},{5,4},{6,7},{7,6},{8,9},{9,8},{10,11... | collective-permute-start | bytes 1671176 | tf_op jit(solution)/shard_map/ppermute | solution.py:40
  112.9 10.1 %collective-permute-start.23 = (bf16[4,272,256]{2,1,0:T(8,128)(2,1)}, bf16[4,272,256]{2,1,0:T(8,128)(2,1)S(1)}, u32[]{:S(2)}, u32[]{:S(2)}) collective-permute-start(bf16[4,272,256]{2,1,0:T(8,128)(2,1)} %get-tuple-element.62), channel_id=1, source_target_pairs={{0,8},{1,33},{2,10},{3,35},{4,12},{5,37},{6,14},{7,39},{8,16},{9,4... | collective-permute-start | bytes 1671176 | tf_op jit(solution)/shard_map/ppermute | solution.py:491
  114.2 8.9 %collective-permute-start.25 = (bf16[4,272,256]{2,1,0:T(8,128)(2,1)}, bf16[4,272,256]{2,1,0:T(8,128)(2,1)S(1)}, u32[]{:S(2)}, u32[]{:S(2)}) collective-permute-start(bf16[4,272,256]{2,1,0:T(8,128)(2,1)} %get-tuple-element.65), channel_id=1, source_target_pairs={{0,24},{1,97},{2,26},{3,99},{4,28},{5,101},{6,30},{7,103},{8,0},{9... | collective-permute-start | bytes 1671176 | tf_op jit(solution)/shard_map/ppermute | solution.py:491
  115.6 13.8 %collective-permute-start.26 = (bf16[4,272,256]{2,1,0:T(8,128)(2,1)}, bf16[4,272,256]{2,1,0:T(8,128)(2,1)S(1)}, u32[]{:S(2)}, u32[]{:S(2)}) collective-permute-start(bf16[4,272,256]{2,1,0:T(8,128)(2,1)} %get-tuple-element.68), channel_id=1, source_target_pairs={{0,16},{1,65},{2,18},{3,67},{4,20},{5,69},{6,22},{7,71},{8,24},{9,... | collective-permute-start | bytes 1671176 | tf_op jit(solution)/shard_map/ppermute | solution.py:491
  116.7 3.4 %copy-start = (bf16[4096,1024]{1,0:T(8,128)(2,1)S(1)}, bf16[4096,1024]{1,0:T(8,128)(2,1)}, u32[]{:S(2)}) copy-start(bf16[4096,1024]{1,0:T(8,128)(2,1)} %all-gather.2.cloned.1.call-done.gathered) | copy-start | bytes 25165828
  120.1 14.2 %copy-start.1 = (bf16[4096,1024]{1,0:T(8,128)(2,1)S(1)}, bf16[4096,1024]{1,0:T(8,128)(2,1)}, u32[]{:S(2)}) copy-start(bf16[4096,1024]{1,0:T(8,128)(2,1)} %all-gather.2.cloned.1.call-done.gathered) | copy-start | bytes 25165828
  129.4 3.3 %collective-permute-start.29 = (bf16[4,272,256]{2,1,0:T(8,128)(2,1)S(1)}, bf16[4,272,256]{2,1,0:T(8,128)(2,1)S(1)}, u32[]{:S(2)}, u32[]{:S(2)}) collective-permute-start(bf16[4,272,256]{2,1,0:T(8,128)(2,1)S(1)} %collective-permute-done.26.refs_2_), channel_id=1, source_target_pairs={{0,1},{1,0},{2,3},{3,2},{4,5},{5,4},{6,7},{7,6},{8,9},{9,8},{10,11... | collective-permute-start | bytes 1671176 | tf_op jit(solution)/shard_map/ppermute | solution.py:40
  131.2 2.4 %collective-permute-start.28 = (bf16[4,272,256]{2,1,0:T(8,128)(2,1)S(1)}, bf16[4,272,256]{2,1,0:T(8,128)(2,1)S(1)}, u32[]{:S(2)}, u32[]{:S(2)}) collective-permute-start(bf16[4,272,256]{2,1,0:T(8,128)(2,1)S(1)} %collective-permute-done.25.refs_1_), channel_id=1, source_target_pairs={{0,1},{1,0},{2,3},{3,2},{4,5},{5,4},{6,7},{7,6},{8,9},{9,8},{10,11... | collective-permute-start | bytes 1671176 | tf_op jit(solution)/shard_map/ppermute | solution.py:40
  131.2 3.2 %collective-permute-start.27 = (bf16[4,272,256]{2,1,0:T(8,128)(2,1)S(1)}, bf16[4,272,256]{2,1,0:T(8,128)(2,1)S(1)}, u32[]{:S(2)}, u32[]{:S(2)}) collective-permute-start(bf16[4,272,256]{2,1,0:T(8,128)(2,1)S(1)} %collective-permute-done.23.refs_0_), channel_id=1, source_target_pairs={{0,1},{1,0},{2,3},{3,2},{4,5},{5,4},{6,7},{7,6},{8,9},{9,8},{10,11... | collective-permute-start | bytes 1671176 | tf_op jit(solution)/shard_map/ppermute | solution.py:40
Sparse Core Ops, SparseCore 0:
  10.1 74.0 all-gather.1

commit v3 on v2

--- a/solution.py
+++ b/solution.py
@@ -10,6 +10,7 @@
 BF = jnp.bfloat16
 F32 = jnp.float32
 LIMIT = 48 * 1024 * 1024
+SMALL = 16 * 1024 * 1024
 EXTRA = 16
 GROUPS = 4
 CORE_SWAP = [(t, t ^ 1) for t in range(8)]
@@ -44,10 +45,10 @@
     return pltpu.CompilerParams(vmem_limit_bytes=LIMIT)
 
 
-def partial_kernel(jobs, where, attention, w, *refs):
+def partial_kernel(jobs, where, att, w, *refs):
     ins = sum(1 for job in jobs if job[2])
-    got, outs = refs[:ins], refs[ins:-3]
-    att, buf, sems = refs[-3:]
+    got, outs = refs[:ins], refs[ins:-2]
+    buf, sems = refs[-2:]
     x, c = where[2], where[3]
     step = buf.shape[1]
     copies = []
@@ -57,11 +58,8 @@
             row = pl.multiple_of((piece * 2 + h) * step, step)
             n = len(copies)
             copies.append(pltpu.make_async_copy(w.at[pl.ds(row, step)], buf.at[n], sems.at[n]))
-    left = pltpu.make_async_copy(attention, att, sems.at[len(copies)])
-    left.start()
     for copy in copies:
         copy.start()
-    left.wait()
     used = 0
     for n, (_, _, add, _) in enumerate(jobs):
         if add:
@@ -90,13 +88,12 @@
     far = pl.BlockSpec(memory_space=pltpu.HBM)
     return pl.pallas_call(
         functools.partial(partial_kernel, jobs),
-        in_specs=[pl.BlockSpec(memory_space=pltpu.SMEM), far, far] + [vmem] * len(got),
+        in_specs=[pl.BlockSpec(memory_space=pltpu.SMEM), vmem, far] + [vmem] * len(got),
         out_specs=[vmem] * len(jobs),
         out_shape=[jax.ShapeDtypeStruct((rows, width), job[3]) for job in jobs],
         scratch_shapes=[
-            pltpu.VMEM((rows, depth), BF),
             pltpu.VMEM((count, step, depth), BF),
-            pltpu.SemaphoreType.DMA((count + 1,)),
+            pltpu.SemaphoreType.DMA((count,)),
         ],
         compiler_params=params(),
         cost_estimate=pl.CostEstimate(
@@ -116,35 +113,37 @@
     return jnp.sum(part.T, axis=0, keepdims=True)
 
 
-def hidden_kernel(own, sent, r1, r2, r3, residual, cot, gain, stats, hidden, sums):
-    h = own[...] + sent[...].astype(F32) + residual[...].astype(F32)
-    h = h + r1[...].astype(F32) + r2[...].astype(F32) + r3[...].astype(F32)
-    hidden[...] = h
-    scaled = cot[...].astype(F32) * gain[...].astype(F32)
-    first = row_sums(h * h)
-    second = row_sums(scaled * h)
-    sums[...] = jnp.concatenate([first, second, stats[...], jnp.zeros((5, 128), F32)], axis=0)
-
-
-def hidden_call(own, sent, r1, r2, r3, residual, cot, gain, stats):
+def hidden_kernel(own, r1, r2, r3, residual, cot, gain, stats, hidden, sums):
+    @pl.loop(0, own.shape[0] // 128)
+    def _(i):
+        band = pl.ds(pl.multiple_of(i * 128, 128), 128)
+        h = own[band, :] + residual[band, :].astype(F32)
+        h = h + r1[band, :].astype(F32) + r2[band, :].astype(F32) + r3[band, :].astype(F32)
+        hidden[band, :] = h
+        scaled = cot[band, :].astype(F32) * gain[...].astype(F32)
+        first = row_sums(h * h)
+        second = row_sums(scaled * h)
+        rest = [stats[...], jnp.zeros((5, 128), F32)]
+        sums[:, band] = jnp.concatenate([first, second] + rest, axis=0)
+
+
+def hidden_call(own, r1, r2, r3, residual, cot, gain, stats):
     rows, width = own.shape
-    big = pl.BlockSpec((128, width), lambda i: (i, 0))
+    vmem = pl.BlockSpec(memory_space=pltpu.VMEM)
     return pl.pallas_call(
         hidden_kernel,
-        grid=(rows // 128,),
-        in_specs=[big] * 7
-        + [pl.BlockSpec((1, width), lambda i: (0, 0)), pl.BlockSpec((1, 128), lambda i: (0, 0))],
-        out_specs=[big, pl.BlockSpec((8, 128), lambda i: (0, i))],
+        in_specs=[vmem] * 8,
+        out_specs=[vmem] * 2,
         out_shape=[
             jax.ShapeDtypeStruct((rows, width), F32),
             jax.ShapeDtypeStruct((8, rows), F32),
         ],
-        compiler_params=params(),
+        compiler_params=pltpu.CompilerParams(vmem_limit_bytes=SMALL),
         cost_estimate=pl.CostEstimate(
             flops=12 * rows * width, bytes_accessed=20 * rows * width, transcendentals=0
         ),
         name="hidden",
-    )(own, sent, r1, r2, r3, residual, cot, gain, stats)
+    )(own, r1, r2, r3, residual, cot, gain, stats)
 
 
 def column(row):
@@ -169,67 +168,56 @@
     return jnp.sum(block.astype(F32), axis=0, keepdims=True)
 
 
-def grad_kernel(
-    features, tokens, hidden, cot, gain, s0, s1, s2, s3, info, grad, total
-):
-    i = pl.program_id(0)
+def grad_kernel(features, tokens, hidden, cot, gain, s0, s1, s2, s3, info, grad, piece, total):
     width = hidden.shape[1]
-    sums = s0[...] + s1[...] + s2[...] + s3[...]
-    square, inner = sums[0:1, :], sums[1:2, :]
-    inverse = lax.rsqrt(square / features + 1e-06)
-    reward, kept, group = info[0:1, :], info[1:2, :], info[2:3, :]
-
-    def picked(offset):
-        value = jnp.zeros_like(reward)
-        for g in range(GROUPS):
-            stat = jnp.broadcast_to(sums[2:3, offset + g : offset + g + 1], value.shape)
-            value = jnp.where(group == float(g), stat, value)
-        return value
-
-    count = jnp.maximum(picked(0), 1.0)
-    mean = picked(GROUPS) / count
-    variance = picked(2 * GROUPS) / count - mean * mean
-    advantage = (reward - mean) / jnp.sqrt(jnp.maximum(variance, 1.0))
-    kept_tokens = jnp.broadcast_to(sums[2:3, 3 * GROUPS : 3 * GROUPS + 1], reward.shape)
-    coef = -advantage * kept * tokens / jnp.maximum(kept_tokens, 1.0)
-    first = coef * inverse
-    second = coef * (inverse * inverse * inverse * inner / features)
-    first = spread(column(first), width)
-    second = spread(column(second), width)
-    h = hidden[...]
-    c = cot[...].astype(F32)
-    grad[...] = (first * (c * gain[...].astype(F32)) - h * second).astype(BF)
-    term = jnp.sum(first * c * h, axis=0, keepdims=True)
-    @pl.when(i == 0)
-    def _():
-        total[...] = term
-
-    @pl.when(i != 0)
-    def _():
-        total[...] += term
+    total[...] = jnp.zeros_like(total)
+
+    @pl.loop(0, hidden.shape[0] // 128)
+    def _(i):
+        band = pl.ds(pl.multiple_of(i * 128, 128), 128)
+        sums = s0[:, band] + s1[:, band] + s2[:, band] + s3[:, band]
+        square, inner = sums[0:1, :], sums[1:2, :]
+        inverse = lax.rsqrt(square / features + 1e-06)
+        reward, kept, group = info[0:1, band], info[1:2, band], info[2:3, band]
+
+        def picked(offset):
+            value = jnp.zeros_like(reward)
+            for g in range(GROUPS):
+                stat = jnp.broadcast_to(sums[2:3, offset + g : offset + g + 1], value.shape)
+                value = jnp.where(group == float(g), stat, value)
+            return value
+
+        count = jnp.maximum(picked(0), 1.0)
+        mean = picked(GROUPS) / count
+        variance = picked(2 * GROUPS) / count - mean * mean
+        advantage = (reward - mean) / jnp.sqrt(jnp.maximum(variance, 1.0))
+        kept_tokens = jnp.broadcast_to(sums[2:3, 3 * GROUPS : 3 * GROUPS + 1], reward.shape)
+        coef = -advantage * kept * tokens / jnp.maximum(kept_tokens, 1.0)
+        first = spread(column(coef * inverse), width)
+        second = spread(column(coef * (inverse * inverse * inverse * inner / features)), width)
+        h = hidden[band, :]
+        c = cot[band, :].astype(F32)
+        value = (first * (c * gain[...].astype(F32)) - h * second).astype(BF)
+        grad[band, :] = value
+        piece[band, :] = value
+        total[...] += jnp.sum(first * c * h, axis=0, keepdims=True)
 
 
 def grad_call(features, tokens, hidden, cot, gain, s0, s1, s2, s3, info):
     rows, width = hidden.shape
-    big = pl.BlockSpec((128, width), lambda i: (i, 0))
-    small = pl.BlockSpec((8, 128), lambda i: (0, i))
+    vmem = pl.BlockSpec(memory_space=pltpu.VMEM)
     return pl.pallas_call(
         functools.partial(grad_kernel, float(features), float(tokens)),
-        grid=(rows // 128,),
-        in_specs=[
-            big,
-            big,
-            pl.BlockSpec((1, width), lambda i: (0, 0)),
-        ]
-        + [small] * 5,
-        out_specs=[big, pl.BlockSpec((1, width), lambda i: (0, 0))],
+        in_specs=[vmem] * 8,
+        out_specs=[vmem] * 3,
         out_shape=[
+            jax.ShapeDtypeStruct((rows, width), BF),
             jax.ShapeDtypeStruct((rows, width), BF),
             jax.ShapeDtypeStruct((1, width), F32),
         ],
-        compiler_params=params(),
+        compiler_params=pltpu.CompilerParams(vmem_limit_bytes=SMALL),
         cost_estimate=pl.CostEstimate(
-            flops=12 * rows * width, bytes_accessed=10 * rows * width, transcendentals=0
+            flops=12 * rows * width, bytes_accessed=8 * rows * width, transcendentals=0
         ),
         name="grad",
     )(hidden, cot, gain, s0, s1, s2, s3, info)
@@ -305,9 +293,9 @@
 
                     @pl.when(slot == s)
                     def _(s=s, j=j, start=start, piece=pieces[k * 2 + other]):
-                        @pl.loop(0, rows // 64)
+                        @pl.loop(0, rows // 128)
                         def _(r):
-                            band = pl.ds(pl.multiple_of(r * 64, 64), 64)
+                            band = pl.ds(pl.multiple_of(r * 128, 128), 128)
                             outs[s][j, band, :] = piece[band, pl.ds(start, half)]
 
 
@@ -323,11 +311,7 @@
     for u in range(4):
         j = lax.rem(mine + u, 4)
         for s in range(4):
-
-            @pl.loop(0, rows // 64)
-            def _(r, u=u, s=s, j=j):
-                band = pl.ds(pl.multiple_of(r * 64, 64), 64)
-                outs[u][s, band, :] = parts[s][j, band, :]
+            outs[u][s, 0:rows, :] = parts[s][j, 0:rows, :]
 
 
 def pack_call(kernel, where, inputs, rows, half, name):
@@ -346,24 +330,29 @@
 
 
 def projection_kernel(members, first, last, where, gathered, *refs):
-    count = len(members)
-    mine, theirs = refs[:count], refs[count : 2 * count]
-    refs = refs[2 * count :]
+    count = sum(len(group) for group in members)
+    parts = refs[:count]
+    refs = refs[count:]
     before = None if first else refs[0]
-    out = refs[0 if first else 1]
+    out = refs[2 if last else 0 if first else 1]
+    if last:
+        refs[3][...] = jnp.sum(refs[1][...], axis=0, keepdims=True)
     z, y, c = where[0], where[1], where[3]
     half = out.shape[-2] // (2 if last else 1)
-    rows = mine[0].shape[1] - EXTRA
-    for n, parts in ((0, mine), (1, theirs)):
+    rows = parts[0].shape[1] - EXTRA
+    used = 0
+    for n in range(2):
         z_first = (c == 0) if n == 0 else (c == 1)
         total = None if first else before[n]
-        for m, u in enumerate(members):
+        for u in members[n]:
+            part = parts[used]
+            used += 1
             for s in range(4):
                 dz, dy = jnp.where(z_first, s, u), jnp.where(z_first, u, s)
                 row = lax.rem(z + 4 - dz, 4) * 4 + lax.rem(y + 4 - dy, 4)
                 row = pl.multiple_of(row * rows, rows)
                 term = lax.dot_general(
-                    parts[m][s, 0:rows, :],
+                    part[s, 0:rows, :],
                     gathered[pl.ds(row, rows), :],
                     (((0,), (0,)), ((), ())),
                     preferred_element_type=F32,
@@ -377,20 +366,24 @@
             out[n] = total
 
 
-def projection_call(where, mine, theirs, gathered, members, before, last):
+def projection_call(where, mine, theirs, gathered, members, before, tails=None):
     rows, half = mine[0].shape[1] - EXTRA, mine[0].shape[2]
     depth = gathered.shape[1]
     vmem = pl.BlockSpec(memory_space=pltpu.VMEM)
-    blocks = 8 * len(members)
-    picked = [mine[u] for u in members] + [theirs[u] for u in members]
-    first = before is None
+    picked = [mine[u] for u in members[0]] + [theirs[u] for u in members[1]]
+    blocks = 4 * len(picked)
+    first, last = before is None, tails is not None
     return pl.pallas_call(
         functools.partial(projection_kernel, members, first, last),
         in_specs=[pl.BlockSpec(memory_space=pltpu.SMEM), vmem]
         + [vmem] * len(picked)
-        + ([] if first else [vmem]),
-        out_specs=vmem,
-        out_shape=jax.ShapeDtypeStruct((2 * half, depth), BF)
+        + ([] if first else [vmem])
+        + ([vmem] if last else []),
+        out_specs=[vmem, vmem] if last else vmem,
+        out_shape=[
+            jax.ShapeDtypeStruct((2 * half, depth), BF),
+            jax.ShapeDtypeStruct((1, 4 * half), F32),
+        ]
         if last
         else jax.ShapeDtypeStruct((2, half, depth), F32),
         compiler_params=pltpu.CompilerParams(vmem_limit_bytes=24 * 1024 * 1024),
@@ -400,7 +393,7 @@
             transcendentals=0,
         ),
         name="projection_grad",
-    )(where, gathered, *picked, *([] if first else [before]))
+    )(where, gathered, *picked, *([] if first else [before]), *([tails] if last else []))
 
 
 def local_stats(rewards, group_ids, kept_flags, lengths):
@@ -447,35 +440,38 @@
     both = (keep2 + swap(send2).astype(F32)).astype(BF)
     arrived[2] = lax.ppermute(both, "tensor", x_shift(2))
     late_where, _ = lax.optimization_barrier((where, both))
-    first, third, send0, keep0 = partial_products(
+    first, third, send0 = partial_products(
         late_where,
         attention,
         out_proj,
-        [(1, False, True, BF), (3, False, True, BF), (0, True, False, BF), (0, False, False, F32)],
+        [(1, False, True, BF), (3, False, True, BF), (0, True, False, BF)],
         [swap(send1), swap(send3)],
     )
     arrived[1] = lax.ppermute(first, "tensor", x_shift(1))
     arrived[3] = lax.ppermute(third, "tensor", x_shift(3))
-    sent0 = swap(send0)
     stats = local_stats(rewards, group_ids, kept_flags, lengths)
     info = token_info(rewards, group_ids, kept_flags, lengths, rows)
-    stats, info, arrived[2], _ = lax.optimization_barrier((stats, info, arrived[2], sent0))
+    stats, info, _ = lax.optimization_barrier((stats, info, third))
+    late_where, arrived[2] = lax.optimization_barrier((where, arrived[2]))
     stats = sum(lax.ppermute(stats, ("dp", "tensor"), scattered(step)) for step in (0, 1))
+    (own,) = partial_products(
+        late_where, attention, out_proj, [(0, False, True, F32)], [swap(send0)]
+    )
     residual, info = lax.optimization_barrier((residual, info))
     hidden, sums = hidden_call(
-        keep0, sent0, arrived[1], arrived[2], arrived[3], residual, cotangent, gain, stats
+        own, arrived[1], arrived[2], arrived[3], residual, cotangent, gain, stats
     )
 
     chip = sums + swap(sums)
     others = [lax.ppermute(chip, "tensor", x_shift(k)) for k in (1, 2, 3)]
     tokens = rows * lax.axis_size("dp")
-    grad_residual, gain_term = grad_call(
+    grad_residual, own_piece, gain_term = grad_call(
         features, tokens, hidden, cotangent, gain, chip, *others, info
     )
 
     pieces = []
     for k in range(4):
-        piece = grad_residual if k == 0 else lax.ppermute(grad_residual, "tensor", x_shift(k))
+        piece = own_piece if k == 0 else lax.ppermute(own_piece, "tensor", x_shift(k))
         pieces.extend([piece, swap(piece)])
 
     half = features // 32
@@ -491,14 +487,17 @@
         lax.ppermute(sends[k], ("dp", "tensor"), plane_shift(1, k)) for k in (1, 2, 3)
     ]
     theirs = [swap(mine[0]), None, None, None]
-    total = projection_call(where, mine, theirs, gathered, (0,), None, False)
+    total = projection_call(where, mine, theirs, gathered, ((0,), (0,)), None)
     for k in (1, 3, 2):
         mine[k], total = lax.optimization_barrier((mine[k], total))
         theirs[k] = swap(mine[k])
-    total = projection_call(where, mine, theirs, gathered, (1, 3, 2), total, True)
-    tails = [part[:, rows:, :].astype(F32) for part in mine]
-    grad_gain = jnp.sum(sum(tails), axis=1).reshape(-1)
-    return (grad_attention, total, grad_residual, grad_gain)
+    total = projection_call(where, mine, theirs, gathered, ((1, 3, 2), ()), total)
+    tails = sum(part[:, rows:, :].astype(F32) for part in mine)
+    tails = jnp.concatenate([tails[j] for j in range(4)], axis=1)
+    grad_out_proj, grad_gain = projection_call(
+        where, mine, theirs, gathered, ((), (1, 3, 2)), total, tails
+    )
+    return (grad_attention, grad_out_proj, grad_residual, grad_gain[0])
 
 
 def solution(mesh):

time: 147 us -> 141 us (0.959)
  starting transfers between devices: 44.5 us -> 38.5 us
  local copies, waits for them, and re-layouts: 9.81 us -> 5.28 us
  waiting for transfers between devices: 39.7 us -> 44.2 us
    ppermute x2, waiting for transfers between devices: 4.22 us -> 8.88 us  [shards(): lax.ppermute(stats, ('dp', 'tensor'), scattered(step))]
    unnamed x31 -> x22, local copies, waits for them, and re-layouts: 9 us -> 4.46 us
    ppermute x13, starting transfers between devices: 17.6 us -> 14.8 us  [swap(): return lax.ppermute(value, 'tensor', CORE_SWAP)]
    ppermute x3, waiting for transfers between devices: 3.08 us -> 5.11 us  [shards(): lax.ppermute(sends[k], ('dp', 'tensor'), plane_shift(0, k))]
    ppermute x3, starting transfers between devices: 5.05 us -> 3.45 us  [shards(): lax.ppermute(sends[k], ('dp', 'tensor'), plane_shift(0, k))]
    ppermute x2, starting transfers between devices: 6.4 us -> 4.81 us  [shards(): lax.ppermute(stats, ('dp', 'tensor'), scattered(step))]
    ppermute x3, starting transfers between devices: 2.24 us -> 3.72 us  [shards(): lax.ppermute(own_piece, 'tensor', x_shift(k))]
    pallas_call x2 -> x3, Pallas kernels: 14 us -> 15.4 us  [partial_products(): pl.pallas_call(functools.partial(partial_kernel, jobs), in_specs=[pl.Bloc...]
  transfers between devices with their start and end apart: 31 -> 31, of which waited for: 15 -> 16; matrix products, arithmetic and copies ran while one was open for 3% -> 2% of each run, Pallas kernels for 21% -> 23%
where the time goes in v3:
time: 141 us
  waiting for transfers between devices  44.2 us (31%)
  starting transfers between devices  38.5 us (27%)
  Pallas kernels  36.1 us (26%)
  between operations  14.3 us (10%)
  local copies, waits for them, and re-layouts  5.28 us (4%)
  other arithmetic  2.23 us (2%)
    pallas_call x3, Pallas kernels, partial_products(): pl.pallas_call(functools.partial(partial_kernel, jobs), in_specs=[pl.Bloc...  15.4 us
    ppermute x3, waiting for transfers between devices, shards(): lax.ppermute(own_piece, 'tensor', x_shift(k))  15.2 us
    ppermute x13, starting transfers between devices, swap(): return lax.ppermute(value, 'tensor', CORE_SWAP)  14.8 us
    ppermute x2, waiting for transfers between devices, shards(): lax.ppermute(stats, ('dp', 'tensor'), scattered(step))  8.88 us
    ppermute x3, waiting for transfers between devices, shards(): lax.ppermute(sends[k], ('dp', 'tensor'), plane_shift(1, k))  8.18 us
    pallas_call x1, Pallas kernels, attention_call(): pl.pallas_call(attention_kernel, in_specs=[pl.BlockSpec(memory_space=pltp...  7.98 us
    pallas_call x3, Pallas kernels, projection_call(): pl.pallas_call(functools.partial(projection_kernel, members, first, last)...  7.51 us
    ppermute x3, waiting for transfers between devices, shards(): lax.ppermute(sends[k], ('dp', 'tensor'), plane_shift(0, k))  5.11 us
  transfers between devices with their start and end apart: 31, of which 16 were waited for; matrix products, arithmetic and copies ran while one was open for 2% of the time, Pallas kernels for 23%

profile of v3, /device:TPU:1, one launch (start us, length us, event | category | flops | bytes accessed | tf_op | source)
XLA Modules:
  0.0 140.6 jit_solution(14775324415922828605)
XLA Ops:
  7.2 0.7 all-gather.2.cloned.1.call-update
  8.0 1.0 copy-done.2
  9.1 6.0 %partial.3 = (bf16[256,1024]{1,0:T(8,128)(2,1)S(1)}, f32[256,1024]{1,0:T(8,128)S(1)}, bf16[256,1024]{1,0:T(8,128)(2,1)S(1)}, bf16[256,1024]{1,0:T(8,128)(2,1)S(1)}) custom-call(s32[4]{0:T(128)S(1)} %pad_add_fusion.where, bf16[256,1024]{1,0:T(8,128)(2,1)S(1)} %copy-done.2, bf16[8192,1024]{1,0:T(8,128)(2,1)} %refs_8_.1), custom_call_target="tpu_custom_call" | custom-call | flops 2147483648 | bytes 8388608 | tf_op jit(solution)/shard_map/partial/pallas_call | solution.py:89
  15.1 1.5 %collective-permute-start = (bf16[256,1024]{1,0:T(8,128)(2,1)S(1)}, bf16[256,1024]{1,0:T(8,128)(2,1)S(1)}, u32[]{:S(2)}, u32[]{:S(2)}) collective-permute-start(bf16[256,1024]{1,0:T(8,128)(2,1)S(1)} %get-tuple-element.42), channel_id=1, source_target_pairs={{0,1},{1,0},{2,3},{3,2},{4,5},{5,4},{6,7},{7,6},{8,9},{9,8},{10,11... | collective-permute-start | bytes 1572872 | tf_op jit(solution)/shard_map/ppermute | solution.py:41
  17.1 0.6 convert_multiply_fusion
  18.1 0.9 add_convert_fusion
  19.1 2.8 %collective-permute-start.1 = (bf16[256,1024]{1,0:T(8,128)(2,1)}, bf16[256,1024]{1,0:T(8,128)(2,1)S(1)}, u32[]{:S(2)}, u32[]{:S(2)}) collective-permute-start(bf16[256,1024]{1,0:T(8,128)(2,1)} %add_convert_fusion), channel_id=1, source_target_pairs={{0,4},{1,5},{2,6},{3,7},{4,0},{5,1},{6,2},{7,3},{8,12},{9,13},{10,... | collective-permute-start | bytes 1572872 | tf_op jit(solution)/shard_map/ppermute | solution.py:441
  21.9 6.0 %partial.4 = (bf16[256,1024]{1,0:T(8,128)(2,1)}, bf16[256,1024]{1,0:T(8,128)(2,1)S(1)}, bf16[256,1024]{1,0:T(8,128)(2,1)}) custom-call(s32[4]{0:T(128)S(1)} %pad_add_fusion.where, bf16[256,1024]{1,0:T(8,128)(2,1)S(1)} %copy-done.2, bf16[8192,1024]{1,0:T(8,128)(2,1)} %refs_8_.1, bf16[256,1024]{1,0:T(8,128)(2,1)S(1)} %collective-permute-done.2.refs_0_, ...), custom_call_target="tpu_custom_call" | custom-call | flops 1610612736 | bytes 6291456 | tf_op jit(solution)/shard_map/partial/pallas_call | solution.py:89
  27.9 0.7 collective-permute-start.4
  28.9 2.4 %collective-permute-start.6 = (bf16[256,1024]{1,0:T(8,128)(2,1)S(1)}, bf16[256,1024]{1,0:T(8,128)(2,1)S(1)}, u32[]{:S(2)}, u32[]{:S(2)}) collective-permute-start(bf16[256,1024]{1,0:T(8,128)(2,1)S(1)} %get-tuple-element.50), channel_id=1, source_target_pairs={{0,6},{1,7},{2,0},{3,1},{4,2},{5,3},{6,4},{7,5},{8,14},{9,15},{10,... | collective-permute-start | bytes 1572872 | tf_op jit(solution)/shard_map/ppermute | solution.py:451
  31.7 0.7 concatenate.9
  32.7 4.8 %collective-permute-start.7 = (f32[1,128]{1,0:T(1,128)S(1)}, f32[1,128]{1,0:T(1,128)S(1)}, u32[]{:S(2)}, u32[]{:S(2)}) collective-permute-start(f32[1,128]{1,0:T(1,128)S(1)} %bitcast.28), channel_id=1, source_target_pairs={{0,0},{1,17},{2,34},{3,51},{4,68},{5,85},{6,102},{7,119},{8,8},{9,... | collective-permute-start | bytes 1544 | tf_op jit(solution)/shard_map/ppermute | solution.py:456
  37.5 4.4 %collective-permute-done.7 = f32[1,128]{1,0:T(1,128)S(1)} collective-permute-done((f32[1,128]{1,0:T(1,128)S(1)}, f32[1,128]{1,0:T(1,128)S(1)}, u32[]{:S(2)}, u32[]{:S(2)}) %collective-permute-start.7) | collective-permute-done | bytes 544 | tf_op jit(solution)/shard_map/ppermute | solution.py:456
  41.9 4.5 %collective-permute-done.8 = f32[1,128]{1,0:T(1,128)S(1)} collective-permute-done((f32[1,128]{1,0:T(1,128)S(1)}, f32[1,128]{1,0:T(1,128)S(1)}, u32[]{:S(2)}, u32[]{:S(2)}) %collective-permute-start.8) | collective-permute-done | bytes 544 | tf_op jit(solution)/shard_map/ppermute | solution.py:456
  46.5 3.4 %partial.5.own = f32[256,1024]{1,0:T(8,128)S(1)} custom-call(s32[4]{0:T(128)S(1)} %pad_add_fusion.where, bf16[256,1024]{1,0:T(8,128)(2,1)S(1)} %copy-done.3, bf16[8192,1024]{1,0:T(8,128)(2,1)} %refs_8_.1, bf16[256,1024]{1,0:T(8,128)(2,1)S(1)} %collective-permute-done.4.refs_0_), custom_call_target="tpu_custom_call" | custom-call | flops 536870912 | bytes 2097152 | tf_op jit(solution)/shard_map/partial/pallas_call | solution.py:89
  49.9 0.6 hidden.1
  50.7 1.2 collective-permute-done.9
  52.0 1.8 %collective-permute-start.11 = (f32[8,256]{1,0:T(8,128)S(1)}, f32[8,256]{1,0:T(8,128)S(1)}, u32[]{:S(2)}, u32[]{:S(2)}) collective-permute-start(f32[8,256]{1,0:T(8,128)S(1)} %add.31.s0), channel_id=1, source_target_pairs={{0,4},{1,5},{2,6},{3,7},{4,0},{5,1},{6,2},{7,3},{8,12},{9,13},{10,... | collective-permute-start | bytes 24584 | tf_op jit(solution)/shard_map/ppermute | solution.py:466
  53.8 0.8 collective-permute-start.12
  54.5 1.4 %collective-permute-done.10.s1 = f32[8,256]{1,0:T(8,128)S(1)} collective-permute-done((f32[8,256]{1,0:T(8,128)S(1)}, f32[8,256]{1,0:T(8,128)S(1)}, u32[]{:S(2)}, u32[]{:S(2)}) %collective-permute-start.10) | collective-permute-done | bytes 8224 | tf_op jit(solution)/shard_map/ppermute | solution.py:466
  56.0 0.7 collective-permute-done.12.s3
  56.7 1.5 %grad.1 = (bf16[256,1024]{1,0:T(8,128)(2,1)}, bf16[256,1024]{1,0:T(8,128)(2,1)S(1)}, f32[1,1024]{1,0:T(1,128)S(1)}) custom-call(f32[256,1024]{1,0:T(8,128)S(1)} %get-tuple-element.54.hidden, bf16[256,1024]{1,0:T(8,128)(2,1)S(1)} %copy-done.4, bf16[1,1024]{1,0:T(2,128)(2,1)S(1)} %broadcast_in_dim.43.gain, f32[8,256]{1,0:T(8,128)S(1)} %add.31.s0, ...), custom_call_target="tpu_custom_call" | custom-call | flops 3145728 | bytes 2097152 | tf_op jit(solution)/shard_map/grad/pallas_call | solution.py:209
  58.1 1.3 collective-permute-start.14
  59.4 1.8 %collective-permute-start.16 = (bf16[256,1024]{1,0:T(8,128)(2,1)S(1)}, bf16[256,1024]{1,0:T(8,128)(2,1)S(1)}, u32[]{:S(2)}, u32[]{:S(2)}) collective-permute-start(bf16[256,1024]{1,0:T(8,128)(2,1)S(1)} %get-tuple-element.57.refs_0_), channel_id=1, source_target_pairs={{0,4},{1,5},{2,6},{3,7},{4,0},{5,1},{6,2},{7,3},{8,12},{9,13},{10,... | collective-permute-start | bytes 1572872 | tf_op jit(solution)/shard_map/ppermute | solution.py:474
  61.8 2.0 %collective-permute-start.13 = (bf16[256,1024]{1,0:T(8,128)(2,1)S(1)}, bf16[256,1024]{1,0:T(8,128)(2,1)S(1)}, u32[]{:S(2)}, u32[]{:S(2)}) collective-permute-start(bf16[256,1024]{1,0:T(8,128)(2,1)S(1)} %get-tuple-element.57.refs_0_), channel_id=1, source_target_pairs={{0,1},{1,0},{2,3},{3,2},{4,5},{5,4},{6,7},{7,6},{8,9},{9,8},{10,11... | collective-permute-start | bytes 1572872 | tf_op jit(solution)/shard_map/ppermute | solution.py:41
  63.9 7.5 %collective-permute-done.14.refs_2_ = bf16[256,1024]{1,0:T(8,128)(2,1)S(1)} collective-permute-done((bf16[256,1024]{1,0:T(8,128)(2,1)S(1)}, bf16[256,1024]{1,0:T(8,128)(2,1)S(1)}, u32[]{:S(2)}, u32[]{:S(2)}) %collective-permute-start.14) | collective-permute-done | bytes 524320 | tf_op jit(solution)/shard_map/ppermute | solution.py:474
  71.4 3.8 %collective-permute-start.15 = (bf16[256,1024]{1,0:T(8,128)(2,1)S(1)}, bf16[256,1024]{1,0:T(8,128)(2,1)S(1)}, u32[]{:S(2)}, u32[]{:S(2)}) collective-permute-start(bf16[256,1024]{1,0:T(8,128)(2,1)S(1)} %collective-permute-done.14.refs_2_), channel_id=1, source_target_pairs={{0,1},{1,0},{2,3},{3,2},{4,5},{5,4},{6,7},{7,6},{8,9},{9,8},{10,11... | collective-permute-start | bytes 1572872 | tf_op jit(solution)/shard_map/ppermute | solution.py:41
  75.2 7.7 %collective-permute-done.16.refs_4_ = bf16[256,1024]{1,0:T(8,128)(2,1)S(1)} collective-permute-done((bf16[256,1024]{1,0:T(8,128)(2,1)S(1)}, bf16[256,1024]{1,0:T(8,128)(2,1)S(1)}, u32[]{:S(2)}, u32[]{:S(2)}) %collective-permute-start.16) | collective-permute-done | bytes 524320 | tf_op jit(solution)/shard_map/ppermute | solution.py:474
  83.0 2.4 %collective-permute-start.17 = (bf16[256,1024]{1,0:T(8,128)(2,1)S(1)}, bf16[256,1024]{1,0:T(8,128)(2,1)S(1)}, u32[]{:S(2)}, u32[]{:S(2)}) collective-permute-start(bf16[256,1024]{1,0:T(8,128)(2,1)S(1)} %collective-permute-done.16.refs_4_), channel_id=1, source_target_pairs={{0,1},{1,0},{2,3},{3,2},{4,5},{5,4},{6,7},{7,6},{8,9},{9,8},{10,11... | collective-permute-start | bytes 1572872 | tf_op jit(solution)/shard_map/ppermute | solution.py:41
  85.5 1.4 collective-permute-done.17.refs_5_
  86.9 0.7 collective-permute-done.19.refs_7_
  87.7 1.3 first_pack.1
  89.4 2.5 %collective-permute-start.21 = (bf16[4,272,256]{2,1,0:T(8,128)(2,1)S(1)}, bf16[4,272,256]{2,1,0:T(8,128)(2,1)S(1)}, u32[]{:S(2)}, u32[]{:S(2)}) collective-permute-start(bf16[4,272,256]{2,1,0:T(8,128)(2,1)S(1)} %get-tuple-element.61), channel_id=1, source_target_pairs={{0,64},{1,17},{2,66},{3,19},{4,68},{5,21},{6,70},{7,23},{8,72},{9,... | collective-permute-start | bytes 1671176 | tf_op jit(solution)/shard_map/ppermute | solution.py:480
  91.8 0.6 collective-permute-start.22
  92.4 8.0 %attention_grad.1 = bf16[256,1024]{1,0:T(8,128)(2,1)} custom-call(s32[4]{0:T(128)S(1)} %pad_add_fusion.where, bf16[256,1024]{1,0:T(8,128)(2,1)S(1)} %get-tuple-element.57.refs_0_, bf16[256,1024]{1,0:T(8,128)(2,1)S(1)} %collective-permute-done.13.refs_1_, bf16[256,1024]{1,0:T(8,128)(2,1)S(1)} %collective-permute-done.14.refs_2_, ...), custom_call_target="tpu_custom_call" | custom-call | flops 4294967296 | bytes 16777216 | tf_op jit(solution)/shard_map/attention_grad/pallas_call | solution.py:252
  100.4 4.6 %collective-permute-done.21.refs_2_ = bf16[4,272,256]{2,1,0:T(8,128)(2,1)S(1)} collective-permute-done((bf16[4,272,256]{2,1,0:T(8,128)(2,1)S(1)}, bf16[4,272,256]{2,1,0:T(8,128)(2,1)S(1)}, u32[]{:S(2)}, u32[]{:S(2)}) %collective-permute-start.21) | collective-permute-done | bytes 557088 | tf_op jit(solution)/shard_map/ppermute | solution.py:480
  105.5 1.8 %second_pack.1 = (bf16[4,272,256]{2,1,0:T(8,128)(2,1)S(1)}, bf16[4,272,256]{2,1,0:T(8,128)(2,1)}, bf16[4,272,256]{2,1,0:T(8,128)(2,1)S(1)}, bf16[4,272,256]{2,1,0:T(8,128)(2,1)}) custom-call(s32[4]{0:T(128)S(1)} %pad_add_fusion.where, bf16[4,272,256]{2,1,0:T(8,128)(2,1)S(1)} %get-tuple-element.59.refs_0_, ...), custom_call_target="tpu_custom_call" | custom-call | bytes 4194304 | tf_op jit(solution)/shard_map/second_pack/pallas_call | solution.py:319
  107.3 1.5 %collective-permute-start.24 = (bf16[4,272,256]{2,1,0:T(8,128)(2,1)S(1)}, bf16[4,272,256]{2,1,0:T(8,128)(2,1)S(1)}, u32[]{:S(2)}, u32[]{:S(2)}) collective-permute-start(bf16[4,272,256]{2,1,0:T(8,128)(2,1)S(1)} %get-tuple-element.66.refs_0_), channel_id=1, source_target_pairs={{0,1},{1,0},{2,3},{3,2},{4,5},{5,4},{6,7},{7,6},{8,9},{9,8},{10,11... | collective-permute-start | bytes 1671176 | tf_op jit(solution)/shard_map/ppermute | solution.py:41
  108.8 1.3 collective-permute-start.23
  110.1 1.4 %collective-permute-start.26 = (bf16[4,272,256]{2,1,0:T(8,128)(2,1)}, bf16[4,272,256]{2,1,0:T(8,128)(2,1)S(1)}, u32[]{:S(2)}, u32[]{:S(2)}) collective-permute-start(bf16[4,272,256]{2,1,0:T(8,128)(2,1)} %get-tuple-element.68), channel_id=1, source_target_pairs={{0,24},{1,97},{2,26},{3,99},{4,28},{5,101},{6,30},{7,103},{8,0},{9... | collective-permute-start | bytes 1671176 | tf_op jit(solution)/shard_map/ppermute | solution.py:487
  111.5 0.9 collective-permute-start.28
  112.4 3.4 %copy-done = bf16[4096,1024]{1,0:T(8,128)(2,1)S(1)} copy-done((bf16[4096,1024]{1,0:T(8,128)(2,1)S(1)}, bf16[4096,1024]{1,0:T(8,128)(2,1)}, u32[]{:S(2)}) %copy-start) | copy-done | bytes 8388632
  115.7 1.8 %projection_grad.3.refs_3_ = f32[2,256,1024]{2,1,0:T(8,128)S(1)} custom-call(s32[4]{0:T(128)S(1)} %pad_add_fusion.where, bf16[4096,1024]{1,0:T(8,128)(2,1)S(1)} %copy-done, bf16[4,272,256]{2,1,0:T(8,128)(2,1)S(1)} %get-tuple-element.66.refs_0_, bf16[4,272,256]{2,1,0:T(8,128)(2,1)S(1)} %collective-permute-done.24.refs_1_), custom_call_target="tpu_custom_call" | custom-call | flops 1073741824 | bytes 5242880 | tf_op jit(solution)/shard_map/projection_grad/pallas_call | solution.py:376
  117.6 1.4 collective-permute-done.23.refs_0_
  119.0 6.8 %collective-permute-done.28.refs_2_ = bf16[4,272,256]{2,1,0:T(8,128)(2,1)S(1)} collective-permute-done((bf16[4,272,256]{2,1,0:T(8,128)(2,1)S(1)}, bf16[4,272,256]{2,1,0:T(8,128)(2,1)S(1)}, u32[]{:S(2)}, u32[]{:S(2)}) %collective-permute-start.28) | collective-permute-done | bytes 557088 | tf_op jit(solution)/shard_map/ppermute | solution.py:487
  125.7 1.5 %collective-permute-start.29 = (bf16[4,272,256]{2,1,0:T(8,128)(2,1)S(1)}, bf16[4,272,256]{2,1,0:T(8,128)(2,1)S(1)}, u32[]{:S(2)}, u32[]{:S(2)}) collective-permute-start(bf16[4,272,256]{2,1,0:T(8,128)(2,1)S(1)} %collective-permute-done.28.refs_2_), channel_id=1, source_target_pairs={{0,1},{1,0},{2,3},{3,2},{4,5},{5,4},{6,7},{7,6},{8,9},{9,8},{10,11... | collective-permute-start | bytes 1671176 | tf_op jit(solution)/shard_map/ppermute | solution.py:41
  127.8 2.4 %projection_grad.4.refs_3_ = f32[2,256,1024]{2,1,0:T(8,128)S(1)} custom-call(s32[4]{0:T(128)S(1)} %pad_add_fusion.where, bf16[4096,1024]{1,0:T(8,128)(2,1)S(1)} %copy-done.1, bf16[4,272,256]{2,1,0:T(8,128)(2,1)S(1)} %collective-permute-done.23.refs_0_, bf16[4,272,256]{2,1,0:T(8,128)(2,1)S(1)} %collective-permute-done.26.refs_1_, ...), custom_call_target="tpu_custom_call" | custom-call | flops 1610612736 | bytes 7864320 | tf_op jit(solution)/shard_map/projection_grad/pallas_call | solution.py:376
  130.4 3.3 %projection_grad.5 = (bf16[512,1024]{1,0:T(8,128)(2,1)}, f32[1,1024]{1,0:T(1,128)}) custom-call(s32[4]{0:T(128)S(1)} %pad_add_fusion.where, bf16[4096,1024]{1,0:T(8,128)(2,1)S(1)} %copy-done.1, bf16[4,272,256]{2,1,0:T(8,128)(2,1)S(1)} %collective-permute-done.25.refs_0_, bf16[4,272,256]{2,1,0:T(8,128)(2,1)S(1)} %collective-permute-done.27.refs_1_, ...), custom_call_target="tpu_custom_call" | custom-call | flops 1610612736 | bytes 7864320 | tf_op jit(solution)/shard_map/projection_grad/pallas_call | solution.py:376
  (68 shorter events, 4.7 us)
Async XLA Ops:
  7.2 105.2 %all-gather.2.cloned.1.call-start = ((), (), s32[]{:S(2)}) async-start(), calls=%async_computation | async-start | bytes 8912896 | tf_op jit(solution)/shard_map/all_gather | solution.py:431
  8.0 1.0 copy-start.2
  9.1 8.0 %copy-start.9 = (s32[4]{0:T(128)S(1)}, s32[4]{0:T(128)}, u32[]{:S(2)}) copy-start(s32[4]{0:T(128)} %param.16) | copy-start | bytes 52
  9.1 8.0 %copy-start.7 = (f32[4]{0:T(128)S(1)}, f32[4]{0:T(128)}, u32[]{:S(2)}) copy-start(f32[4]{0:T(128)} %param.14) | copy-start | bytes 52
  9.1 8.0 %copy-start.10 = (s32[1,4]{1,0:T(1,128)S(1)}, s32[1,4]{1,0:T(1,128)}, u32[]{:S(2)}) copy-start(s32[1,4]{1,0:T(1,128)} %param.17) | copy-start | bytes 52
  15.1 3.0 %collective-permute-start = (bf16[256,1024]{1,0:T(8,128)(2,1)S(1)}, bf16[256,1024]{1,0:T(8,128)(2,1)S(1)}, u32[]{:S(2)}, u32[]{:S(2)}) collective-permute-start(bf16[256,1024]{1,0:T(8,128)(2,1)S(1)} %get-tuple-element.42), channel_id=1, source_target_pairs={{0,1},{1,0},{2,3},{3,2},{4,5},{5,4},{6,7},{7,6},{8,9},{9,8},{10,11... | collective-permute-start | bytes 1572872 | tf_op jit(solution)/shard_map/ppermute | solution.py:41
  16.6 5.3 %collective-permute-start.2 = (bf16[256,1024]{1,0:T(8,128)(2,1)S(1)}, bf16[256,1024]{1,0:T(8,128)(2,1)S(1)}, u32[]{:S(2)}, u32[]{:S(2)}) collective-permute-start(bf16[256,1024]{1,0:T(8,128)(2,1)S(1)} %get-tuple-element.45), channel_id=1, source_target_pairs={{0,1},{1,0},{2,3},{3,2},{4,5},{5,4},{6,7},{7,6},{8,9},{9,8},{10,11... | collective-permute-start | bytes 1572872 | tf_op jit(solution)/shard_map/ppermute | solution.py:41
  16.7 5.2 %collective-permute-start.3 = (bf16[256,1024]{1,0:T(8,128)(2,1)S(1)}, bf16[256,1024]{1,0:T(8,128)(2,1)S(1)}, u32[]{:S(2)}, u32[]{:S(2)}) collective-permute-start(bf16[256,1024]{1,0:T(8,128)(2,1)S(1)} %get-tuple-element.46), channel_id=1, source_target_pairs={{0,1},{1,0},{2,3},{3,2},{4,5},{5,4},{6,7},{7,6},{8,9},{9,8},{10,11... | collective-permute-start | bytes 1572872 | tf_op jit(solution)/shard_map/ppermute | solution.py:41
  19.1 12.3 %copy-start.8 = (s32[4]{0:T(128)S(1)}, s32[4]{0:T(128)}, u32[]{:S(2)}) copy-start(s32[4]{0:T(128)} %param.15) | copy-start | bytes 52
  19.1 22.9 %copy-start.6 = (bf16[1024]{0:T(1024)(128)(2,1)S(1)}, bf16[1024]{0:T(1024)(128)(2,1)}, u32[]{:S(2)}) copy-start(bf16[1024]{0:T(1024)(128)(2,1)} %param.12) | copy-start | bytes 6148
  19.1 27.4 %copy-start.3 = (bf16[256,1024]{1,0:T(8,128)(2,1)S(1)}, bf16[256,1024]{1,0:T(8,128)(2,1)}, u32[]{:S(2)}) copy-start(bf16[256,1024]{1,0:T(8,128)(2,1)} %att.5) | copy-start | bytes 1572868
  19.1 27.4 %collective-permute-start.1 = (bf16[256,1024]{1,0:T(8,128)(2,1)}, bf16[256,1024]{1,0:T(8,128)(2,1)S(1)}, u32[]{:S(2)}, u32[]{:S(2)}) collective-permute-start(bf16[256,1024]{1,0:T(8,128)(2,1)} %add_convert_fusion), channel_id=1, source_target_pairs={{0,4},{1,5},{2,6},{3,7},{4,0},{5,1},{6,2},{7,3},{8,12},{9,13},{10,... | collective-permute-start | bytes 1572872 | tf_op jit(solution)/shard_map/ppermute | solution.py:441
  27.9 18.6 %collective-permute-start.4 = (bf16[256,1024]{1,0:T(8,128)(2,1)}, bf16[256,1024]{1,0:T(8,128)(2,1)S(1)}, u32[]{:S(2)}, u32[]{:S(2)}) collective-permute-start(bf16[256,1024]{1,0:T(8,128)(2,1)} %get-tuple-element.47), channel_id=1, source_target_pairs={{0,1},{1,0},{2,3},{3,2},{4,5},{5,4},{6,7},{7,6},{8,9},{9,8},{10,11... | collective-permute-start | bytes 1572872 | tf_op jit(solution)/shard_map/ppermute | solution.py:41
  28.6 21.3 %collective-permute-start.5 = (bf16[256,1024]{1,0:T(8,128)(2,1)}, bf16[256,1024]{1,0:T(8,128)(2,1)S(1)}, u32[]{:S(2)}, u32[]{:S(2)}) collective-permute-start(bf16[256,1024]{1,0:T(8,128)(2,1)} %get-tuple-element.48), channel_id=1, source_target_pairs={{0,2},{1,3},{2,4},{3,5},{4,6},{5,7},{6,0},{7,1},{8,10},{9,11},{10,... | collective-permute-start | bytes 1572872 | tf_op jit(solution)/shard_map/ppermute | solution.py:450
  28.9 21.0 %collective-permute-start.6 = (bf16[256,1024]{1,0:T(8,128)(2,1)S(1)}, bf16[256,1024]{1,0:T(8,128)(2,1)S(1)}, u32[]{:S(2)}, u32[]{:S(2)}) collective-permute-start(bf16[256,1024]{1,0:T(8,128)(2,1)S(1)} %get-tuple-element.50), channel_id=1, source_target_pairs={{0,6},{1,7},{2,0},{3,1},{4,2},{5,3},{6,4},{7,5},{8,14},{9,15},{10,... | collective-permute-start | bytes 1572872 | tf_op jit(solution)/shard_map/ppermute | solution.py:451
  32.7 9.2 %collective-permute-start.7 = (f32[1,128]{1,0:T(1,128)S(1)}, f32[1,128]{1,0:T(1,128)S(1)}, u32[]{:S(2)}, u32[]{:S(2)}) collective-permute-start(f32[1,128]{1,0:T(1,128)S(1)} %bitcast.28), channel_id=1, source_target_pairs={{0,0},{1,17},{2,34},{3,51},{4,68},{5,85},{6,102},{7,119},{8,8},{9,... | collective-permute-start | bytes 1544 | tf_op jit(solution)/shard_map/ppermute | solution.py:456
  41.9 4.5 %collective-permute-start.8 = (f32[1,128]{1,0:T(1,128)S(1)}, f32[1,128]{1,0:T(1,128)S(1)}, u32[]{:S(2)}, u32[]{:S(2)}) collective-permute-start(f32[1,128]{1,0:T(1,128)S(1)} %bitcast.29), channel_id=1, source_target_pairs={{0,8},{1,25},{2,42},{3,59},{4,76},{5,93},{6,110},{7,127},{8,16},{9... | collective-permute-start | bytes 1544 | tf_op jit(solution)/shard_map/ppermute | solution.py:456
  46.4 3.5 %copy-start.4 = (bf16[256,1024]{1,0:T(8,128)(2,1)S(1)}, bf16[256,1024]{1,0:T(8,128)(2,1)}, u32[]{:S(2)}) copy-start(bf16[256,1024]{1,0:T(8,128)(2,1)} %cot.3) | copy-start | bytes 1572868
  46.4 3.5 %copy-start.5 = (bf16[256,1024]{1,0:T(8,128)(2,1)S(1)}, bf16[256,1024]{1,0:T(8,128)(2,1)}, u32[]{:S(2)}) copy-start(bf16[256,1024]{1,0:T(8,128)(2,1)} %residual) | copy-start | bytes 1572868
  50.6 1.3 collective-permute-start.9
  51.8 4.1 %collective-permute-start.10 = (f32[8,256]{1,0:T(8,128)S(1)}, f32[8,256]{1,0:T(8,128)S(1)}, u32[]{:S(2)}, u32[]{:S(2)}) collective-permute-start(f32[8,256]{1,0:T(8,128)S(1)} %add.31.s0), channel_id=1, source_target_pairs={{0,2},{1,3},{2,4},{3,5},{4,6},{5,7},{6,0},{7,1},{8,10},{9,11},{10,... | collective-permute-start | bytes 24584 | tf_op jit(solution)/shard_map/ppermute | solution.py:466
  52.0 4.1 %collective-permute-start.11 = (f32[8,256]{1,0:T(8,128)S(1)}, f32[8,256]{1,0:T(8,128)S(1)}, u32[]{:S(2)}, u32[]{:S(2)}) collective-permute-start(f32[8,256]{1,0:T(8,128)S(1)} %add.31.s0), channel_id=1, source_target_pairs={{0,4},{1,5},{2,6},{3,7},{4,0},{5,1},{6,2},{7,3},{8,12},{9,13},{10,... | collective-permute-start | bytes 24584 | tf_op jit(solution)/shard_map/ppermute | solution.py:466
  53.8 2.9 %collective-permute-start.12 = (f32[8,256]{1,0:T(8,128)S(1)}, f32[8,256]{1,0:T(8,128)S(1)}, u32[]{:S(2)}, u32[]{:S(2)}) collective-permute-start(f32[8,256]{1,0:T(8,128)S(1)} %add.31.s0), channel_id=1, source_target_pairs={{0,6},{1,7},{2,0},{3,1},{4,2},{5,3},{6,4},{7,5},{8,14},{9,15},{10,... | collective-permute-start | bytes 24584 | tf_op jit(solution)/shard_map/ppermute | solution.py:466
  58.1 13.3 %collective-permute-start.14 = (bf16[256,1024]{1,0:T(8,128)(2,1)S(1)}, bf16[256,1024]{1,0:T(8,128)(2,1)S(1)}, u32[]{:S(2)}, u32[]{:S(2)}) collective-permute-start(bf16[256,1024]{1,0:T(8,128)(2,1)S(1)} %get-tuple-element.57.refs_0_), channel_id=1, source_target_pairs={{0,2},{1,3},{2,4},{3,5},{4,6},{5,7},{6,0},{7,1},{8,10},{9,11},{10,... | collective-permute-start | bytes 1572872 | tf_op jit(solution)/shard_map/ppermute | solution.py:474
  59.4 23.5 %collective-permute-start.16 = (bf16[256,1024]{1,0:T(8,128)(2,1)S(1)}, bf16[256,1024]{1,0:T(8,128)(2,1)S(1)}, u32[]{:S(2)}, u32[]{:S(2)}) collective-permute-start(bf16[256,1024]{1,0:T(8,128)(2,1)S(1)} %get-tuple-element.57.refs_0_), channel_id=1, source_target_pairs={{0,4},{1,5},{2,6},{3,7},{4,0},{5,1},{6,2},{7,3},{8,12},{9,13},{10,... | collective-permute-start | bytes 1572872 | tf_op jit(solution)/shard_map/ppermute | solution.py:474
  61.3 24.1 %collective-permute-start.18 = (bf16[256,1024]{1,0:T(8,128)(2,1)S(1)}, bf16[256,1024]{1,0:T(8,128)(2,1)S(1)}, u32[]{:S(2)}, u32[]{:S(2)}) collective-permute-start(bf16[256,1024]{1,0:T(8,128)(2,1)S(1)} %get-tuple-element.57.refs_0_), channel_id=1, source_target_pairs={{0,6},{1,7},{2,0},{3,1},{4,2},{5,3},{6,4},{7,5},{8,14},{9,15},{10,... | collective-permute-start | bytes 1572872 | tf_op jit(solution)/shard_map/ppermute | solution.py:474
  61.8 23.7 %collective-permute-start.13 = (bf16[256,1024]{1,0:T(8,128)(2,1)S(1)}, bf16[256,1024]{1,0:T(8,128)(2,1)S(1)}, u32[]{:S(2)}, u32[]{:S(2)}) collective-permute-start(bf16[256,1024]{1,0:T(8,128)(2,1)S(1)} %get-tuple-element.57.refs_0_), channel_id=1, source_target_pairs={{0,1},{1,0},{2,3},{3,2},{4,5},{5,4},{6,7},{7,6},{8,9},{9,8},{10,11... | collective-permute-start | bytes 1572872 | tf_op jit(solution)/shard_map/ppermute | solution.py:41
  71.4 14.2 %collective-permute-start.15 = (bf16[256,1024]{1,0:T(8,128)(2,1)S(1)}, bf16[256,1024]{1,0:T(8,128)(2,1)S(1)}, u32[]{:S(2)}, u32[]{:S(2)}) collective-permute-start(bf16[256,1024]{1,0:T(8,128)(2,1)S(1)} %collective-permute-done.14.refs_2_), channel_id=1, source_target_pairs={{0,1},{1,0},{2,3},{3,2},{4,5},{5,4},{6,7},{7,6},{8,9},{9,8},{10,11... | collective-permute-start | bytes 1572872 | tf_op jit(solution)/shard_map/ppermute | solution.py:41
  83.0 4.0 %collective-permute-start.17 = (bf16[256,1024]{1,0:T(8,128)(2,1)S(1)}, bf16[256,1024]{1,0:T(8,128)(2,1)S(1)}, u32[]{:S(2)}, u32[]{:S(2)}) collective-permute-start(bf16[256,1024]{1,0:T(8,128)(2,1)S(1)} %collective-permute-done.16.refs_4_), channel_id=1, source_target_pairs={{0,1},{1,0},{2,3},{3,2},{4,5},{5,4},{6,7},{7,6},{8,9},{9,8},{10,11... | collective-permute-start | bytes 1572872 | tf_op jit(solution)/shard_map/ppermute | solution.py:41
  85.4 2.3 %collective-permute-start.19 = (bf16[256,1024]{1,0:T(8,128)(2,1)S(1)}, bf16[256,1024]{1,0:T(8,128)(2,1)S(1)}, u32[]{:S(2)}, u32[]{:S(2)}) collective-permute-start(bf16[256,1024]{1,0:T(8,128)(2,1)S(1)} %collective-permute-done.18.refs_6_), channel_id=1, source_target_pairs={{0,1},{1,0},{2,3},{3,2},{4,5},{5,4},{6,7},{7,6},{8,9},{9,8},{10,11... | collective-permute-start | bytes 1572872 | tf_op jit(solution)/shard_map/ppermute | solution.py:41
  89.0 11.4 %collective-permute-start.20 = (bf16[4,272,256]{2,1,0:T(8,128)(2,1)S(1)}, bf16[4,272,256]{2,1,0:T(8,128)(2,1)S(1)}, u32[]{:S(2)}, u32[]{:S(2)}) collective-permute-start(bf16[4,272,256]{2,1,0:T(8,128)(2,1)S(1)} %get-tuple-element.60), channel_id=1, source_target_pairs={{0,32},{1,9},{2,34},{3,11},{4,36},{5,13},{6,38},{7,15},{8,40},{9,1... | collective-permute-start | bytes 1671176 | tf_op jit(solution)/shard_map/ppermute | solution.py:480
  89.4 15.6 %collective-permute-start.21 = (bf16[4,272,256]{2,1,0:T(8,128)(2,1)S(1)}, bf16[4,272,256]{2,1,0:T(8,128)(2,1)S(1)}, u32[]{:S(2)}, u32[]{:S(2)}) collective-permute-start(bf16[4,272,256]{2,1,0:T(8,128)(2,1)S(1)} %get-tuple-element.61), channel_id=1, source_target_pairs={{0,64},{1,17},{2,66},{3,19},{4,68},{5,21},{6,70},{7,23},{8,72},{9,... | collective-permute-start | bytes 1671176 | tf_op jit(solution)/shard_map/ppermute | solution.py:480
  91.8 13.7 %collective-permute-start.22 = (bf16[4,272,256]{2,1,0:T(8,128)(2,1)S(1)}, bf16[4,272,256]{2,1,0:T(8,128)(2,1)S(1)}, u32[]{:S(2)}, u32[]{:S(2)}) collective-permute-start(bf16[4,272,256]{2,1,0:T(8,128)(2,1)S(1)} %get-tuple-element.62), channel_id=1, source_target_pairs={{0,96},{1,25},{2,98},{3,27},{4,100},{5,29},{6,102},{7,31},{8,104},... | collective-permute-start | bytes 1671176 | tf_op jit(solution)/shard_map/ppermute | solution.py:480
  107.3 5.0 %collective-permute-start.24 = (bf16[4,272,256]{2,1,0:T(8,128)(2,1)S(1)}, bf16[4,272,256]{2,1,0:T(8,128)(2,1)S(1)}, u32[]{:S(2)}, u32[]{:S(2)}) collective-permute-start(bf16[4,272,256]{2,1,0:T(8,128)(2,1)S(1)} %get-tuple-element.66.refs_0_), channel_id=1, source_target_pairs={{0,1},{1,0},{2,3},{3,2},{4,5},{5,4},{6,7},{7,6},{8,9},{9,8},{10,11... | collective-permute-start | bytes 1671176 | tf_op jit(solution)/shard_map/ppermute | solution.py:41
  108.8 10.1 %collective-permute-start.23 = (bf16[4,272,256]{2,1,0:T(8,128)(2,1)}, bf16[4,272,256]{2,1,0:T(8,128)(2,1)S(1)}, u32[]{:S(2)}, u32[]{:S(2)}) collective-permute-start(bf16[4,272,256]{2,1,0:T(8,128)(2,1)} %get-tuple-element.65), channel_id=1, source_target_pairs={{0,8},{1,33},{2,10},{3,35},{4,12},{5,37},{6,14},{7,39},{8,16},{9,4... | collective-permute-start | bytes 1671176 | tf_op jit(solution)/shard_map/ppermute | solution.py:487
  110.1 8.9 %collective-permute-start.26 = (bf16[4,272,256]{2,1,0:T(8,128)(2,1)}, bf16[4,272,256]{2,1,0:T(8,128)(2,1)S(1)}, u32[]{:S(2)}, u32[]{:S(2)}) collective-permute-start(bf16[4,272,256]{2,1,0:T(8,128)(2,1)} %get-tuple-element.68), channel_id=1, source_target_pairs={{0,24},{1,97},{2,26},{3,99},{4,28},{5,101},{6,30},{7,103},{8,0},{9... | collective-permute-start | bytes 1671176 | tf_op jit(solution)/shard_map/ppermute | solution.py:487
  111.5 14.2 %collective-permute-start.28 = (bf16[4,272,256]{2,1,0:T(8,128)(2,1)S(1)}, bf16[4,272,256]{2,1,0:T(8,128)(2,1)S(1)}, u32[]{:S(2)}, u32[]{:S(2)}) collective-permute-start(bf16[4,272,256]{2,1,0:T(8,128)(2,1)S(1)} %get-tuple-element.71), channel_id=1, source_target_pairs={{0,16},{1,65},{2,18},{3,67},{4,20},{5,69},{6,22},{7,71},{8,24},{9,... | collective-permute-start | bytes 1671176 | tf_op jit(solution)/shard_map/ppermute | solution.py:487
  112.4 3.4 %copy-start = (bf16[4096,1024]{1,0:T(8,128)(2,1)S(1)}, bf16[4096,1024]{1,0:T(8,128)(2,1)}, u32[]{:S(2)}) copy-start(bf16[4096,1024]{1,0:T(8,128)(2,1)} %all-gather.2.cloned.1.call-done.gathered) | copy-start | bytes 25165828
  115.7 12.0 %copy-start.1 = (bf16[4096,1024]{1,0:T(8,128)(2,1)S(1)}, bf16[4096,1024]{1,0:T(8,128)(2,1)}, u32[]{:S(2)}) copy-start(bf16[4096,1024]{1,0:T(8,128)(2,1)} %all-gather.2.cloned.1.call-done.gathered) | copy-start | bytes 25165828
  125.7 4.5 %collective-permute-start.29 = (bf16[4,272,256]{2,1,0:T(8,128)(2,1)S(1)}, bf16[4,272,256]{2,1,0:T(8,128)(2,1)S(1)}, u32[]{:S(2)}, u32[]{:S(2)}) collective-permute-start(bf16[4,272,256]{2,1,0:T(8,128)(2,1)S(1)} %collective-permute-done.28.refs_2_), channel_id=1, source_target_pairs={{0,1},{1,0},{2,3},{3,2},{4,5},{5,4},{6,7},{7,6},{8,9},{9,8},{10,11... | collective-permute-start | bytes 1671176 | tf_op jit(solution)/shard_map/ppermute | solution.py:41
  127.2 3.0 %collective-permute-start.27 = (bf16[4,272,256]{2,1,0:T(8,128)(2,1)S(1)}, bf16[4,272,256]{2,1,0:T(8,128)(2,1)S(1)}, u32[]{:S(2)}, u32[]{:S(2)}) collective-permute-start(bf16[4,272,256]{2,1,0:T(8,128)(2,1)S(1)} %collective-permute-done.26.refs_1_), channel_id=1, source_target_pairs={{0,1},{1,0},{2,3},{3,2},{4,5},{5,4},{6,7},{7,6},{8,9},{9,8},{10,11... | collective-permute-start | bytes 1671176 | tf_op jit(solution)/shard_map/ppermute | solution.py:41
  127.2 3.2 %collective-permute-start.25 = (bf16[4,272,256]{2,1,0:T(8,128)(2,1)S(1)}, bf16[4,272,256]{2,1,0:T(8,128)(2,1)S(1)}, u32[]{:S(2)}, u32[]{:S(2)}) collective-permute-start(bf16[4,272,256]{2,1,0:T(8,128)(2,1)S(1)} %collective-permute-done.23.refs_0_), channel_id=1, source_target_pairs={{0,1},{1,0},{2,3},{3,2},{4,5},{5,4},{6,7},{7,6},{8,9},{9,8},{10,11... | collective-permute-start | bytes 1671176 | tf_op jit(solution)/shard_map/ppermute | solution.py:41
Sparse Core Ops, SparseCore 0:
  10.1 74.2 all-gather.1

commit v4 on v3

--- a/solution.py
+++ b/solution.py
@@ -105,6 +105,56 @@
     )(where, attention, out_proj, *got)
 
 
+def halves_kernel(first, second, top, bottom):
+    rows = top.shape[0]
+
+    @pl.loop(0, rows // 64)
+    def _(i):
+        for n, out in ((0, top), (1, bottom)):
+            band = pl.ds(pl.multiple_of(n * rows + i * 64, 64), 64)
+            here = pl.ds(pl.multiple_of(i * 64, 64), 64)
+            out[here, :] = (first[band, :] + second[band, :].astype(F32)).astype(BF)
+
+
+def passed_kernel(first, third, top, bottom, next_first, next_third):
+    rows = top.shape[0]
+
+    @pl.loop(0, rows // 64)
+    def _(i):
+        low = pl.ds(pl.multiple_of(i * 64, 64), 64)
+        high = pl.ds(pl.multiple_of(rows + i * 64, 64), 64)
+        next_first[low, :] = (first[low, :] + top[low, :].astype(F32)).astype(BF)
+        next_first[high, :] = first[high, :].astype(BF)
+        next_third[low, :] = third[low, :].astype(BF)
+        next_third[high, :] = (third[high, :] + bottom[low, :].astype(F32)).astype(BF)
+
+
+def joined_kernel(top, bottom, out):
+    rows = top.shape[0]
+
+    @pl.loop(0, rows // 64)
+    def _(i):
+        low = pl.ds(pl.multiple_of(i * 64, 64), 64)
+        high = pl.ds(pl.multiple_of(rows + i * 64, 64), 64)
+        out[low, :] = top[low, :]
+        out[high, :] = bottom[low, :]
+
+
+def small_call(kernel, inputs, shapes, name):
+    vmem = pl.BlockSpec(memory_space=pltpu.VMEM)
+    return pl.pallas_call(
+        kernel,
+        in_specs=[vmem] * len(inputs),
+        out_specs=[vmem] * len(shapes),
+        out_shape=[jax.ShapeDtypeStruct(shape, BF) for shape in shapes],
+        compiler_params=pltpu.CompilerParams(vmem_limit_bytes=SMALL),
+        cost_estimate=pl.CostEstimate(
+            flops=inputs[0].size, bytes_accessed=8 * inputs[0].size, transcendentals=0
+        ),
+        name=name,
+    )(*inputs)
+
+
 def row_sums(value):
     rows, width = value.shape
     part = value[:, 0:128]
@@ -113,21 +163,21 @@
     return jnp.sum(part.T, axis=0, keepdims=True)
 
 
-def hidden_kernel(own, r1, r2, r3, residual, cot, gain, stats, hidden, sums):
+def hidden_kernel(own, r1, r3, residual, cot, gain, even, odd, hidden, sums):
     @pl.loop(0, own.shape[0] // 128)
     def _(i):
         band = pl.ds(pl.multiple_of(i * 128, 128), 128)
         h = own[band, :] + residual[band, :].astype(F32)
-        h = h + r1[band, :].astype(F32) + r2[band, :].astype(F32) + r3[band, :].astype(F32)
+        h = h + r1[band, :].astype(F32) + r3[band, :].astype(F32)
         hidden[band, :] = h
         scaled = cot[band, :].astype(F32) * gain[...].astype(F32)
         first = row_sums(h * h)
         second = row_sums(scaled * h)
-        rest = [stats[...], jnp.zeros((5, 128), F32)]
+        rest = [even[...] + odd[...], jnp.zeros((5, 128), F32)]
         sums[:, band] = jnp.concatenate([first, second] + rest, axis=0)
 
 
-def hidden_call(own, r1, r2, r3, residual, cot, gain, stats):
+def hidden_call(own, r1, r3, residual, cot, gain, even, odd):
     rows, width = own.shape
     vmem = pl.BlockSpec(memory_space=pltpu.VMEM)
     return pl.pallas_call(
@@ -143,7 +193,7 @@
             flops=12 * rows * width, bytes_accessed=20 * rows * width, transcendentals=0
         ),
         name="hidden",
-    )(own, r1, r2, r3, residual, cot, gain, stats)
+    )(own, r1, r3, residual, cot, gain, even, odd)
 
 
 def column(row):
@@ -428,8 +478,6 @@
     where = jnp.stack([d // 4, d % 4, t // 2, t % 2]).astype(jnp.int32)
     gain = norm_gain[None, :]
 
-    gathered = lax.all_gather(attention, "dp", axis=0, tiled=True)
-
     arrived = {}
     send2, keep2, send1, send3 = partial_products(
         where,
@@ -437,29 +485,37 @@
         out_proj,
         [(2, True, False, BF), (2, False, False, F32), (1, True, False, BF), (3, True, False, BF)],
     )
-    both = (keep2 + swap(send2).astype(F32)).astype(BF)
-    arrived[2] = lax.ppermute(both, "tensor", x_shift(2))
-    late_where, _ = lax.optimization_barrier((where, both))
+    gathered = lax.all_gather(attention, "dp", axis=0, tiled=True)
+    width = features // 8
+    top, bottom = small_call(
+        halves_kernel, [keep2, swap(send2)], [(rows // 2, width)] * 2, "halves"
+    )
+    late_where, _, _ = lax.optimization_barrier((where, top, bottom))
+    top = lax.ppermute(top, "tensor", x_shift(1))
+    bottom = lax.ppermute(bottom, "tensor", x_shift(3))
     first, third, send0 = partial_products(
         late_where,
         attention,
         out_proj,
-        [(1, False, True, BF), (3, False, True, BF), (0, True, False, BF)],
+        [(1, False, True, F32), (3, False, True, F32), (0, True, False, BF)],
         [swap(send1), swap(send3)],
+    )
+    first, third = small_call(
+        passed_kernel, [first, third, top, bottom], [(rows, width)] * 2, "passed"
     )
     arrived[1] = lax.ppermute(first, "tensor", x_shift(1))
     arrived[3] = lax.ppermute(third, "tensor", x_shift(3))
     stats = local_stats(rewards, group_ids, kept_flags, lengths)
     info = token_info(rewards, group_ids, kept_flags, lengths, rows)
     stats, info, _ = lax.optimization_barrier((stats, info, third))
-    late_where, arrived[2] = lax.optimization_barrier((where, arrived[2]))
-    stats = sum(lax.ppermute(stats, ("dp", "tensor"), scattered(step)) for step in (0, 1))
+    late_where, _ = lax.optimization_barrier((where, third))
+    stats = [lax.ppermute(stats, ("dp", "tensor"), scattered(step)) for step in (0, 1)]
     (own,) = partial_products(
         late_where, attention, out_proj, [(0, False, True, F32)], [swap(send0)]
     )
     residual, info = lax.optimization_barrier((residual, info))
     hidden, sums = hidden_call(
-        own, arrived[1], arrived[2], arrived[3], residual, cotangent, gain, stats
+        own, arrived[1], arrived[3], residual, cotangent, gain, *stats
     )
 
     chip = sums + swap(sums)
@@ -469,30 +525,33 @@
         features, tokens, hidden, cotangent, gain, chip, *others, info
     )
 
+    near = {k: lax.ppermute(own_piece, "tensor", x_shift(k)) for k in (1, 3)}
+    top = lax.ppermute(near[1][: rows // 2], "tensor", x_shift(1))
+    bottom = lax.ppermute(near[3][rows // 2 :], "tensor", x_shift(3))
+    (far,) = small_call(joined_kernel, [top, bottom], [(rows, width)], "joined")
     pieces = []
-    for k in range(4):
-        piece = own_piece if k == 0 else lax.ppermute(own_piece, "tensor", x_shift(k))
+    for piece in (own_piece, near[1], far, near[3]):
         pieces.extend([piece, swap(piece)])
-
     half = features // 32
     sends = pack_call(first_pack_kernel, where, pieces + [gain_term], rows, half, "first_pack")
-    parts = [sends[0]] + [
-        lax.ppermute(sends[k], ("dp", "tensor"), plane_shift(0, k)) for k in (1, 2, 3)
-    ]
+    parts = {0: sends[0]}
+    for k in (2, 1, 3):
+        parts[k] = lax.ppermute(sends[k], ("dp", "tensor"), plane_shift(0, k))
+    parts = [parts[k] for k in range(4)]
     late_where, _ = lax.optimization_barrier((where, sends))
     grad_attention = attention_call(late_where, pieces, out_proj)
     pack_where, _ = lax.optimization_barrier((where, grad_attention))
     sends = pack_call(second_pack_kernel, pack_where, parts, rows, half, "second_pack")
-    mine = [sends[0]] + [
-        lax.ppermute(sends[k], ("dp", "tensor"), plane_shift(1, k)) for k in (1, 2, 3)
-    ]
+    mine = {0: sends[0]}
+    for k in (2, 1, 3):
+        mine[k] = lax.ppermute(sends[k], ("dp", "tensor"), plane_shift(1, k))
     theirs = [swap(mine[0]), None, None, None]
     total = projection_call(where, mine, theirs, gathered, ((0,), (0,)), None)
     for k in (1, 3, 2):
         mine[k], total = lax.optimization_barrier((mine[k], total))
         theirs[k] = swap(mine[k])
     total = projection_call(where, mine, theirs, gathered, ((1, 3, 2), ()), total)
-    tails = sum(part[:, rows:, :].astype(F32) for part in mine)
+    tails = sum(part[:, rows:, :].astype(F32) for part in mine.values())
     tails = jnp.concatenate([tails[j] for j in range(4)], axis=1)
     grad_out_proj, grad_gain = projection_call(
         where, mine, theirs, gathered, ((), (1, 3, 2)), total, tails

time: 141 us -> 133 us (0.943)
  waiting for transfers between devices: 44.2 us -> 29.2 us
  starting transfers between devices: 38.5 us -> 47 us
    ppermute x2, waiting for transfers between devices: 8.88 us -> 0.01 us  [shards(): lax.ppermute(stats, ('dp', 'tensor'), scattered(step))]
    ppermute x10 -> x12, waiting for transfers between devices: 28.5 us -> 22.6 us  [the longest x2 10.4 us: shards(): near = {k: lax.ppermute(own_piece, 'tensor', x_shift(k)) for k in (1, 3)}]
    ppermute x10 -> x12, starting transfers between devices: 13.5 us -> 17 us  [the longest x3 5.14 us: shards(): parts[k] = lax.ppermute(sends[k], ('dp', 'tensor'), plane_shift(0, k))]
    ppermute x2, starting transfers between devices: 4.81 us -> 7.19 us  [shards(): lax.ppermute(stats, ('dp', 'tensor'), scattered(step))]
    ppermute x3, starting transfers between devices: 2.68 us -> 4.32 us  [shards(): others = [lax.ppermute(chip, 'tensor', x_shift(k)) for k in (1, 2, 3)]]
  transfers between devices with their start and end apart: 31 -> 33, of which waited for: 16 -> 12; matrix products, arithmetic and copies ran while one was open for 2% -> 2% of each run, Pallas kernels for 23% -> 25%
where the time goes in v4:
time: 133 us
  starting transfers between devices  47 us (35%)
  Pallas kernels  36 us (27%)
  waiting for transfers between devices  29.2 us (22%)
  between operations  14.3 us (11%)
  local copies, waits for them, and re-layouts  5.31 us (4%)
    ppermute x13, starting transfers between devices, swap(): return lax.ppermute(value, 'tensor', CORE_SWAP)  15.8 us
    pallas_call x3, Pallas kernels, partial_products(): pl.pallas_call(functools.partial(partial_kernel, jobs), in_specs=[pl.Bloc...  14.2 us
    ppermute x2, waiting for transfers between devices, shards(): near = {k: lax.ppermute(own_piece, 'tensor', x_shift(k)) for k in (1, 3)}  10.4 us
    pallas_call x1, Pallas kernels, attention_call(): pl.pallas_call(attention_kernel, in_specs=[pl.BlockSpec(memory_space=pltp...  7.98 us
    ppermute x3, waiting for transfers between devices, shards(): mine[k] = lax.ppermute(sends[k], ('dp', 'tensor'), plane_shift(1, k))  7.57 us
    pallas_call x3, Pallas kernels, projection_call(): pl.pallas_call(functools.partial(projection_kernel, members, first, last)...  7.51 us
    ppermute x2, starting transfers between devices, shards(): lax.ppermute(stats, ('dp', 'tensor'), scattered(step))  7.19 us
    ppermute x3, starting transfers between devices, shards(): parts[k] = lax.ppermute(sends[k], ('dp', 'tensor'), plane_shift(0, k))  5.14 us
  transfers between devices with their start and end apart: 33, of which 12 were waited for; matrix products, arithmetic and copies ran while one was open for 2% of the time, Pallas kernels for 25%

profile of v4, /device:TPU:1, one launch (start us, length us, event | category | flops | bytes accessed | tf_op | source)
XLA Modules:
  0.0 133.2 jit_solution(9215771254888974702)
XLA Ops:
  7.2 0.7 all-gather.2.cloned.1.call-update
  8.0 1.0 copy-done.2
  9.1 6.0 %partial.3 = (bf16[256,1024]{1,0:T(8,128)(2,1)S(1)}, f32[256,1024]{1,0:T(8,128)S(1)}, bf16[256,1024]{1,0:T(8,128)(2,1)S(1)}, bf16[256,1024]{1,0:T(8,128)(2,1)S(1)}) custom-call(s32[4]{0:T(128)S(1)} %pad_add_fusion.where, bf16[256,1024]{1,0:T(8,128)(2,1)S(1)} %copy-done.2, bf16[8192,1024]{1,0:T(8,128)(2,1)} %refs_8_.1), custom_call_target="tpu_custom_call" | custom-call | flops 2147483648 | bytes 8388608 | tf_op jit(solution)/shard_map/partial/pallas_call | solution.py:89
  15.1 1.5 %collective-permute-start = (bf16[256,1024]{1,0:T(8,128)(2,1)S(1)}, bf16[256,1024]{1,0:T(8,128)(2,1)S(1)}, u32[]{:S(2)}, u32[]{:S(2)}) collective-permute-start(bf16[256,1024]{1,0:T(8,128)(2,1)S(1)} %get-tuple-element.45), channel_id=1, source_target_pairs={{0,1},{1,0},{2,3},{3,2},{4,5},{5,4},{6,7},{7,6},{8,9},{9,8},{10,11... | collective-permute-start | bytes 1572872 | tf_op jit(solution)/shard_map/ppermute | solution.py:41
  17.1 1.0 collective-permute-done.second
  18.2 1.4 %collective-permute-start.3 = (bf16[128,1024]{1,0:T(8,128)(2,1)S(1)}, bf16[128,1024]{1,0:T(8,128)(2,1)S(1)}, u32[]{:S(2)}, u32[]{:S(2)}) collective-permute-start(bf16[128,1024]{1,0:T(8,128)(2,1)S(1)} %get-tuple-element.46), channel_id=1, source_target_pairs={{0,2},{1,3},{2,4},{3,5},{4,6},{5,7},{6,0},{7,1},{8,10},{9,11},{10,... | collective-permute-start | bytes 786440 | tf_op jit(solution)/shard_map/ppermute | solution.py:494
  19.6 1.4 %collective-permute-start.4 = (bf16[128,1024]{1,0:T(8,128)(2,1)S(1)}, bf16[128,1024]{1,0:T(8,128)(2,1)S(1)}, u32[]{:S(2)}, u32[]{:S(2)}) collective-permute-start(bf16[128,1024]{1,0:T(8,128)(2,1)S(1)} %get-tuple-element.47), channel_id=1, source_target_pairs={{0,6},{1,7},{2,0},{3,1},{4,2},{5,3},{6,4},{7,5},{8,14},{9,15},{10,... | collective-permute-start | bytes 786440 | tf_op jit(solution)/shard_map/ppermute | solution.py:495
  21.0 0.6 convert_multiply_fusion
  21.6 5.2 %partial.4 = (f32[256,1024]{1,0:T(8,128)S(1)}, f32[256,1024]{1,0:T(8,128)S(1)}, bf16[256,1024]{1,0:T(8,128)(2,1)S(1)}) custom-call(s32[4]{0:T(128)S(1)} %pad_add_fusion.where, bf16[256,1024]{1,0:T(8,128)(2,1)S(1)} %copy-done.2, bf16[8192,1024]{1,0:T(8,128)(2,1)} %refs_8_.1, bf16[256,1024]{1,0:T(8,128)(2,1)S(1)} %collective-permute-done.1.refs_0_, ...), custom_call_target="tpu_custom_call" | custom-call | flops 1610612736 | bytes 6291456 | tf_op jit(solution)/shard_map/partial/pallas_call | solution.py:89
  26.8 1.0 collective-permute-start.5
  27.8 0.9 passed.1
  28.9 2.5 %collective-permute-start.7 = (bf16[256,1024]{1,0:T(8,128)(2,1)S(1)}, bf16[256,1024]{1,0:T(8,128)(2,1)S(1)}, u32[]{:S(2)}, u32[]{:S(2)}) collective-permute-start(bf16[256,1024]{1,0:T(8,128)(2,1)S(1)} %get-tuple-element.53), channel_id=1, source_target_pairs={{0,6},{1,7},{2,0},{3,1},{4,2},{5,3},{6,4},{7,5},{8,14},{9,15},{10,... | collective-permute-start | bytes 1572872 | tf_op jit(solution)/shard_map/ppermute | solution.py:507
  31.8 0.7 concatenate.9
  32.8 5.0 %collective-permute-start.8 = (f32[1,128]{1,0:T(1,128)S(1)}, f32[1,128]{1,0:T(1,128)S(1)}, u32[]{:S(2)}, u32[]{:S(2)}) collective-permute-start(f32[1,128]{1,0:T(1,128)S(1)} %bitcast.28), channel_id=1, source_target_pairs={{0,0},{1,17},{2,34},{3,51},{4,68},{5,85},{6,102},{7,119},{8,8},{9,... | collective-permute-start | bytes 1544 | tf_op jit(solution)/shard_map/ppermute | solution.py:512
  37.9 2.2 %collective-permute-start.9 = (f32[1,128]{1,0:T(1,128)S(1)}, f32[1,128]{1,0:T(1,128)S(1)}, u32[]{:S(2)}, u32[]{:S(2)}) collective-permute-start(f32[1,128]{1,0:T(1,128)S(1)} %bitcast.29), channel_id=1, source_target_pairs={{0,8},{1,25},{2,42},{3,59},{4,76},{5,93},{6,110},{7,127},{8,16},{9... | collective-permute-start | bytes 1544 | tf_op jit(solution)/shard_map/ppermute | solution.py:512
  40.0 3.0 %partial.5.own = f32[256,1024]{1,0:T(8,128)S(1)} custom-call(s32[4]{0:T(128)S(1)} %pad_add_fusion.where, bf16[256,1024]{1,0:T(8,128)(2,1)S(1)} %copy-done.3, bf16[8192,1024]{1,0:T(8,128)(2,1)} %refs_8_.1, bf16[256,1024]{1,0:T(8,128)(2,1)S(1)} %collective-permute-done.5.refs_0_), custom_call_target="tpu_custom_call" | custom-call | flops 536870912 | bytes 2097152 | tf_op jit(solution)/shard_map/partial/pallas_call | solution.py:89
  43.8 1.4 %collective-permute-start.10 = (f32[8,256]{1,0:T(8,128)S(1)}, f32[8,256]{1,0:T(8,128)S(1)}, u32[]{:S(2)}, u32[]{:S(2)}) collective-permute-start(f32[8,256]{1,0:T(8,128)S(1)} %get-tuple-element.61), channel_id=1, source_target_pairs={{0,1},{1,0},{2,3},{3,2},{4,5},{5,4},{6,7},{7,6},{8,9},{9,8},{10,11... | collective-permute-start | bytes 24584 | tf_op jit(solution)/shard_map/ppermute | solution.py:41
  45.2 0.8 collective-permute-done.10
  46.0 1.0 collective-permute-start.11
  47.0 2.7 %collective-permute-start.12 = (f32[8,256]{1,0:T(8,128)S(1)}, f32[8,256]{1,0:T(8,128)S(1)}, u32[]{:S(2)}, u32[]{:S(2)}) collective-permute-start(f32[8,256]{1,0:T(8,128)S(1)} %add.23.s0), channel_id=1, source_target_pairs={{0,4},{1,5},{2,6},{3,7},{4,0},{5,1},{6,2},{7,3},{8,12},{9,13},{10,... | collective-permute-start | bytes 24584 | tf_op jit(solution)/shard_map/ppermute | solution.py:522
  49.6 0.7 collective-permute-start.13
  50.3 0.7 collective-permute-done.12.s2
  51.0 1.5 %collective-permute-done.13.s3 = f32[8,256]{1,0:T(8,128)S(1)} collective-permute-done((f32[8,256]{1,0:T(8,128)S(1)}, f32[8,256]{1,0:T(8,128)S(1)}, u32[]{:S(2)}, u32[]{:S(2)}) %collective-permute-start.13) | collective-permute-done | bytes 8224 | tf_op jit(solution)/shard_map/ppermute | solution.py:522
  52.5 1.5 %grad.1 = (bf16[256,1024]{1,0:T(8,128)(2,1)}, bf16[256,1024]{1,0:T(8,128)(2,1)S(1)}, f32[1,1024]{1,0:T(1,128)S(1)}) custom-call(f32[256,1024]{1,0:T(8,128)S(1)} %get-tuple-element.60.hidden, bf16[256,1024]{1,0:T(8,128)(2,1)S(1)} %copy-done.4, bf16[1,1024]{1,0:T(2,128)(2,1)S(1)} %broadcast_in_dim.43.gain, f32[8,256]{1,0:T(8,128)S(1)} %add.23.s0, ...), custom_call_target="tpu_custom_call" | custom-call | flops 3145728 | bytes 2097152 | tf_op jit(solution)/shard_map/grad/pallas_call | solution.py:259
  54.0 2.7 %collective-permute-start.18 = (bf16[256,1024]{1,0:T(8,128)(2,1)S(1)}, bf16[256,1024]{1,0:T(8,128)(2,1)S(1)}, u32[]{:S(2)}, u32[]{:S(2)}) collective-permute-start(bf16[256,1024]{1,0:T(8,128)(2,1)S(1)} %get-tuple-element.63.refs_0_), channel_id=1, source_target_pairs={{0,6},{1,7},{2,0},{3,1},{4,2},{5,3},{6,4},{7,5},{8,14},{9,15},{10,... | collective-permute-start | bytes 1572872 | tf_op jit(solution)/shard_map/ppermute | solution.py:528
  56.7 10.4 %collective-permute-done.15.refs_2_ = bf16[256,1024]{1,0:T(8,128)(2,1)S(1)} collective-permute-done((bf16[256,1024]{1,0:T(8,128)(2,1)S(1)}, bf16[256,1024]{1,0:T(8,128)(2,1)S(1)}, u32[]{:S(2)}, u32[]{:S(2)}) %collective-permute-start.15) | collective-permute-done | bytes 524320 | tf_op jit(solution)/shard_map/ppermute | solution.py:528
  67.2 2.7 %collective-permute-start.19 = (bf16[128,1024]{1,0:T(8,128)(2,1)S(1)}, bf16[128,1024]{1,0:T(8,128)(2,1)S(1)}, u32[]{:S(2)}, u32[]{:S(2)}) collective-permute-start(bf16[128,1024]{1,0:T(8,128)(2,1)S(1)} %slice.41), channel_id=1, source_target_pairs={{0,6},{1,7},{2,0},{3,1},{4,2},{5,3},{6,4},{7,5},{8,14},{9,15},{10,... | collective-permute-start | bytes 786440 | tf_op jit(solution)/shard_map/ppermute | solution.py:530
  69.9 3.0 %collective-permute-start.14 = (bf16[256,1024]{1,0:T(8,128)(2,1)S(1)}, bf16[256,1024]{1,0:T(8,128)(2,1)S(1)}, u32[]{:S(2)}, u32[]{:S(2)}) collective-permute-start(bf16[256,1024]{1,0:T(8,128)(2,1)S(1)} %get-tuple-element.63.refs_0_), channel_id=1, source_target_pairs={{0,1},{1,0},{2,3},{3,2},{4,5},{5,4},{6,7},{7,6},{8,9},{9,8},{10,11... | collective-permute-start | bytes 1572872 | tf_op jit(solution)/shard_map/ppermute | solution.py:41
  74.1 3.3 %collective-permute-start.20 = (bf16[256,1024]{1,0:T(8,128)(2,1)S(1)}, bf16[256,1024]{1,0:T(8,128)(2,1)S(1)}, u32[]{:S(2)}, u32[]{:S(2)}) collective-permute-start(bf16[256,1024]{1,0:T(8,128)(2,1)S(1)} %joined.1.refs_4_), channel_id=1, source_target_pairs={{0,1},{1,0},{2,3},{3,2},{4,5},{5,4},{6,7},{7,6},{8,9},{9,8},{10,11... | collective-permute-start | bytes 1572872 | tf_op jit(solution)/shard_map/ppermute | solution.py:41
  77.4 1.5 %collective-permute-done.20.refs_5_ = bf16[256,1024]{1,0:T(8,128)(2,1)S(1)} collective-permute-done((bf16[256,1024]{1,0:T(8,128)(2,1)S(1)}, bf16[256,1024]{1,0:T(8,128)(2,1)S(1)}, u32[]{:S(2)}, u32[]{:S(2)}) %collective-permute-start.20) | collective-permute-done | bytes 524320 | tf_op jit(solution)/shard_map/ppermute | solution.py:41
  78.9 1.5 %first_pack.1 = (bf16[4,272,256]{2,1,0:T(8,128)(2,1)S(1)}, bf16[4,272,256]{2,1,0:T(8,128)(2,1)S(1)}, bf16[4,272,256]{2,1,0:T(8,128)(2,1)S(1)}, bf16[4,272,256]{2,1,0:T(8,128)(2,1)S(1)}) custom-call(s32[4]{0:T(128)S(1)} %pad_add_fusion.where, bf16[256,1024]{1,0:T(8,128)(2,1)S(1)} %get-tuple-element.63.refs_0_, ...), custom_call_target="tpu_custom_call" | custom-call | bytes 4194304 | tf_op jit(solution)/shard_map/first_pack/pallas_call | solution.py:369
  80.4 1.5 %collective-permute-start.22 = (bf16[4,272,256]{2,1,0:T(8,128)(2,1)S(1)}, bf16[4,272,256]{2,1,0:T(8,128)(2,1)S(1)}, u32[]{:S(2)}, u32[]{:S(2)}) collective-permute-start(bf16[4,272,256]{2,1,0:T(8,128)(2,1)S(1)} %get-tuple-element.66), channel_id=1, source_target_pairs={{0,32},{1,9},{2,34},{3,11},{4,36},{5,13},{6,38},{7,15},{8,40},{9,1... | collective-permute-start | bytes 1671176 | tf_op jit(solution)/shard_map/ppermute | solution.py:539
  81.9 2.6 %collective-permute-start.23 = (bf16[4,272,256]{2,1,0:T(8,128)(2,1)S(1)}, bf16[4,272,256]{2,1,0:T(8,128)(2,1)S(1)}, u32[]{:S(2)}, u32[]{:S(2)}) collective-permute-start(bf16[4,272,256]{2,1,0:T(8,128)(2,1)S(1)} %get-tuple-element.67), channel_id=1, source_target_pairs={{0,64},{1,17},{2,66},{3,19},{4,68},{5,21},{6,70},{7,23},{8,72},{9,... | collective-permute-start | bytes 1671176 | tf_op jit(solution)/shard_map/ppermute | solution.py:539
  84.5 1.1 collective-permute-start.24
  85.6 8.0 %attention_grad.1 = bf16[256,1024]{1,0:T(8,128)(2,1)} custom-call(s32[4]{0:T(128)S(1)} %pad_add_fusion.where, bf16[256,1024]{1,0:T(8,128)(2,1)S(1)} %get-tuple-element.63.refs_0_, bf16[256,1024]{1,0:T(8,128)(2,1)S(1)} %collective-permute-done.14.refs_1_, bf16[256,1024]{1,0:T(8,128)(2,1)S(1)} %collective-permute-done.15.refs_2_, ...), custom_call_target="tpu_custom_call" | custom-call | flops 4294967296 | bytes 16777216 | tf_op jit(solution)/shard_map/attention_grad/pallas_call | solution.py:302
  93.6 4.1 %collective-permute-done.23.refs_2_ = bf16[4,272,256]{2,1,0:T(8,128)(2,1)S(1)} collective-permute-done((bf16[4,272,256]{2,1,0:T(8,128)(2,1)S(1)}, bf16[4,272,256]{2,1,0:T(8,128)(2,1)S(1)}, u32[]{:S(2)}, u32[]{:S(2)}) %collective-permute-start.23) | collective-permute-done | bytes 557088 | tf_op jit(solution)/shard_map/ppermute | solution.py:539
  97.7 1.8 %second_pack.1 = (bf16[4,272,256]{2,1,0:T(8,128)(2,1)S(1)}, bf16[4,272,256]{2,1,0:T(8,128)(2,1)}, bf16[4,272,256]{2,1,0:T(8,128)(2,1)S(1)}, bf16[4,272,256]{2,1,0:T(8,128)(2,1)}) custom-call(s32[4]{0:T(128)S(1)} %pad_add_fusion.where, bf16[4,272,256]{2,1,0:T(8,128)(2,1)S(1)} %get-tuple-element.65.refs_0_, ...), custom_call_target="tpu_custom_call" | custom-call | bytes 4194304 | tf_op jit(solution)/shard_map/second_pack/pallas_call | solution.py:369
  99.4 2.2 %collective-permute-start.26 = (bf16[4,272,256]{2,1,0:T(8,128)(2,1)S(1)}, bf16[4,272,256]{2,1,0:T(8,128)(2,1)S(1)}, u32[]{:S(2)}, u32[]{:S(2)}) collective-permute-start(bf16[4,272,256]{2,1,0:T(8,128)(2,1)S(1)} %get-tuple-element.72.refs_0_), channel_id=1, source_target_pairs={{0,1},{1,0},{2,3},{3,2},{4,5},{5,4},{6,7},{7,6},{8,9},{9,8},{10,11... | collective-permute-start | bytes 1671176 | tf_op jit(solution)/shard_map/ppermute | solution.py:41
  101.6 1.2 collective-permute-start.25
  102.8 1.4 %collective-permute-start.28 = (bf16[4,272,256]{2,1,0:T(8,128)(2,1)}, bf16[4,272,256]{2,1,0:T(8,128)(2,1)S(1)}, u32[]{:S(2)}, u32[]{:S(2)}) collective-permute-start(bf16[4,272,256]{2,1,0:T(8,128)(2,1)} %get-tuple-element.74), channel_id=1, source_target_pairs={{0,24},{1,97},{2,26},{3,99},{4,28},{5,101},{6,30},{7,103},{8,0},{9... | collective-permute-start | bytes 1671176 | tf_op jit(solution)/shard_map/ppermute | solution.py:547
  104.3 1.0 collective-permute-start.30
  105.3 3.4 %copy-done = bf16[4096,1024]{1,0:T(8,128)(2,1)S(1)} copy-done((bf16[4096,1024]{1,0:T(8,128)(2,1)S(1)}, bf16[4096,1024]{1,0:T(8,128)(2,1)}, u32[]{:S(2)}) %copy-start) | copy-done | bytes 8388632
  108.7 1.8 %projection_grad.3.refs_3_ = f32[2,256,1024]{2,1,0:T(8,128)S(1)} custom-call(s32[4]{0:T(128)S(1)} %pad_add_fusion.where, bf16[4096,1024]{1,0:T(8,128)(2,1)S(1)} %copy-done, bf16[4,272,256]{2,1,0:T(8,128)(2,1)S(1)} %get-tuple-element.72.refs_0_, bf16[4,272,256]{2,1,0:T(8,128)(2,1)S(1)} %collective-permute-done.26.refs_1_), custom_call_target="tpu_custom_call" | custom-call | flops 1073741824 | bytes 5242880 | tf_op jit(solution)/shard_map/projection_grad/pallas_call | solution.py:426
  110.5 1.2 collective-permute-done.25.refs_0_
  111.7 6.3 %collective-permute-done.30.refs_2_ = bf16[4,272,256]{2,1,0:T(8,128)(2,1)S(1)} collective-permute-done((bf16[4,272,256]{2,1,0:T(8,128)(2,1)S(1)}, bf16[4,272,256]{2,1,0:T(8,128)(2,1)S(1)}, u32[]{:S(2)}, u32[]{:S(2)}) %collective-permute-start.30) | collective-permute-done | bytes 557088 | tf_op jit(solution)/shard_map/ppermute | solution.py:547
  118.1 1.8 %collective-permute-start.31 = (bf16[4,272,256]{2,1,0:T(8,128)(2,1)S(1)}, bf16[4,272,256]{2,1,0:T(8,128)(2,1)S(1)}, u32[]{:S(2)}, u32[]{:S(2)}) collective-permute-start(bf16[4,272,256]{2,1,0:T(8,128)(2,1)S(1)} %collective-permute-done.30.refs_2_), channel_id=1, source_target_pairs={{0,1},{1,0},{2,3},{3,2},{4,5},{5,4},{6,7},{7,6},{8,9},{9,8},{10,11... | collective-permute-start | bytes 1671176 | tf_op jit(solution)/shard_map/ppermute | solution.py:41
  120.4 2.4 %projection_grad.4.refs_3_ = f32[2,256,1024]{2,1,0:T(8,128)S(1)} custom-call(s32[4]{0:T(128)S(1)} %pad_add_fusion.where, bf16[4096,1024]{1,0:T(8,128)(2,1)S(1)} %copy-done.1, bf16[4,272,256]{2,1,0:T(8,128)(2,1)S(1)} %collective-permute-done.25.refs_0_, bf16[4,272,256]{2,1,0:T(8,128)(2,1)S(1)} %collective-permute-done.28.refs_1_, ...), custom_call_target="tpu_custom_call" | custom-call | flops 1610612736 | bytes 7864320 | tf_op jit(solution)/shard_map/projection_grad/pallas_call | solution.py:426
  123.0 3.3 %projection_grad.5 = (bf16[512,1024]{1,0:T(8,128)(2,1)}, f32[1,1024]{1,0:T(1,128)}) custom-call(s32[4]{0:T(128)S(1)} %pad_add_fusion.where, bf16[4096,1024]{1,0:T(8,128)(2,1)S(1)} %copy-done.1, bf16[4,272,256]{2,1,0:T(8,128)(2,1)S(1)} %collective-permute-done.27.refs_0_, bf16[4,272,256]{2,1,0:T(8,128)(2,1)S(1)} %collective-permute-done.29.refs_1_, ...), custom_call_target="tpu_custom_call" | custom-call | flops 1610612736 | bytes 7864320 | tf_op jit(solution)/shard_map/projection_grad/pallas_call | solution.py:426
  (75 shorter events, 4.2 us)
Async XLA Ops:
  7.2 98.1 %all-gather.2.cloned.1.call-start = ((), (), s32[]{:S(2)}) async-start(), calls=%async_computation | async-start | bytes 8912896 | tf_op jit(solution)/shard_map/all_gather | solution.py:488
  8.0 1.0 copy-start.2
  9.1 11.9 %copy-start.7 = (f32[4]{0:T(128)S(1)}, f32[4]{0:T(128)}, u32[]{:S(2)}) copy-start(f32[4]{0:T(128)} %param.14) | copy-start | bytes 52
  9.1 11.9 %copy-start.9 = (s32[4]{0:T(128)S(1)}, s32[4]{0:T(128)}, u32[]{:S(2)}) copy-start(s32[4]{0:T(128)} %param.16) | copy-start | bytes 52
  9.1 11.9 %copy-start.10 = (s32[1,4]{1,0:T(1,128)S(1)}, s32[1,4]{1,0:T(1,128)}, u32[]{:S(2)}) copy-start(s32[1,4]{1,0:T(1,128)} %param.17) | copy-start | bytes 52
  15.1 3.0 %collective-permute-start = (bf16[256,1024]{1,0:T(8,128)(2,1)S(1)}, bf16[256,1024]{1,0:T(8,128)(2,1)S(1)}, u32[]{:S(2)}, u32[]{:S(2)}) collective-permute-start(bf16[256,1024]{1,0:T(8,128)(2,1)S(1)} %get-tuple-element.45), channel_id=1, source_target_pairs={{0,1},{1,0},{2,3},{3,2},{4,5},{5,4},{6,7},{7,6},{8,9},{9,8},{10,11... | collective-permute-start | bytes 1572872 | tf_op jit(solution)/shard_map/ppermute | solution.py:41
  16.6 5.0 %collective-permute-start.1 = (bf16[256,1024]{1,0:T(8,128)(2,1)S(1)}, bf16[256,1024]{1,0:T(8,128)(2,1)S(1)}, u32[]{:S(2)}, u32[]{:S(2)}) collective-permute-start(bf16[256,1024]{1,0:T(8,128)(2,1)S(1)} %get-tuple-element.49), channel_id=1, source_target_pairs={{0,1},{1,0},{2,3},{3,2},{4,5},{5,4},{6,7},{7,6},{8,9},{9,8},{10,11... | collective-permute-start | bytes 1572872 | tf_op jit(solution)/shard_map/ppermute | solution.py:41
  16.7 4.9 %collective-permute-start.2 = (bf16[256,1024]{1,0:T(8,128)(2,1)S(1)}, bf16[256,1024]{1,0:T(8,128)(2,1)S(1)}, u32[]{:S(2)}, u32[]{:S(2)}) collective-permute-start(bf16[256,1024]{1,0:T(8,128)(2,1)S(1)} %get-tuple-element.50), channel_id=1, source_target_pairs={{0,1},{1,0},{2,3},{3,2},{4,5},{5,4},{6,7},{7,6},{8,9},{9,8},{10,11... | collective-permute-start | bytes 1572872 | tf_op jit(solution)/shard_map/ppermute | solution.py:41
  18.2 9.6 %collective-permute-start.3 = (bf16[128,1024]{1,0:T(8,128)(2,1)S(1)}, bf16[128,1024]{1,0:T(8,128)(2,1)S(1)}, u32[]{:S(2)}, u32[]{:S(2)}) collective-permute-start(bf16[128,1024]{1,0:T(8,128)(2,1)S(1)} %get-tuple-element.46), channel_id=1, source_target_pairs={{0,2},{1,3},{2,4},{3,5},{4,6},{5,7},{6,0},{7,1},{8,10},{9,11},{10,... | collective-permute-start | bytes 786440 | tf_op jit(solution)/shard_map/ppermute | solution.py:494
  19.6 8.2 %collective-permute-start.4 = (bf16[128,1024]{1,0:T(8,128)(2,1)S(1)}, bf16[128,1024]{1,0:T(8,128)(2,1)S(1)}, u32[]{:S(2)}, u32[]{:S(2)}) collective-permute-start(bf16[128,1024]{1,0:T(8,128)(2,1)S(1)} %get-tuple-element.47), channel_id=1, source_target_pairs={{0,6},{1,7},{2,0},{3,1},{4,2},{5,3},{6,4},{7,5},{8,14},{9,15},{10,... | collective-permute-start | bytes 786440 | tf_op jit(solution)/shard_map/ppermute | solution.py:495
  21.6 9.9 %copy-start.8 = (s32[4]{0:T(128)S(1)}, s32[4]{0:T(128)}, u32[]{:S(2)}) copy-start(s32[4]{0:T(128)} %param.15) | copy-start | bytes 52
  21.6 10.2 %copy-start.6 = (bf16[1024]{0:T(1024)(128)(2,1)S(1)}, bf16[1024]{0:T(1024)(128)(2,1)}, u32[]{:S(2)}) copy-start(bf16[1024]{0:T(1024)(128)(2,1)} %param.12) | copy-start | bytes 6148
  21.6 18.5 %copy-start.3 = (bf16[256,1024]{1,0:T(8,128)(2,1)S(1)}, bf16[256,1024]{1,0:T(8,128)(2,1)}, u32[]{:S(2)}) copy-start(bf16[256,1024]{1,0:T(8,128)(2,1)} %att.5) | copy-start | bytes 1572868
  26.8 13.3 %collective-permute-start.5 = (bf16[256,1024]{1,0:T(8,128)(2,1)S(1)}, bf16[256,1024]{1,0:T(8,128)(2,1)S(1)}, u32[]{:S(2)}, u32[]{:S(2)}) collective-permute-start(bf16[256,1024]{1,0:T(8,128)(2,1)S(1)} %get-tuple-element.55), channel_id=1, source_target_pairs={{0,1},{1,0},{2,3},{3,2},{4,5},{5,4},{6,7},{7,6},{8,9},{9,8},{10,11... | collective-permute-start | bytes 1572872 | tf_op jit(solution)/shard_map/ppermute | solution.py:41
  28.7 14.4 %collective-permute-start.6 = (bf16[256,1024]{1,0:T(8,128)(2,1)}, bf16[256,1024]{1,0:T(8,128)(2,1)S(1)}, u32[]{:S(2)}, u32[]{:S(2)}) collective-permute-start(bf16[256,1024]{1,0:T(8,128)(2,1)} %get-tuple-element.56), channel_id=1, source_target_pairs={{0,2},{1,3},{2,4},{3,5},{4,6},{5,7},{6,0},{7,1},{8,10},{9,11},{10,... | collective-permute-start | bytes 1572872 | tf_op jit(solution)/shard_map/ppermute | solution.py:506
  28.9 14.3 %collective-permute-start.7 = (bf16[256,1024]{1,0:T(8,128)(2,1)S(1)}, bf16[256,1024]{1,0:T(8,128)(2,1)S(1)}, u32[]{:S(2)}, u32[]{:S(2)}) collective-permute-start(bf16[256,1024]{1,0:T(8,128)(2,1)S(1)} %get-tuple-element.53), channel_id=1, source_target_pairs={{0,6},{1,7},{2,0},{3,1},{4,2},{5,3},{6,4},{7,5},{8,14},{9,15},{10,... | collective-permute-start | bytes 1572872 | tf_op jit(solution)/shard_map/ppermute | solution.py:507
  32.8 10.4 %copy-start.4 = (bf16[256,1024]{1,0:T(8,128)(2,1)S(1)}, bf16[256,1024]{1,0:T(8,128)(2,1)}, u32[]{:S(2)}) copy-start(bf16[256,1024]{1,0:T(8,128)(2,1)} %cot.3) | copy-start | bytes 1572868
  32.8 10.4 %copy-start.5 = (bf16[256,1024]{1,0:T(8,128)(2,1)S(1)}, bf16[256,1024]{1,0:T(8,128)(2,1)}, u32[]{:S(2)}) copy-start(bf16[256,1024]{1,0:T(8,128)(2,1)} %residual) | copy-start | bytes 1572868
  32.8 10.3 %collective-permute-start.8 = (f32[1,128]{1,0:T(1,128)S(1)}, f32[1,128]{1,0:T(1,128)S(1)}, u32[]{:S(2)}, u32[]{:S(2)}) collective-permute-start(f32[1,128]{1,0:T(1,128)S(1)} %bitcast.28), channel_id=1, source_target_pairs={{0,0},{1,17},{2,34},{3,51},{4,68},{5,85},{6,102},{7,119},{8,8},{9,... | collective-permute-start | bytes 1544 | tf_op jit(solution)/shard_map/ppermute | solution.py:512
  37.9 5.2 %collective-permute-start.9 = (f32[1,128]{1,0:T(1,128)S(1)}, f32[1,128]{1,0:T(1,128)S(1)}, u32[]{:S(2)}, u32[]{:S(2)}) collective-permute-start(f32[1,128]{1,0:T(1,128)S(1)} %bitcast.29), channel_id=1, source_target_pairs={{0,8},{1,25},{2,42},{3,59},{4,76},{5,93},{6,110},{7,127},{8,16},{9... | collective-permute-start | bytes 1544 | tf_op jit(solution)/shard_map/ppermute | solution.py:512
  43.8 2.2 %collective-permute-start.10 = (f32[8,256]{1,0:T(8,128)S(1)}, f32[8,256]{1,0:T(8,128)S(1)}, u32[]{:S(2)}, u32[]{:S(2)}) collective-permute-start(f32[8,256]{1,0:T(8,128)S(1)} %get-tuple-element.61), channel_id=1, source_target_pairs={{0,1},{1,0},{2,3},{3,2},{4,5},{5,4},{6,7},{7,6},{8,9},{9,8},{10,11... | collective-permute-start | bytes 24584 | tf_op jit(solution)/shard_map/ppermute | solution.py:41
  46.0 4.3 %collective-permute-start.11 = (f32[8,256]{1,0:T(8,128)S(1)}, f32[8,256]{1,0:T(8,128)S(1)}, u32[]{:S(2)}, u32[]{:S(2)}) collective-permute-start(f32[8,256]{1,0:T(8,128)S(1)} %add.23.s0), channel_id=1, source_target_pairs={{0,2},{1,3},{2,4},{3,5},{4,6},{5,7},{6,0},{7,1},{8,10},{9,11},{10,... | collective-permute-start | bytes 24584 | tf_op jit(solution)/shard_map/ppermute | solution.py:522
  47.0 4.1 %collective-permute-start.12 = (f32[8,256]{1,0:T(8,128)S(1)}, f32[8,256]{1,0:T(8,128)S(1)}, u32[]{:S(2)}, u32[]{:S(2)}) collective-permute-start(f32[8,256]{1,0:T(8,128)S(1)} %add.23.s0), channel_id=1, source_target_pairs={{0,4},{1,5},{2,6},{3,7},{4,0},{5,1},{6,2},{7,3},{8,12},{9,13},{10,... | collective-permute-start | bytes 24584 | tf_op jit(solution)/shard_map/ppermute | solution.py:522
  49.6 2.9 %collective-permute-start.13 = (f32[8,256]{1,0:T(8,128)S(1)}, f32[8,256]{1,0:T(8,128)S(1)}, u32[]{:S(2)}, u32[]{:S(2)}) collective-permute-start(f32[8,256]{1,0:T(8,128)S(1)} %add.23.s0), channel_id=1, source_target_pairs={{0,6},{1,7},{2,0},{3,1},{4,2},{5,3},{6,4},{7,5},{8,14},{9,15},{10,... | collective-permute-start | bytes 24584 | tf_op jit(solution)/shard_map/ppermute | solution.py:522
  54.0 13.1 %collective-permute-start.15 = (bf16[256,1024]{1,0:T(8,128)(2,1)S(1)}, bf16[256,1024]{1,0:T(8,128)(2,1)S(1)}, u32[]{:S(2)}, u32[]{:S(2)}) collective-permute-start(bf16[256,1024]{1,0:T(8,128)(2,1)S(1)} %get-tuple-element.63.refs_0_), channel_id=1, source_target_pairs={{0,2},{1,3},{2,4},{3,5},{4,6},{5,7},{6,0},{7,1},{8,10},{9,11},{10,... | collective-permute-start | bytes 1572872 | tf_op jit(solution)/shard_map/ppermute | solution.py:528
  54.0 13.2 %collective-permute-start.18 = (bf16[256,1024]{1,0:T(8,128)(2,1)S(1)}, bf16[256,1024]{1,0:T(8,128)(2,1)S(1)}, u32[]{:S(2)}, u32[]{:S(2)}) collective-permute-start(bf16[256,1024]{1,0:T(8,128)(2,1)S(1)} %get-tuple-element.63.refs_0_), channel_id=1, source_target_pairs={{0,6},{1,7},{2,0},{3,1},{4,2},{5,3},{6,4},{7,5},{8,14},{9,15},{10,... | collective-permute-start | bytes 1572872 | tf_op jit(solution)/shard_map/ppermute | solution.py:528
  67.1 6.9 %collective-permute-start.17 = (bf16[128,1024]{1,0:T(8,128)(2,1)S(1)}, bf16[128,1024]{1,0:T(8,128)(2,1)S(1)}, u32[]{:S(2)}, u32[]{:S(2)}) collective-permute-start(bf16[128,1024]{1,0:T(8,128)(2,1)S(1)} %slice.40), channel_id=1, source_target_pairs={{0,2},{1,3},{2,4},{3,5},{4,6},{5,7},{6,0},{7,1},{8,10},{9,11},{10,... | collective-permute-start | bytes 786440 | tf_op jit(solution)/shard_map/ppermute | solution.py:529
  67.2 6.8 %collective-permute-start.19 = (bf16[128,1024]{1,0:T(8,128)(2,1)S(1)}, bf16[128,1024]{1,0:T(8,128)(2,1)S(1)}, u32[]{:S(2)}, u32[]{:S(2)}) collective-permute-start(bf16[128,1024]{1,0:T(8,128)(2,1)S(1)} %slice.41), channel_id=1, source_target_pairs={{0,6},{1,7},{2,0},{3,1},{4,2},{5,3},{6,4},{7,5},{8,14},{9,15},{10,... | collective-permute-start | bytes 786440 | tf_op jit(solution)/shard_map/ppermute | solution.py:530
  69.9 7.4 %collective-permute-start.14 = (bf16[256,1024]{1,0:T(8,128)(2,1)S(1)}, bf16[256,1024]{1,0:T(8,128)(2,1)S(1)}, u32[]{:S(2)}, u32[]{:S(2)}) collective-permute-start(bf16[256,1024]{1,0:T(8,128)(2,1)S(1)} %get-tuple-element.63.refs_0_), channel_id=1, source_target_pairs={{0,1},{1,0},{2,3},{3,2},{4,5},{5,4},{6,7},{7,6},{8,9},{9,8},{10,11... | collective-permute-start | bytes 1572872 | tf_op jit(solution)/shard_map/ppermute | solution.py:41
  73.0 4.4 %collective-permute-start.16 = (bf16[256,1024]{1,0:T(8,128)(2,1)S(1)}, bf16[256,1024]{1,0:T(8,128)(2,1)S(1)}, u32[]{:S(2)}, u32[]{:S(2)}) collective-permute-start(bf16[256,1024]{1,0:T(8,128)(2,1)S(1)} %collective-permute-done.15.refs_2_), channel_id=1, source_target_pairs={{0,1},{1,0},{2,3},{3,2},{4,5},{5,4},{6,7},{7,6},{8,9},{9,8},{10,11... | collective-permute-start | bytes 1572872 | tf_op jit(solution)/shard_map/ppermute | solution.py:41
  73.0 4.4 %collective-permute-start.21 = (bf16[256,1024]{1,0:T(8,128)(2,1)S(1)}, bf16[256,1024]{1,0:T(8,128)(2,1)S(1)}, u32[]{:S(2)}, u32[]{:S(2)}) collective-permute-start(bf16[256,1024]{1,0:T(8,128)(2,1)S(1)} %collective-permute-done.18.refs_6_), channel_id=1, source_target_pairs={{0,1},{1,0},{2,3},{3,2},{4,5},{5,4},{6,7},{7,6},{8,9},{9,8},{10,11... | collective-permute-start | bytes 1572872 | tf_op jit(solution)/shard_map/ppermute | solution.py:41
  74.1 4.8 %collective-permute-start.20 = (bf16[256,1024]{1,0:T(8,128)(2,1)S(1)}, bf16[256,1024]{1,0:T(8,128)(2,1)S(1)}, u32[]{:S(2)}, u32[]{:S(2)}) collective-permute-start(bf16[256,1024]{1,0:T(8,128)(2,1)S(1)} %joined.1.refs_4_), channel_id=1, source_target_pairs={{0,1},{1,0},{2,3},{3,2},{4,5},{5,4},{6,7},{7,6},{8,9},{9,8},{10,11... | collective-permute-start | bytes 1572872 | tf_op jit(solution)/shard_map/ppermute | solution.py:41
  80.4 13.1 %collective-permute-start.22 = (bf16[4,272,256]{2,1,0:T(8,128)(2,1)S(1)}, bf16[4,272,256]{2,1,0:T(8,128)(2,1)S(1)}, u32[]{:S(2)}, u32[]{:S(2)}) collective-permute-start(bf16[4,272,256]{2,1,0:T(8,128)(2,1)S(1)} %get-tuple-element.66), channel_id=1, source_target_pairs={{0,32},{1,9},{2,34},{3,11},{4,36},{5,13},{6,38},{7,15},{8,40},{9,1... | collective-permute-start | bytes 1671176 | tf_op jit(solution)/shard_map/ppermute | solution.py:539
  81.9 15.8 %collective-permute-start.23 = (bf16[4,272,256]{2,1,0:T(8,128)(2,1)S(1)}, bf16[4,272,256]{2,1,0:T(8,128)(2,1)S(1)}, u32[]{:S(2)}, u32[]{:S(2)}) collective-permute-start(bf16[4,272,256]{2,1,0:T(8,128)(2,1)S(1)} %get-tuple-element.67), channel_id=1, source_target_pairs={{0,64},{1,17},{2,66},{3,19},{4,68},{5,21},{6,70},{7,23},{8,72},{9,... | collective-permute-start | bytes 1671176 | tf_op jit(solution)/shard_map/ppermute | solution.py:539
  84.5 13.2 %collective-permute-start.24 = (bf16[4,272,256]{2,1,0:T(8,128)(2,1)S(1)}, bf16[4,272,256]{2,1,0:T(8,128)(2,1)S(1)}, u32[]{:S(2)}, u32[]{:S(2)}) collective-permute-start(bf16[4,272,256]{2,1,0:T(8,128)(2,1)S(1)} %get-tuple-element.68), channel_id=1, source_target_pairs={{0,96},{1,25},{2,98},{3,27},{4,100},{5,29},{6,102},{7,31},{8,104},... | collective-permute-start | bytes 1671176 | tf_op jit(solution)/shard_map/ppermute | solution.py:539
  99.4 5.9 %collective-permute-start.26 = (bf16[4,272,256]{2,1,0:T(8,128)(2,1)S(1)}, bf16[4,272,256]{2,1,0:T(8,128)(2,1)S(1)}, u32[]{:S(2)}, u32[]{:S(2)}) collective-permute-start(bf16[4,272,256]{2,1,0:T(8,128)(2,1)S(1)} %get-tuple-element.72.refs_0_), channel_id=1, source_target_pairs={{0,1},{1,0},{2,3},{3,2},{4,5},{5,4},{6,7},{7,6},{8,9},{9,8},{10,11... | collective-permute-start | bytes 1671176 | tf_op jit(solution)/shard_map/ppermute | solution.py:41
  101.6 10.1 %collective-permute-start.25 = (bf16[4,272,256]{2,1,0:T(8,128)(2,1)}, bf16[4,272,256]{2,1,0:T(8,128)(2,1)S(1)}, u32[]{:S(2)}, u32[]{:S(2)}) collective-permute-start(bf16[4,272,256]{2,1,0:T(8,128)(2,1)} %get-tuple-element.71), channel_id=1, source_target_pairs={{0,8},{1,33},{2,10},{3,35},{4,12},{5,37},{6,14},{7,39},{8,16},{9,4... | collective-permute-start | bytes 1671176 | tf_op jit(solution)/shard_map/ppermute | solution.py:547
  102.8 8.9 %collective-permute-start.28 = (bf16[4,272,256]{2,1,0:T(8,128)(2,1)}, bf16[4,272,256]{2,1,0:T(8,128)(2,1)S(1)}, u32[]{:S(2)}, u32[]{:S(2)}) collective-permute-start(bf16[4,272,256]{2,1,0:T(8,128)(2,1)} %get-tuple-element.74), channel_id=1, source_target_pairs={{0,24},{1,97},{2,26},{3,99},{4,28},{5,101},{6,30},{7,103},{8,0},{9... | collective-permute-start | bytes 1671176 | tf_op jit(solution)/shard_map/ppermute | solution.py:547
  104.3 13.8 %collective-permute-start.30 = (bf16[4,272,256]{2,1,0:T(8,128)(2,1)S(1)}, bf16[4,272,256]{2,1,0:T(8,128)(2,1)S(1)}, u32[]{:S(2)}, u32[]{:S(2)}) collective-permute-start(bf16[4,272,256]{2,1,0:T(8,128)(2,1)S(1)} %get-tuple-element.77), channel_id=1, source_target_pairs={{0,16},{1,65},{2,18},{3,67},{4,20},{5,69},{6,22},{7,71},{8,24},{9,... | collective-permute-start | bytes 1671176 | tf_op jit(solution)/shard_map/ppermute | solution.py:547
  105.3 3.4 %copy-start = (bf16[4096,1024]{1,0:T(8,128)(2,1)S(1)}, bf16[4096,1024]{1,0:T(8,128)(2,1)}, u32[]{:S(2)}) copy-start(bf16[4096,1024]{1,0:T(8,128)(2,1)} %all-gather.2.cloned.1.call-done.gathered) | copy-start | bytes 25165828
  108.7 11.7 %copy-start.1 = (bf16[4096,1024]{1,0:T(8,128)(2,1)S(1)}, bf16[4096,1024]{1,0:T(8,128)(2,1)}, u32[]{:S(2)}) copy-start(bf16[4096,1024]{1,0:T(8,128)(2,1)} %all-gather.2.cloned.1.call-done.gathered) | copy-start | bytes 25165828
  118.1 4.7 %collective-permute-start.31 = (bf16[4,272,256]{2,1,0:T(8,128)(2,1)S(1)}, bf16[4,272,256]{2,1,0:T(8,128)(2,1)S(1)}, u32[]{:S(2)}, u32[]{:S(2)}) collective-permute-start(bf16[4,272,256]{2,1,0:T(8,128)(2,1)S(1)} %collective-permute-done.30.refs_2_), channel_id=1, source_target_pairs={{0,1},{1,0},{2,3},{3,2},{4,5},{5,4},{6,7},{7,6},{8,9},{9,8},{10,11... | collective-permute-start | bytes 1671176 | tf_op jit(solution)/shard_map/ppermute | solution.py:41
  119.8 3.0 %collective-permute-start.29 = (bf16[4,272,256]{2,1,0:T(8,128)(2,1)S(1)}, bf16[4,272,256]{2,1,0:T(8,128)(2,1)S(1)}, u32[]{:S(2)}, u32[]{:S(2)}) collective-permute-start(bf16[4,272,256]{2,1,0:T(8,128)(2,1)S(1)} %collective-permute-done.28.refs_1_), channel_id=1, source_target_pairs={{0,1},{1,0},{2,3},{3,2},{4,5},{5,4},{6,7},{7,6},{8,9},{9,8},{10,11... | collective-permute-start | bytes 1671176 | tf_op jit(solution)/shard_map/ppermute | solution.py:41
  119.8 3.2 %collective-permute-start.27 = (bf16[4,272,256]{2,1,0:T(8,128)(2,1)S(1)}, bf16[4,272,256]{2,1,0:T(8,128)(2,1)S(1)}, u32[]{:S(2)}, u32[]{:S(2)}) collective-permute-start(bf16[4,272,256]{2,1,0:T(8,128)(2,1)S(1)} %collective-permute-done.25.refs_0_), channel_id=1, source_target_pairs={{0,1},{1,0},{2,3},{3,2},{4,5},{5,4},{6,7},{7,6},{8,9},{9,8},{10,11... | collective-permute-start | bytes 1671176 | tf_op jit(solution)/shard_map/ppermute | solution.py:41
Sparse Core Ops, SparseCore 0:
  10.1 74.1 all-gather.1

commit v5 on v4

--- a/solution.py
+++ b/solution.py
@@ -547,14 +547,17 @@
         mine[k] = lax.ppermute(sends[k], ("dp", "tensor"), plane_shift(1, k))
     theirs = [swap(mine[0]), None, None, None]
     total = projection_call(where, mine, theirs, gathered, ((0,), (0,)), None)
-    for k in (1, 3, 2):
+    for k in (1, 3):
         mine[k], total = lax.optimization_barrier((mine[k], total))
         theirs[k] = swap(mine[k])
-    total = projection_call(where, mine, theirs, gathered, ((1, 3, 2), ()), total)
+    total = projection_call(where, mine, theirs, gathered, ((1, 3), ()), total)
+    mine[2], total = lax.optimization_barrier((mine[2], total))
+    theirs[2] = swap(mine[2])
     tails = sum(part[:, rows:, :].astype(F32) for part in mine.values())
     tails = jnp.concatenate([tails[j] for j in range(4)], axis=1)
+    total = projection_call(where, mine, theirs, gathered, ((2,), (1, 3)), total)
     grad_out_proj, grad_gain = projection_call(
-        where, mine, theirs, gathered, ((), (1, 3, 2)), total, tails
+        where, mine, theirs, gathered, ((), (2,)), total, tails
     )
     return (grad_attention, grad_out_proj, grad_residual, grad_gain[0])
 

time: 133 us -> 133 us (level); the launches traced: 133 us -> 131 us
  waiting for transfers between devices: 29.2 us -> 25.9 us
    ppermute x3, waiting for transfers between devices: 7.57 us -> 4.46 us  [shards(): mine[k] = lax.ppermute(sends[k], ('dp', 'tensor'), plane_shift(1, k))]
    pallas_call x3 -> x4, Pallas kernels: 7.51 us -> 8.23 us  [projection_call(): pl.pallas_call(functools.partial(projection_kernel, members, first, last)...]
  transfers between devices with their start and end apart: 33 -> 33, of which waited for: 12 -> 11; matrix products, arithmetic and copies ran while one was open for 2% -> 2% of each run, Pallas kernels for 25% -> 26%
where the time goes in v5:
time: 133 us; the launch traced here: 131 us
  starting transfers between devices  47.8 us (36%)
  Pallas kernels  36.8 us (28%)
  waiting for transfers between devices  25.9 us (19%)
  between operations  14.3 us (11%)
  local copies, waits for them, and re-layouts  5.32 us (4%)
    ppermute x13, starting transfers between devices, swap(): return lax.ppermute(value, 'tensor', CORE_SWAP)  16.5 us
    pallas_call x3, Pallas kernels, partial_products(): pl.pallas_call(functools.partial(partial_kernel, jobs), in_specs=[pl.Bloc...  14.2 us
    ppermute x2, waiting for transfers between devices, shards(): near = {k: lax.ppermute(own_piece, 'tensor', x_shift(k)) for k in (1, 3)}  10.4 us
    pallas_call x4, Pallas kernels, projection_call(): pl.pallas_call(functools.partial(projection_kernel, members, first, last)...  8.23 us
    pallas_call x1, Pallas kernels, attention_call(): pl.pallas_call(attention_kernel, in_specs=[pl.BlockSpec(memory_space=pltp...  7.98 us
    ppermute x2, starting transfers between devices, shards(): lax.ppermute(stats, ('dp', 'tensor'), scattered(step))  7.2 us
    ppermute x3, starting transfers between devices, shards(): parts[k] = lax.ppermute(sends[k], ('dp', 'tensor'), plane_shift(0, k))  5.15 us
    unnamed x22, local copies, waits for them, and re-layouts  4.47 us
  transfers between devices with their start and end apart: 33, of which 11 were waited for; matrix products, arithmetic and copies ran while one was open for 2% of the time, Pallas kernels for 26%

profile of v5, /device:TPU:1, one launch (start us, length us, event | category | flops | bytes accessed | tf_op | source)
XLA Modules:
  0.0 131.4 jit_solution(16971066275800442928)
XLA Ops:
  7.2 0.7 all-gather.2.cloned.1.call-update
  8.0 1.0 copy-done.2
  9.1 6.0 %partial.3 = (bf16[256,1024]{1,0:T(8,128)(2,1)S(1)}, f32[256,1024]{1,0:T(8,128)S(1)}, bf16[256,1024]{1,0:T(8,128)(2,1)S(1)}, bf16[256,1024]{1,0:T(8,128)(2,1)S(1)}) custom-call(s32[4]{0:T(128)S(1)} %pad_add_fusion.where, bf16[256,1024]{1,0:T(8,128)(2,1)S(1)} %copy-done.2, bf16[8192,1024]{1,0:T(8,128)(2,1)} %refs_8_.1), custom_call_target="tpu_custom_call" | custom-call | flops 2147483648 | bytes 8388608 | tf_op jit(solution)/shard_map/partial/pallas_call | solution.py:89
  15.1 1.5 %collective-permute-start = (bf16[256,1024]{1,0:T(8,128)(2,1)S(1)}, bf16[256,1024]{1,0:T(8,128)(2,1)S(1)}, u32[]{:S(2)}, u32[]{:S(2)}) collective-permute-start(bf16[256,1024]{1,0:T(8,128)(2,1)S(1)} %get-tuple-element.45), channel_id=1, source_target_pairs={{0,1},{1,0},{2,3},{3,2},{4,5},{5,4},{6,7},{7,6},{8,9},{9,8},{10,11... | collective-permute-start | bytes 1572872 | tf_op jit(solution)/shard_map/ppermute | solution.py:41
  17.1 1.0 collective-permute-done.second
  18.2 1.4 %collective-permute-start.3 = (bf16[128,1024]{1,0:T(8,128)(2,1)S(1)}, bf16[128,1024]{1,0:T(8,128)(2,1)S(1)}, u32[]{:S(2)}, u32[]{:S(2)}) collective-permute-start(bf16[128,1024]{1,0:T(8,128)(2,1)S(1)} %get-tuple-element.46), channel_id=1, source_target_pairs={{0,2},{1,3},{2,4},{3,5},{4,6},{5,7},{6,0},{7,1},{8,10},{9,11},{10,... | collective-permute-start | bytes 786440 | tf_op jit(solution)/shard_map/ppermute | solution.py:494
  19.6 1.4 %collective-permute-start.4 = (bf16[128,1024]{1,0:T(8,128)(2,1)S(1)}, bf16[128,1024]{1,0:T(8,128)(2,1)S(1)}, u32[]{:S(2)}, u32[]{:S(2)}) collective-permute-start(bf16[128,1024]{1,0:T(8,128)(2,1)S(1)} %get-tuple-element.47), channel_id=1, source_target_pairs={{0,6},{1,7},{2,0},{3,1},{4,2},{5,3},{6,4},{7,5},{8,14},{9,15},{10,... | collective-permute-start | bytes 786440 | tf_op jit(solution)/shard_map/ppermute | solution.py:495
  21.6 5.2 %partial.4 = (f32[256,1024]{1,0:T(8,128)S(1)}, f32[256,1024]{1,0:T(8,128)S(1)}, bf16[256,1024]{1,0:T(8,128)(2,1)S(1)}) custom-call(s32[4]{0:T(128)S(1)} %pad_add_fusion.where, bf16[256,1024]{1,0:T(8,128)(2,1)S(1)} %copy-done.2, bf16[8192,1024]{1,0:T(8,128)(2,1)} %refs_8_.1, bf16[256,1024]{1,0:T(8,128)(2,1)S(1)} %collective-permute-done.1.refs_0_, ...), custom_call_target="tpu_custom_call" | custom-call | flops 1610612736 | bytes 6291456 | tf_op jit(solution)/shard_map/partial/pallas_call | solution.py:89
  26.8 1.0 collective-permute-start.5
  27.8 0.9 passed.1
  28.9 2.5 %collective-permute-start.7 = (bf16[256,1024]{1,0:T(8,128)(2,1)S(1)}, bf16[256,1024]{1,0:T(8,128)(2,1)S(1)}, u32[]{:S(2)}, u32[]{:S(2)}) collective-permute-start(bf16[256,1024]{1,0:T(8,128)(2,1)S(1)} %get-tuple-element.53), channel_id=1, source_target_pairs={{0,6},{1,7},{2,0},{3,1},{4,2},{5,3},{6,4},{7,5},{8,14},{9,15},{10,... | collective-permute-start | bytes 1572872 | tf_op jit(solution)/shard_map/ppermute | solution.py:507
  31.9 0.7 concatenate.9
  32.8 5.0 %collective-permute-start.8 = (f32[1,128]{1,0:T(1,128)S(1)}, f32[1,128]{1,0:T(1,128)S(1)}, u32[]{:S(2)}, u32[]{:S(2)}) collective-permute-start(f32[1,128]{1,0:T(1,128)S(1)} %bitcast.28), channel_id=1, source_target_pairs={{0,0},{1,17},{2,34},{3,51},{4,68},{5,85},{6,102},{7,119},{8,8},{9,... | collective-permute-start | bytes 1544 | tf_op jit(solution)/shard_map/ppermute | solution.py:512
  37.9 2.2 %collective-permute-start.9 = (f32[1,128]{1,0:T(1,128)S(1)}, f32[1,128]{1,0:T(1,128)S(1)}, u32[]{:S(2)}, u32[]{:S(2)}) collective-permute-start(f32[1,128]{1,0:T(1,128)S(1)} %bitcast.29), channel_id=1, source_target_pairs={{0,8},{1,25},{2,42},{3,59},{4,76},{5,93},{6,110},{7,127},{8,16},{9... | collective-permute-start | bytes 1544 | tf_op jit(solution)/shard_map/ppermute | solution.py:512
  40.1 3.1 %partial.5.own = f32[256,1024]{1,0:T(8,128)S(1)} custom-call(s32[4]{0:T(128)S(1)} %pad_add_fusion.where, bf16[256,1024]{1,0:T(8,128)(2,1)S(1)} %copy-done.3, bf16[8192,1024]{1,0:T(8,128)(2,1)} %refs_8_.1, bf16[256,1024]{1,0:T(8,128)(2,1)S(1)} %collective-permute-done.5.refs_0_), custom_call_target="tpu_custom_call" | custom-call | flops 536870912 | bytes 2097152 | tf_op jit(solution)/shard_map/partial/pallas_call | solution.py:89
  43.8 1.4 %collective-permute-start.10 = (f32[8,256]{1,0:T(8,128)S(1)}, f32[8,256]{1,0:T(8,128)S(1)}, u32[]{:S(2)}, u32[]{:S(2)}) collective-permute-start(f32[8,256]{1,0:T(8,128)S(1)} %get-tuple-element.61), channel_id=1, source_target_pairs={{0,1},{1,0},{2,3},{3,2},{4,5},{5,4},{6,7},{7,6},{8,9},{9,8},{10,11... | collective-permute-start | bytes 24584 | tf_op jit(solution)/shard_map/ppermute | solution.py:41
  45.2 0.8 collective-permute-done.10
  46.0 0.9 collective-permute-start.11
  47.0 2.7 %collective-permute-start.12 = (f32[8,256]{1,0:T(8,128)S(1)}, f32[8,256]{1,0:T(8,128)S(1)}, u32[]{:S(2)}, u32[]{:S(2)}) collective-permute-start(f32[8,256]{1,0:T(8,128)S(1)} %add.23.s0), channel_id=1, source_target_pairs={{0,4},{1,5},{2,6},{3,7},{4,0},{5,1},{6,2},{7,3},{8,12},{9,13},{10,... | collective-permute-start | bytes 24584 | tf_op jit(solution)/shard_map/ppermute | solution.py:522
  50.3 0.7 collective-permute-done.12.s2
  51.0 1.6 %collective-permute-done.13.s3 = f32[8,256]{1,0:T(8,128)S(1)} collective-permute-done((f32[8,256]{1,0:T(8,128)S(1)}, f32[8,256]{1,0:T(8,128)S(1)}, u32[]{:S(2)}, u32[]{:S(2)}) %collective-permute-start.13) | collective-permute-done | bytes 8224 | tf_op jit(solution)/shard_map/ppermute | solution.py:522
  52.6 1.5 %grad.1 = (bf16[256,1024]{1,0:T(8,128)(2,1)}, bf16[256,1024]{1,0:T(8,128)(2,1)S(1)}, f32[1,1024]{1,0:T(1,128)S(1)}) custom-call(f32[256,1024]{1,0:T(8,128)S(1)} %get-tuple-element.60.hidden, bf16[256,1024]{1,0:T(8,128)(2,1)S(1)} %copy-done.4, bf16[1,1024]{1,0:T(2,128)(2,1)S(1)} %broadcast_in_dim.43.gain, f32[8,256]{1,0:T(8,128)S(1)} %add.23.s0, ...), custom_call_target="tpu_custom_call" | custom-call | flops 3145728 | bytes 2097152 | tf_op jit(solution)/shard_map/grad/pallas_call | solution.py:259
  54.0 2.7 %collective-permute-start.18 = (bf16[256,1024]{1,0:T(8,128)(2,1)S(1)}, bf16[256,1024]{1,0:T(8,128)(2,1)S(1)}, u32[]{:S(2)}, u32[]{:S(2)}) collective-permute-start(bf16[256,1024]{1,0:T(8,128)(2,1)S(1)} %get-tuple-element.63.refs_0_), channel_id=1, source_target_pairs={{0,6},{1,7},{2,0},{3,1},{4,2},{5,3},{6,4},{7,5},{8,14},{9,15},{10,... | collective-permute-start | bytes 1572872 | tf_op jit(solution)/shard_map/ppermute | solution.py:528
  56.7 10.4 %collective-permute-done.15.refs_2_ = bf16[256,1024]{1,0:T(8,128)(2,1)S(1)} collective-permute-done((bf16[256,1024]{1,0:T(8,128)(2,1)S(1)}, bf16[256,1024]{1,0:T(8,128)(2,1)S(1)}, u32[]{:S(2)}, u32[]{:S(2)}) %collective-permute-start.15) | collective-permute-done | bytes 524320 | tf_op jit(solution)/shard_map/ppermute | solution.py:528
  67.2 2.7 %collective-permute-start.19 = (bf16[128,1024]{1,0:T(8,128)(2,1)S(1)}, bf16[128,1024]{1,0:T(8,128)(2,1)S(1)}, u32[]{:S(2)}, u32[]{:S(2)}) collective-permute-start(bf16[128,1024]{1,0:T(8,128)(2,1)S(1)} %slice.41), channel_id=1, source_target_pairs={{0,6},{1,7},{2,0},{3,1},{4,2},{5,3},{6,4},{7,5},{8,14},{9,15},{10,... | collective-permute-start | bytes 786440 | tf_op jit(solution)/shard_map/ppermute | solution.py:530
  70.0 3.0 %collective-permute-start.14 = (bf16[256,1024]{1,0:T(8,128)(2,1)S(1)}, bf16[256,1024]{1,0:T(8,128)(2,1)S(1)}, u32[]{:S(2)}, u32[]{:S(2)}) collective-permute-start(bf16[256,1024]{1,0:T(8,128)(2,1)S(1)} %get-tuple-element.63.refs_0_), channel_id=1, source_target_pairs={{0,1},{1,0},{2,3},{3,2},{4,5},{5,4},{6,7},{7,6},{8,9},{9,8},{10,11... | collective-permute-start | bytes 1572872 | tf_op jit(solution)/shard_map/ppermute | solution.py:41
  74.1 3.3 %collective-permute-start.20 = (bf16[256,1024]{1,0:T(8,128)(2,1)S(1)}, bf16[256,1024]{1,0:T(8,128)(2,1)S(1)}, u32[]{:S(2)}, u32[]{:S(2)}) collective-permute-start(bf16[256,1024]{1,0:T(8,128)(2,1)S(1)} %joined.1.refs_4_), channel_id=1, source_target_pairs={{0,1},{1,0},{2,3},{3,2},{4,5},{5,4},{6,7},{7,6},{8,9},{9,8},{10,11... | collective-permute-start | bytes 1572872 | tf_op jit(solution)/shard_map/ppermute | solution.py:41
  77.4 1.5 %collective-permute-done.20.refs_5_ = bf16[256,1024]{1,0:T(8,128)(2,1)S(1)} collective-permute-done((bf16[256,1024]{1,0:T(8,128)(2,1)S(1)}, bf16[256,1024]{1,0:T(8,128)(2,1)S(1)}, u32[]{:S(2)}, u32[]{:S(2)}) %collective-permute-start.20) | collective-permute-done | bytes 524320 | tf_op jit(solution)/shard_map/ppermute | solution.py:41
  78.9 1.5 %first_pack.1 = (bf16[4,272,256]{2,1,0:T(8,128)(2,1)S(1)}, bf16[4,272,256]{2,1,0:T(8,128)(2,1)S(1)}, bf16[4,272,256]{2,1,0:T(8,128)(2,1)S(1)}, bf16[4,272,256]{2,1,0:T(8,128)(2,1)S(1)}) custom-call(s32[4]{0:T(128)S(1)} %pad_add_fusion.where, bf16[256,1024]{1,0:T(8,128)(2,1)S(1)} %get-tuple-element.63.refs_0_, ...), custom_call_target="tpu_custom_call" | custom-call | bytes 4194304 | tf_op jit(solution)/shard_map/first_pack/pallas_call | solution.py:369
  80.4 1.5 %collective-permute-start.22 = (bf16[4,272,256]{2,1,0:T(8,128)(2,1)S(1)}, bf16[4,272,256]{2,1,0:T(8,128)(2,1)S(1)}, u32[]{:S(2)}, u32[]{:S(2)}) collective-permute-start(bf16[4,272,256]{2,1,0:T(8,128)(2,1)S(1)} %get-tuple-element.66), channel_id=1, source_target_pairs={{0,32},{1,9},{2,34},{3,11},{4,36},{5,13},{6,38},{7,15},{8,40},{9,1... | collective-permute-start | bytes 1671176 | tf_op jit(solution)/shard_map/ppermute | solution.py:539
  81.9 2.6 %collective-permute-start.23 = (bf16[4,272,256]{2,1,0:T(8,128)(2,1)S(1)}, bf16[4,272,256]{2,1,0:T(8,128)(2,1)S(1)}, u32[]{:S(2)}, u32[]{:S(2)}) collective-permute-start(bf16[4,272,256]{2,1,0:T(8,128)(2,1)S(1)} %get-tuple-element.67), channel_id=1, source_target_pairs={{0,64},{1,17},{2,66},{3,19},{4,68},{5,21},{6,70},{7,23},{8,72},{9,... | collective-permute-start | bytes 1671176 | tf_op jit(solution)/shard_map/ppermute | solution.py:539
  84.5 1.1 collective-permute-start.24
  85.6 8.0 %attention_grad.1 = bf16[256,1024]{1,0:T(8,128)(2,1)} custom-call(s32[4]{0:T(128)S(1)} %pad_add_fusion.where, bf16[256,1024]{1,0:T(8,128)(2,1)S(1)} %get-tuple-element.63.refs_0_, bf16[256,1024]{1,0:T(8,128)(2,1)S(1)} %collective-permute-done.14.refs_1_, bf16[256,1024]{1,0:T(8,128)(2,1)S(1)} %collective-permute-done.15.refs_2_, ...), custom_call_target="tpu_custom_call" | custom-call | flops 4294967296 | bytes 16777216 | tf_op jit(solution)/shard_map/attention_grad/pallas_call | solution.py:302
  93.6 4.1 %collective-permute-done.23.refs_2_ = bf16[4,272,256]{2,1,0:T(8,128)(2,1)S(1)} collective-permute-done((bf16[4,272,256]{2,1,0:T(8,128)(2,1)S(1)}, bf16[4,272,256]{2,1,0:T(8,128)(2,1)S(1)}, u32[]{:S(2)}, u32[]{:S(2)}) %collective-permute-start.23) | collective-permute-done | bytes 557088 | tf_op jit(solution)/shard_map/ppermute | solution.py:539
  97.7 1.8 %second_pack.1 = (bf16[4,272,256]{2,1,0:T(8,128)(2,1)S(1)}, bf16[4,272,256]{2,1,0:T(8,128)(2,1)}, bf16[4,272,256]{2,1,0:T(8,128)(2,1)S(1)}, bf16[4,272,256]{2,1,0:T(8,128)(2,1)}) custom-call(s32[4]{0:T(128)S(1)} %pad_add_fusion.where, bf16[4,272,256]{2,1,0:T(8,128)(2,1)S(1)} %get-tuple-element.65.refs_0_, ...), custom_call_target="tpu_custom_call" | custom-call | bytes 4194304 | tf_op jit(solution)/shard_map/second_pack/pallas_call | solution.py:369
  99.4 2.2 %collective-permute-start.27 = (bf16[4,272,256]{2,1,0:T(8,128)(2,1)S(1)}, bf16[4,272,256]{2,1,0:T(8,128)(2,1)S(1)}, u32[]{:S(2)}, u32[]{:S(2)}) collective-permute-start(bf16[4,272,256]{2,1,0:T(8,128)(2,1)S(1)} %get-tuple-element.73.refs_0_), channel_id=1, source_target_pairs={{0,1},{1,0},{2,3},{3,2},{4,5},{5,4},{6,7},{7,6},{8,9},{9,8},{10,11... | collective-permute-start | bytes 1671176 | tf_op jit(solution)/shard_map/ppermute | solution.py:41
  101.6 1.2 collective-permute-start.26
  102.9 1.4 %collective-permute-start.28 = (bf16[4,272,256]{2,1,0:T(8,128)(2,1)}, bf16[4,272,256]{2,1,0:T(8,128)(2,1)S(1)}, u32[]{:S(2)}, u32[]{:S(2)}) collective-permute-start(bf16[4,272,256]{2,1,0:T(8,128)(2,1)} %get-tuple-element.75), channel_id=1, source_target_pairs={{0,24},{1,97},{2,26},{3,99},{4,28},{5,101},{6,30},{7,103},{8,0},{9... | collective-permute-start | bytes 1671176 | tf_op jit(solution)/shard_map/ppermute | solution.py:547
  104.3 1.0 collective-permute-start.25
  105.3 3.4 %copy-done = bf16[4096,1024]{1,0:T(8,128)(2,1)S(1)} copy-done((bf16[4096,1024]{1,0:T(8,128)(2,1)S(1)}, bf16[4096,1024]{1,0:T(8,128)(2,1)}, u32[]{:S(2)}) %copy-start) | copy-done | bytes 8388632
  108.7 1.8 %projection_grad.4.refs_2_ = f32[2,256,1024]{2,1,0:T(8,128)S(1)} custom-call(s32[4]{0:T(128)S(1)} %pad_add_fusion.where, bf16[4096,1024]{1,0:T(8,128)(2,1)S(1)} %copy-done, bf16[4,272,256]{2,1,0:T(8,128)(2,1)S(1)} %get-tuple-element.73.refs_0_, bf16[4,272,256]{2,1,0:T(8,128)(2,1)S(1)} %collective-permute-done.27.refs_1_), custom_call_target="tpu_custom_call" | custom-call | flops 1073741824 | bytes 5242880 | tf_op jit(solution)/shard_map/projection_grad/pallas_call | solution.py:426
  110.5 1.2 collective-permute-done.26.refs_0_
  111.7 1.2 collective-permute-start.31
  113.0 1.8 %projection_grad.5.refs_3_ = f32[2,256,1024]{2,1,0:T(8,128)S(1)} custom-call(s32[4]{0:T(128)S(1)} %pad_add_fusion.where, bf16[4096,1024]{1,0:T(8,128)(2,1)S(1)} %copy-done.1, bf16[4,272,256]{2,1,0:T(8,128)(2,1)S(1)} %collective-permute-done.26.refs_0_, bf16[4,272,256]{2,1,0:T(8,128)(2,1)S(1)} %collective-permute-done.28.refs_1_, ...), custom_call_target="tpu_custom_call" | custom-call | flops 1073741824 | bytes 5242880 | tf_op jit(solution)/shard_map/projection_grad/pallas_call | solution.py:426
  114.8 3.2 %collective-permute-done.25.refs_0_ = bf16[4,272,256]{2,1,0:T(8,128)(2,1)S(1)} collective-permute-done((bf16[4,272,256]{2,1,0:T(8,128)(2,1)S(1)}, bf16[4,272,256]{2,1,0:T(8,128)(2,1)S(1)}, u32[]{:S(2)}, u32[]{:S(2)}) %collective-permute-start.25) | collective-permute-done | bytes 557088 | tf_op jit(solution)/shard_map/ppermute | solution.py:547
  118.1 1.8 %collective-permute-start.29 = (bf16[4,272,256]{2,1,0:T(8,128)(2,1)S(1)}, bf16[4,272,256]{2,1,0:T(8,128)(2,1)S(1)}, u32[]{:S(2)}, u32[]{:S(2)}) collective-permute-start(bf16[4,272,256]{2,1,0:T(8,128)(2,1)S(1)} %collective-permute-done.25.refs_0_), channel_id=1, source_target_pairs={{0,1},{1,0},{2,3},{3,2},{4,5},{5,4},{6,7},{7,6},{8,9},{9,8},{10,11... | collective-permute-start | bytes 1671176 | tf_op jit(solution)/shard_map/ppermute | solution.py:41
  119.9 2.3 %projection_grad.6.refs_1_ = f32[2,256,1024]{2,1,0:T(8,128)S(1)} custom-call(s32[4]{0:T(128)S(1)} %pad_add_fusion.where, bf16[4096,1024]{1,0:T(8,128)(2,1)S(1)} %copy-done.1, bf16[4,272,256]{2,1,0:T(8,128)(2,1)S(1)} %collective-permute-done.25.refs_0_, bf16[4,272,256]{2,1,0:T(8,128)(2,1)S(1)} %collective-permute-done.30.refs_1_, ...), custom_call_target="tpu_custom_call" | custom-call | flops 1610612736 | bytes 7864320 | tf_op jit(solution)/shard_map/projection_grad/pallas_call | solution.py:426
  122.3 2.2 %projection_grad.7 = (bf16[512,1024]{1,0:T(8,128)(2,1)}, f32[1,1024]{1,0:T(1,128)}) custom-call(s32[4]{0:T(128)S(1)} %pad_add_fusion.where, bf16[4096,1024]{1,0:T(8,128)(2,1)S(1)} %copy-done.1, bf16[4,272,256]{2,1,0:T(8,128)(2,1)S(1)} %collective-permute-done.29.refs_0_, f32[2,256,1024]{2,1,0:T(8,128)S(1)} %projection_grad.6.refs_1_, ...), custom_call_target="tpu_custom_call" | custom-call | flops 536870912 | bytes 2621440 | tf_op jit(solution)/shard_map/projection_grad/pallas_call | solution.py:426
  (76 shorter events, 4.8 us)
Async XLA Ops:
  7.2 98.2 %all-gather.2.cloned.1.call-start = ((), (), s32[]{:S(2)}) async-start(), calls=%async_computation | async-start | bytes 8912896 | tf_op jit(solution)/shard_map/all_gather | solution.py:488
  8.0 1.0 copy-start.2
  9.1 11.9 %copy-start.7 = (f32[4]{0:T(128)S(1)}, f32[4]{0:T(128)}, u32[]{:S(2)}) copy-start(f32[4]{0:T(128)} %param.14) | copy-start | bytes 52
  9.1 11.9 %copy-start.9 = (s32[4]{0:T(128)S(1)}, s32[4]{0:T(128)}, u32[]{:S(2)}) copy-start(s32[4]{0:T(128)} %param.16) | copy-start | bytes 52
  9.1 11.9 %copy-start.10 = (s32[1,4]{1,0:T(1,128)S(1)}, s32[1,4]{1,0:T(1,128)}, u32[]{:S(2)}) copy-start(s32[1,4]{1,0:T(1,128)} %param.17) | copy-start | bytes 52
  15.1 3.0 %collective-permute-start = (bf16[256,1024]{1,0:T(8,128)(2,1)S(1)}, bf16[256,1024]{1,0:T(8,128)(2,1)S(1)}, u32[]{:S(2)}, u32[]{:S(2)}) collective-permute-start(bf16[256,1024]{1,0:T(8,128)(2,1)S(1)} %get-tuple-element.45), channel_id=1, source_target_pairs={{0,1},{1,0},{2,3},{3,2},{4,5},{5,4},{6,7},{7,6},{8,9},{9,8},{10,11... | collective-permute-start | bytes 1572872 | tf_op jit(solution)/shard_map/ppermute | solution.py:41
  16.6 5.0 %collective-permute-start.1 = (bf16[256,1024]{1,0:T(8,128)(2,1)S(1)}, bf16[256,1024]{1,0:T(8,128)(2,1)S(1)}, u32[]{:S(2)}, u32[]{:S(2)}) collective-permute-start(bf16[256,1024]{1,0:T(8,128)(2,1)S(1)} %get-tuple-element.49), channel_id=1, source_target_pairs={{0,1},{1,0},{2,3},{3,2},{4,5},{5,4},{6,7},{7,6},{8,9},{9,8},{10,11... | collective-permute-start | bytes 1572872 | tf_op jit(solution)/shard_map/ppermute | solution.py:41
  16.7 4.9 %collective-permute-start.2 = (bf16[256,1024]{1,0:T(8,128)(2,1)S(1)}, bf16[256,1024]{1,0:T(8,128)(2,1)S(1)}, u32[]{:S(2)}, u32[]{:S(2)}) collective-permute-start(bf16[256,1024]{1,0:T(8,128)(2,1)S(1)} %get-tuple-element.50), channel_id=1, source_target_pairs={{0,1},{1,0},{2,3},{3,2},{4,5},{5,4},{6,7},{7,6},{8,9},{9,8},{10,11... | collective-permute-start | bytes 1572872 | tf_op jit(solution)/shard_map/ppermute | solution.py:41
  18.2 9.6 %collective-permute-start.3 = (bf16[128,1024]{1,0:T(8,128)(2,1)S(1)}, bf16[128,1024]{1,0:T(8,128)(2,1)S(1)}, u32[]{:S(2)}, u32[]{:S(2)}) collective-permute-start(bf16[128,1024]{1,0:T(8,128)(2,1)S(1)} %get-tuple-element.46), channel_id=1, source_target_pairs={{0,2},{1,3},{2,4},{3,5},{4,6},{5,7},{6,0},{7,1},{8,10},{9,11},{10,... | collective-permute-start | bytes 786440 | tf_op jit(solution)/shard_map/ppermute | solution.py:494
  19.6 8.3 %collective-permute-start.4 = (bf16[128,1024]{1,0:T(8,128)(2,1)S(1)}, bf16[128,1024]{1,0:T(8,128)(2,1)S(1)}, u32[]{:S(2)}, u32[]{:S(2)}) collective-permute-start(bf16[128,1024]{1,0:T(8,128)(2,1)S(1)} %get-tuple-element.47), channel_id=1, source_target_pairs={{0,6},{1,7},{2,0},{3,1},{4,2},{5,3},{6,4},{7,5},{8,14},{9,15},{10,... | collective-permute-start | bytes 786440 | tf_op jit(solution)/shard_map/ppermute | solution.py:495
  26.7 4.7 %copy-start.8 = (s32[4]{0:T(128)S(1)}, s32[4]{0:T(128)}, u32[]{:S(2)}) copy-start(s32[4]{0:T(128)} %param.15) | copy-start | bytes 52
  26.7 5.0 %copy-start.6 = (bf16[1024]{0:T(1024)(128)(2,1)S(1)}, bf16[1024]{0:T(1024)(128)(2,1)}, u32[]{:S(2)}) copy-start(bf16[1024]{0:T(1024)(128)(2,1)} %param.12) | copy-start | bytes 6148
  26.8 13.3 %copy-start.3 = (bf16[256,1024]{1,0:T(8,128)(2,1)S(1)}, bf16[256,1024]{1,0:T(8,128)(2,1)}, u32[]{:S(2)}) copy-start(bf16[256,1024]{1,0:T(8,128)(2,1)} %att.5) | copy-start | bytes 1572868
  26.8 13.3 %collective-permute-start.5 = (bf16[256,1024]{1,0:T(8,128)(2,1)S(1)}, bf16[256,1024]{1,0:T(8,128)(2,1)S(1)}, u32[]{:S(2)}, u32[]{:S(2)}) collective-permute-start(bf16[256,1024]{1,0:T(8,128)(2,1)S(1)} %get-tuple-element.55), channel_id=1, source_target_pairs={{0,1},{1,0},{2,3},{3,2},{4,5},{5,4},{6,7},{7,6},{8,9},{9,8},{10,11... | collective-permute-start | bytes 1572872 | tf_op jit(solution)/shard_map/ppermute | solution.py:41
  28.8 14.5 %collective-permute-start.6 = (bf16[256,1024]{1,0:T(8,128)(2,1)}, bf16[256,1024]{1,0:T(8,128)(2,1)S(1)}, u32[]{:S(2)}, u32[]{:S(2)}) collective-permute-start(bf16[256,1024]{1,0:T(8,128)(2,1)} %get-tuple-element.56), channel_id=1, source_target_pairs={{0,2},{1,3},{2,4},{3,5},{4,6},{5,7},{6,0},{7,1},{8,10},{9,11},{10,... | collective-permute-start | bytes 1572872 | tf_op jit(solution)/shard_map/ppermute | solution.py:506
  28.9 14.3 %collective-permute-start.7 = (bf16[256,1024]{1,0:T(8,128)(2,1)S(1)}, bf16[256,1024]{1,0:T(8,128)(2,1)S(1)}, u32[]{:S(2)}, u32[]{:S(2)}) collective-permute-start(bf16[256,1024]{1,0:T(8,128)(2,1)S(1)} %get-tuple-element.53), channel_id=1, source_target_pairs={{0,6},{1,7},{2,0},{3,1},{4,2},{5,3},{6,4},{7,5},{8,14},{9,15},{10,... | collective-permute-start | bytes 1572872 | tf_op jit(solution)/shard_map/ppermute | solution.py:507
  32.8 10.4 %copy-start.4 = (bf16[256,1024]{1,0:T(8,128)(2,1)S(1)}, bf16[256,1024]{1,0:T(8,128)(2,1)}, u32[]{:S(2)}) copy-start(bf16[256,1024]{1,0:T(8,128)(2,1)} %cot.3) | copy-start | bytes 1572868
  32.8 10.4 %copy-start.5 = (bf16[256,1024]{1,0:T(8,128)(2,1)S(1)}, bf16[256,1024]{1,0:T(8,128)(2,1)}, u32[]{:S(2)}) copy-start(bf16[256,1024]{1,0:T(8,128)(2,1)} %residual) | copy-start | bytes 1572868
  32.8 10.3 %collective-permute-start.8 = (f32[1,128]{1,0:T(1,128)S(1)}, f32[1,128]{1,0:T(1,128)S(1)}, u32[]{:S(2)}, u32[]{:S(2)}) collective-permute-start(f32[1,128]{1,0:T(1,128)S(1)} %bitcast.28), channel_id=1, source_target_pairs={{0,0},{1,17},{2,34},{3,51},{4,68},{5,85},{6,102},{7,119},{8,8},{9,... | collective-permute-start | bytes 1544 | tf_op jit(solution)/shard_map/ppermute | solution.py:512
  37.9 5.2 %collective-permute-start.9 = (f32[1,128]{1,0:T(1,128)S(1)}, f32[1,128]{1,0:T(1,128)S(1)}, u32[]{:S(2)}, u32[]{:S(2)}) collective-permute-start(f32[1,128]{1,0:T(1,128)S(1)} %bitcast.29), channel_id=1, source_target_pairs={{0,8},{1,25},{2,42},{3,59},{4,76},{5,93},{6,110},{7,127},{8,16},{9... | collective-permute-start | bytes 1544 | tf_op jit(solution)/shard_map/ppermute | solution.py:512
  43.8 2.2 %collective-permute-start.10 = (f32[8,256]{1,0:T(8,128)S(1)}, f32[8,256]{1,0:T(8,128)S(1)}, u32[]{:S(2)}, u32[]{:S(2)}) collective-permute-start(f32[8,256]{1,0:T(8,128)S(1)} %get-tuple-element.61), channel_id=1, source_target_pairs={{0,1},{1,0},{2,3},{3,2},{4,5},{5,4},{6,7},{7,6},{8,9},{9,8},{10,11... | collective-permute-start | bytes 24584 | tf_op jit(solution)/shard_map/ppermute | solution.py:41
  46.0 4.3 %collective-permute-start.11 = (f32[8,256]{1,0:T(8,128)S(1)}, f32[8,256]{1,0:T(8,128)S(1)}, u32[]{:S(2)}, u32[]{:S(2)}) collective-permute-start(f32[8,256]{1,0:T(8,128)S(1)} %add.23.s0), channel_id=1, source_target_pairs={{0,2},{1,3},{2,4},{3,5},{4,6},{5,7},{6,0},{7,1},{8,10},{9,11},{10,... | collective-permute-start | bytes 24584 | tf_op jit(solution)/shard_map/ppermute | solution.py:522
  47.0 4.1 %collective-permute-start.12 = (f32[8,256]{1,0:T(8,128)S(1)}, f32[8,256]{1,0:T(8,128)S(1)}, u32[]{:S(2)}, u32[]{:S(2)}) collective-permute-start(f32[8,256]{1,0:T(8,128)S(1)} %add.23.s0), channel_id=1, source_target_pairs={{0,4},{1,5},{2,6},{3,7},{4,0},{5,1},{6,2},{7,3},{8,12},{9,13},{10,... | collective-permute-start | bytes 24584 | tf_op jit(solution)/shard_map/ppermute | solution.py:522
  49.7 2.9 %collective-permute-start.13 = (f32[8,256]{1,0:T(8,128)S(1)}, f32[8,256]{1,0:T(8,128)S(1)}, u32[]{:S(2)}, u32[]{:S(2)}) collective-permute-start(f32[8,256]{1,0:T(8,128)S(1)} %add.23.s0), channel_id=1, source_target_pairs={{0,6},{1,7},{2,0},{3,1},{4,2},{5,3},{6,4},{7,5},{8,14},{9,15},{10,... | collective-permute-start | bytes 24584 | tf_op jit(solution)/shard_map/ppermute | solution.py:522
  54.0 13.1 %collective-permute-start.15 = (bf16[256,1024]{1,0:T(8,128)(2,1)S(1)}, bf16[256,1024]{1,0:T(8,128)(2,1)S(1)}, u32[]{:S(2)}, u32[]{:S(2)}) collective-permute-start(bf16[256,1024]{1,0:T(8,128)(2,1)S(1)} %get-tuple-element.63.refs_0_), channel_id=1, source_target_pairs={{0,2},{1,3},{2,4},{3,5},{4,6},{5,7},{6,0},{7,1},{8,10},{9,11},{10,... | collective-permute-start | bytes 1572872 | tf_op jit(solution)/shard_map/ppermute | solution.py:528
  54.0 13.2 %collective-permute-start.18 = (bf16[256,1024]{1,0:T(8,128)(2,1)S(1)}, bf16[256,1024]{1,0:T(8,128)(2,1)S(1)}, u32[]{:S(2)}, u32[]{:S(2)}) collective-permute-start(bf16[256,1024]{1,0:T(8,128)(2,1)S(1)} %get-tuple-element.63.refs_0_), channel_id=1, source_target_pairs={{0,6},{1,7},{2,0},{3,1},{4,2},{5,3},{6,4},{7,5},{8,14},{9,15},{10,... | collective-permute-start | bytes 1572872 | tf_op jit(solution)/shard_map/ppermute | solution.py:528
  67.1 6.9 %collective-permute-start.17 = (bf16[128,1024]{1,0:T(8,128)(2,1)S(1)}, bf16[128,1024]{1,0:T(8,128)(2,1)S(1)}, u32[]{:S(2)}, u32[]{:S(2)}) collective-permute-start(bf16[128,1024]{1,0:T(8,128)(2,1)S(1)} %slice.40), channel_id=1, source_target_pairs={{0,2},{1,3},{2,4},{3,5},{4,6},{5,7},{6,0},{7,1},{8,10},{9,11},{10,... | collective-permute-start | bytes 786440 | tf_op jit(solution)/shard_map/ppermute | solution.py:529
  67.2 6.8 %collective-permute-start.19 = (bf16[128,1024]{1,0:T(8,128)(2,1)S(1)}, bf16[128,1024]{1,0:T(8,128)(2,1)S(1)}, u32[]{:S(2)}, u32[]{:S(2)}) collective-permute-start(bf16[128,1024]{1,0:T(8,128)(2,1)S(1)} %slice.41), channel_id=1, source_target_pairs={{0,6},{1,7},{2,0},{3,1},{4,2},{5,3},{6,4},{7,5},{8,14},{9,15},{10,... | collective-permute-start | bytes 786440 | tf_op jit(solution)/shard_map/ppermute | solution.py:530
  70.0 7.4 %collective-permute-start.14 = (bf16[256,1024]{1,0:T(8,128)(2,1)S(1)}, bf16[256,1024]{1,0:T(8,128)(2,1)S(1)}, u32[]{:S(2)}, u32[]{:S(2)}) collective-permute-start(bf16[256,1024]{1,0:T(8,128)(2,1)S(1)} %get-tuple-element.63.refs_0_), channel_id=1, source_target_pairs={{0,1},{1,0},{2,3},{3,2},{4,5},{5,4},{6,7},{7,6},{8,9},{9,8},{10,11... | collective-permute-start | bytes 1572872 | tf_op jit(solution)/shard_map/ppermute | solution.py:41
  73.0 4.4 %collective-permute-start.16 = (bf16[256,1024]{1,0:T(8,128)(2,1)S(1)}, bf16[256,1024]{1,0:T(8,128)(2,1)S(1)}, u32[]{:S(2)}, u32[]{:S(2)}) collective-permute-start(bf16[256,1024]{1,0:T(8,128)(2,1)S(1)} %collective-permute-done.15.refs_2_), channel_id=1, source_target_pairs={{0,1},{1,0},{2,3},{3,2},{4,5},{5,4},{6,7},{7,6},{8,9},{9,8},{10,11... | collective-permute-start | bytes 1572872 | tf_op jit(solution)/shard_map/ppermute | solution.py:41
  73.0 4.4 %collective-permute-start.21 = (bf16[256,1024]{1,0:T(8,128)(2,1)S(1)}, bf16[256,1024]{1,0:T(8,128)(2,1)S(1)}, u32[]{:S(2)}, u32[]{:S(2)}) collective-permute-start(bf16[256,1024]{1,0:T(8,128)(2,1)S(1)} %collective-permute-done.18.refs_6_), channel_id=1, source_target_pairs={{0,1},{1,0},{2,3},{3,2},{4,5},{5,4},{6,7},{7,6},{8,9},{9,8},{10,11... | collective-permute-start | bytes 1572872 | tf_op jit(solution)/shard_map/ppermute | solution.py:41
  74.1 4.8 %collective-permute-start.20 = (bf16[256,1024]{1,0:T(8,128)(2,1)S(1)}, bf16[256,1024]{1,0:T(8,128)(2,1)S(1)}, u32[]{:S(2)}, u32[]{:S(2)}) collective-permute-start(bf16[256,1024]{1,0:T(8,128)(2,1)S(1)} %joined.1.refs_4_), channel_id=1, source_target_pairs={{0,1},{1,0},{2,3},{3,2},{4,5},{5,4},{6,7},{7,6},{8,9},{9,8},{10,11... | collective-permute-start | bytes 1572872 | tf_op jit(solution)/shard_map/ppermute | solution.py:41
  80.4 13.1 %collective-permute-start.22 = (bf16[4,272,256]{2,1,0:T(8,128)(2,1)S(1)}, bf16[4,272,256]{2,1,0:T(8,128)(2,1)S(1)}, u32[]{:S(2)}, u32[]{:S(2)}) collective-permute-start(bf16[4,272,256]{2,1,0:T(8,128)(2,1)S(1)} %get-tuple-element.66), channel_id=1, source_target_pairs={{0,32},{1,9},{2,34},{3,11},{4,36},{5,13},{6,38},{7,15},{8,40},{9,1... | collective-permute-start | bytes 1671176 | tf_op jit(solution)/shard_map/ppermute | solution.py:539
  81.9 15.8 %collective-permute-start.23 = (bf16[4,272,256]{2,1,0:T(8,128)(2,1)S(1)}, bf16[4,272,256]{2,1,0:T(8,128)(2,1)S(1)}, u32[]{:S(2)}, u32[]{:S(2)}) collective-permute-start(bf16[4,272,256]{2,1,0:T(8,128)(2,1)S(1)} %get-tuple-element.67), channel_id=1, source_target_pairs={{0,64},{1,17},{2,66},{3,19},{4,68},{5,21},{6,70},{7,23},{8,72},{9,... | collective-permute-start | bytes 1671176 | tf_op jit(solution)/shard_map/ppermute | solution.py:539
  84.5 13.2 %collective-permute-start.24 = (bf16[4,272,256]{2,1,0:T(8,128)(2,1)S(1)}, bf16[4,272,256]{2,1,0:T(8,128)(2,1)S(1)}, u32[]{:S(2)}, u32[]{:S(2)}) collective-permute-start(bf16[4,272,256]{2,1,0:T(8,128)(2,1)S(1)} %get-tuple-element.68), channel_id=1, source_target_pairs={{0,96},{1,25},{2,98},{3,27},{4,100},{5,29},{6,102},{7,31},{8,104},... | collective-permute-start | bytes 1671176 | tf_op jit(solution)/shard_map/ppermute | solution.py:539
  99.4 5.9 %collective-permute-start.27 = (bf16[4,272,256]{2,1,0:T(8,128)(2,1)S(1)}, bf16[4,272,256]{2,1,0:T(8,128)(2,1)S(1)}, u32[]{:S(2)}, u32[]{:S(2)}) collective-permute-start(bf16[4,272,256]{2,1,0:T(8,128)(2,1)S(1)} %get-tuple-element.73.refs_0_), channel_id=1, source_target_pairs={{0,1},{1,0},{2,3},{3,2},{4,5},{5,4},{6,7},{7,6},{8,9},{9,8},{10,11... | collective-permute-start | bytes 1671176 | tf_op jit(solution)/shard_map/ppermute | solution.py:41
  101.6 10.1 %collective-permute-start.26 = (bf16[4,272,256]{2,1,0:T(8,128)(2,1)}, bf16[4,272,256]{2,1,0:T(8,128)(2,1)S(1)}, u32[]{:S(2)}, u32[]{:S(2)}) collective-permute-start(bf16[4,272,256]{2,1,0:T(8,128)(2,1)} %get-tuple-element.72), channel_id=1, source_target_pairs={{0,8},{1,33},{2,10},{3,35},{4,12},{5,37},{6,14},{7,39},{8,16},{9,4... | collective-permute-start | bytes 1671176 | tf_op jit(solution)/shard_map/ppermute | solution.py:547
  102.9 8.9 %collective-permute-start.28 = (bf16[4,272,256]{2,1,0:T(8,128)(2,1)}, bf16[4,272,256]{2,1,0:T(8,128)(2,1)S(1)}, u32[]{:S(2)}, u32[]{:S(2)}) collective-permute-start(bf16[4,272,256]{2,1,0:T(8,128)(2,1)} %get-tuple-element.75), channel_id=1, source_target_pairs={{0,24},{1,97},{2,26},{3,99},{4,28},{5,101},{6,30},{7,103},{8,0},{9... | collective-permute-start | bytes 1671176 | tf_op jit(solution)/shard_map/ppermute | solution.py:547
  104.3 13.8 %collective-permute-start.25 = (bf16[4,272,256]{2,1,0:T(8,128)(2,1)S(1)}, bf16[4,272,256]{2,1,0:T(8,128)(2,1)S(1)}, u32[]{:S(2)}, u32[]{:S(2)}) collective-permute-start(bf16[4,272,256]{2,1,0:T(8,128)(2,1)S(1)} %get-tuple-element.71), channel_id=1, source_target_pairs={{0,16},{1,65},{2,18},{3,67},{4,20},{5,69},{6,22},{7,71},{8,24},{9,... | collective-permute-start | bytes 1671176 | tf_op jit(solution)/shard_map/ppermute | solution.py:547
  105.3 3.4 %copy-start = (bf16[4096,1024]{1,0:T(8,128)(2,1)S(1)}, bf16[4096,1024]{1,0:T(8,128)(2,1)}, u32[]{:S(2)}) copy-start(bf16[4096,1024]{1,0:T(8,128)(2,1)} %all-gather.2.cloned.1.call-done.gathered) | copy-start | bytes 25165828
  108.7 4.3 %copy-start.1 = (bf16[4096,1024]{1,0:T(8,128)(2,1)S(1)}, bf16[4096,1024]{1,0:T(8,128)(2,1)}, u32[]{:S(2)}) copy-start(bf16[4096,1024]{1,0:T(8,128)(2,1)} %all-gather.2.cloned.1.call-done.gathered) | copy-start | bytes 25165828
  111.7 8.2 %collective-permute-start.31 = (bf16[4,272,256]{2,1,0:T(8,128)(2,1)S(1)}, bf16[4,272,256]{2,1,0:T(8,128)(2,1)S(1)}, u32[]{:S(2)}, u32[]{:S(2)}) collective-permute-start(bf16[4,272,256]{2,1,0:T(8,128)(2,1)S(1)} %collective-permute-done.28.refs_1_), channel_id=1, source_target_pairs={{0,1},{1,0},{2,3},{3,2},{4,5},{5,4},{6,7},{7,6},{8,9},{9,8},{10,11... | collective-permute-start | bytes 1671176 | tf_op jit(solution)/shard_map/ppermute | solution.py:41
  113.0 6.9 %collective-permute-start.30 = (bf16[4,272,256]{2,1,0:T(8,128)(2,1)S(1)}, bf16[4,272,256]{2,1,0:T(8,128)(2,1)S(1)}, u32[]{:S(2)}, u32[]{:S(2)}) collective-permute-start(bf16[4,272,256]{2,1,0:T(8,128)(2,1)S(1)} %collective-permute-done.26.refs_0_), channel_id=1, source_target_pairs={{0,1},{1,0},{2,3},{3,2},{4,5},{5,4},{6,7},{7,6},{8,9},{9,8},{10,11... | collective-permute-start | bytes 1671176 | tf_op jit(solution)/shard_map/ppermute | solution.py:41
  118.1 4.2 %collective-permute-start.29 = (bf16[4,272,256]{2,1,0:T(8,128)(2,1)S(1)}, bf16[4,272,256]{2,1,0:T(8,128)(2,1)S(1)}, u32[]{:S(2)}, u32[]{:S(2)}) collective-permute-start(bf16[4,272,256]{2,1,0:T(8,128)(2,1)S(1)} %collective-permute-done.25.refs_0_), channel_id=1, source_target_pairs={{0,1},{1,0},{2,3},{3,2},{4,5},{5,4},{6,7},{7,6},{8,9},{9,8},{10,11... | collective-permute-start | bytes 1671176 | tf_op jit(solution)/shard_map/ppermute | solution.py:41
Sparse Core Ops, SparseCore 0:
  10.1 74.0 all-gather.1

commit v6 on v5

--- a/solution.py
+++ b/solution.py
@@ -116,17 +116,16 @@
             out[here, :] = (first[band, :] + second[band, :].astype(F32)).astype(BF)
 
 
-def passed_kernel(first, third, top, bottom, next_first, next_third):
-    rows = top.shape[0]
+def passed_kernel(low, value, half, out):
+    rows = half.shape[0]
 
     @pl.loop(0, rows // 64)
     def _(i):
-        low = pl.ds(pl.multiple_of(i * 64, 64), 64)
-        high = pl.ds(pl.multiple_of(rows + i * 64, 64), 64)
-        next_first[low, :] = (first[low, :] + top[low, :].astype(F32)).astype(BF)
-        next_first[high, :] = first[high, :].astype(BF)
-        next_third[low, :] = third[low, :].astype(BF)
-        next_third[high, :] = (third[high, :] + bottom[low, :].astype(F32)).astype(BF)
+        here = pl.ds(pl.multiple_of(i * 64, 64), 64)
+        added = pl.ds(pl.multiple_of((0 if low else rows) + i * 64, 64), 64)
+        alone = pl.ds(pl.multiple_of((rows if low else 0) + i * 64, 64), 64)
+        out[added, :] = (value[added, :] + half[here, :].astype(F32)).astype(BF)
+        out[alone, :] = value[alone, :].astype(BF)
 
 
 def joined_kernel(top, bottom, out):
@@ -500,14 +499,17 @@
         [(1, False, True, F32), (3, False, True, F32), (0, True, False, BF)],
         [swap(send1), swap(send3)],
     )
-    first, third = small_call(
-        passed_kernel, [first, third, top, bottom], [(rows, width)] * 2, "passed"
+    (first,) = small_call(
+        functools.partial(passed_kernel, True), [first, top], [(rows, width)], "passed"
     )
     arrived[1] = lax.ppermute(first, "tensor", x_shift(1))
+    (third,) = small_call(
+        functools.partial(passed_kernel, False), [third, bottom], [(rows, width)], "passed"
+    )
     arrived[3] = lax.ppermute(third, "tensor", x_shift(3))
     stats = local_stats(rewards, group_ids, kept_flags, lengths)
     info = token_info(rewards, group_ids, kept_flags, lengths, rows)
-    stats, info, _ = lax.optimization_barrier((stats, info, third))
+    stats, _ = lax.optimization_barrier((stats, third))
     late_where, _ = lax.optimization_barrier((where, third))
     stats = [lax.ppermute(stats, ("dp", "tensor"), scattered(step)) for step in (0, 1)]
     (own,) = partial_products(
@@ -519,7 +521,7 @@
     )
 
     chip = sums + swap(sums)
-    others = [lax.ppermute(chip, "tensor", x_shift(k)) for k in (1, 2, 3)]
+    others = [lax.ppermute(chip, "tensor", x_shift(k)) for k in (2, 1, 3)]
     tokens = rows * lax.axis_size("dp")
     grad_residual, own_piece, gain_term = grad_call(
         features, tokens, hidden, cotangent, gain, chip, *others, info

time: 133 us -> 133 us (level)
    pallas_call x3, Pallas kernels: 14.2 us -> 15.8 us  [partial_products(): pl.pallas_call(functools.partial(partial_kernel, jobs), in_specs=[pl.Bloc...]
  transfers between devices with their start and end apart: 33 -> 33, of which waited for: 11 -> 10; matrix products, arithmetic and copies ran while one was open for 2% -> 2% of each run, Pallas kernels for 26% -> 27%
where the time goes in v6:
time: 133 us; the launch traced here: 131 us
  starting transfers between devices  47.3 us (36%)
  Pallas kernels  37.6 us (28%)
  waiting for transfers between devices  25.4 us (19%)
  between operations  14.4 us (11%)
  local copies, waits for them, and re-layouts  5.32 us (4%)
    ppermute x13, starting transfers between devices, swap(): return lax.ppermute(value, 'tensor', CORE_SWAP)  15.8 us
    pallas_call x3, Pallas kernels, partial_products(): pl.pallas_call(functools.partial(partial_kernel, jobs), in_specs=[pl.Bloc...  15.8 us
    ppermute x2, waiting for transfers between devices, shards(): near = {k: lax.ppermute(own_piece, 'tensor', x_shift(k)) for k in (1, 3)}  10.4 us
    pallas_call x4, Pallas kernels, projection_call(): pl.pallas_call(functools.partial(projection_kernel, members, first, last)...  8.24 us
    pallas_call x1, Pallas kernels, attention_call(): pl.pallas_call(attention_kernel, in_specs=[pl.BlockSpec(memory_space=pltp...  7.98 us
    ppermute x2, starting transfers between devices, shards(): lax.ppermute(stats, ('dp', 'tensor'), scattered(step))  7.18 us
    ppermute x3, starting transfers between devices, shards(): parts[k] = lax.ppermute(sends[k], ('dp', 'tensor'), plane_shift(0, k))  5.12 us
    ppermute x3, waiting for transfers between devices, shards(): mine[k] = lax.ppermute(sends[k], ('dp', 'tensor'), plane_shift(1, k))  4.48 us
  transfers between devices with their start and end apart: 33, of which 10 were waited for; matrix products, arithmetic and copies ran while one was open for 2% of the time, Pallas kernels for 27%

profile of v6, /device:TPU:1, one launch (start us, length us, event | category | flops | bytes accessed | tf_op | source)
XLA Modules:
  0.0 131.3 jit_solution(12107076988075089898)
XLA Ops:
  7.2 0.7 all-gather.2.cloned.1.call-update
  8.0 1.0 copy-done.2
  9.1 6.8 %partial.3 = (bf16[256,1024]{1,0:T(8,128)(2,1)}, f32[256,1024]{1,0:T(8,128)S(1)}, bf16[256,1024]{1,0:T(8,128)(2,1)}, bf16[256,1024]{1,0:T(8,128)(2,1)}) custom-call(s32[4]{0:T(128)S(1)} %pad_add_fusion.where, bf16[256,1024]{1,0:T(8,128)(2,1)S(1)} %copy-done.2, bf16[8192,1024]{1,0:T(8,128)(2,1)} %refs_8_.1), custom_call_target="tpu_custom_call" | custom-call | flops 2147483648 | bytes 8388608 | tf_op jit(solution)/shard_map/partial/pallas_call | solution.py:89
  15.9 1.5 %collective-permute-start = (bf16[256,1024]{1,0:T(8,128)(2,1)}, bf16[256,1024]{1,0:T(8,128)(2,1)S(1)}, u32[]{:S(2)}, u32[]{:S(2)}) collective-permute-start(bf16[256,1024]{1,0:T(8,128)(2,1)} %get-tuple-element.42), channel_id=1, source_target_pairs={{0,1},{1,0},{2,3},{3,2},{4,5},{5,4},{6,7},{7,6},{8,9},{9,8},{10,11... | collective-permute-start | bytes 1572872 | tf_op jit(solution)/shard_map/ppermute | solution.py:41
  18.2 0.9 collective-permute-done.second
  19.2 1.4 %collective-permute-start.5 = (bf16[128,1024]{1,0:T(8,128)(2,1)S(1)}, bf16[128,1024]{1,0:T(8,128)(2,1)S(1)}, u32[]{:S(2)}, u32[]{:S(2)}) collective-permute-start(bf16[128,1024]{1,0:T(8,128)(2,1)S(1)} %get-tuple-element.43), channel_id=1, source_target_pairs={{0,2},{1,3},{2,4},{3,5},{4,6},{5,7},{6,0},{7,1},{8,10},{9,11},{10,... | collective-permute-start | bytes 786440 | tf_op jit(solution)/shard_map/ppermute | solution.py:493
  20.6 1.4 %collective-permute-start.3 = (bf16[128,1024]{1,0:T(8,128)(2,1)S(1)}, bf16[128,1024]{1,0:T(8,128)(2,1)S(1)}, u32[]{:S(2)}, u32[]{:S(2)}) collective-permute-start(bf16[128,1024]{1,0:T(8,128)(2,1)S(1)} %get-tuple-element.44), channel_id=1, source_target_pairs={{0,6},{1,7},{2,0},{3,1},{4,2},{5,3},{6,4},{7,5},{8,14},{9,15},{10,... | collective-permute-start | bytes 786440 | tf_op jit(solution)/shard_map/ppermute | solution.py:494
  22.1 5.9 %partial.4 = (f32[256,1024]{1,0:T(8,128)S(1)}, f32[256,1024]{1,0:T(8,128)S(1)}, bf16[256,1024]{1,0:T(8,128)(2,1)}) custom-call(s32[4]{0:T(128)S(1)} %pad_add_fusion.where, bf16[256,1024]{1,0:T(8,128)(2,1)S(1)} %copy-done.3, bf16[8192,1024]{1,0:T(8,128)(2,1)} %refs_8_.1, bf16[256,1024]{1,0:T(8,128)(2,1)S(1)} %collective-permute-done.1.refs_0_, ...), custom_call_target="tpu_custom_call" | custom-call | flops 1610612736 | bytes 6291456 | tf_op jit(solution)/shard_map/partial/pallas_call | solution.py:89
  28.1 1.0 collective-permute-start.4
  29.4 2.6 %collective-permute-start.7 = (bf16[256,1024]{1,0:T(8,128)(2,1)S(1)}, bf16[256,1024]{1,0:T(8,128)(2,1)S(1)}, u32[]{:S(2)}, u32[]{:S(2)}) collective-permute-start(bf16[256,1024]{1,0:T(8,128)(2,1)S(1)} %passed.2), channel_id=1, source_target_pairs={{0,6},{1,7},{2,0},{3,1},{4,2},{5,3},{6,4},{7,5},{8,14},{9,15},{10,... | collective-permute-start | bytes 1572872 | tf_op jit(solution)/shard_map/ppermute | solution.py:509
  32.1 0.6 convert_multiply_fusion
  32.8 0.7 concatenate.10
  33.6 5.0 %collective-permute-start.8 = (f32[1,128]{1,0:T(1,128)S(1)}, f32[1,128]{1,0:T(1,128)S(1)}, u32[]{:S(2)}, u32[]{:S(2)}) collective-permute-start(f32[1,128]{1,0:T(1,128)S(1)} %bitcast.28), channel_id=1, source_target_pairs={{0,0},{1,17},{2,34},{3,51},{4,68},{5,85},{6,102},{7,119},{8,8},{9,... | collective-permute-start | bytes 1544 | tf_op jit(solution)/shard_map/ppermute | solution.py:514
  38.6 2.2 %collective-permute-start.9 = (f32[1,128]{1,0:T(1,128)S(1)}, f32[1,128]{1,0:T(1,128)S(1)}, u32[]{:S(2)}, u32[]{:S(2)}) collective-permute-start(f32[1,128]{1,0:T(1,128)S(1)} %bitcast.29), channel_id=1, source_target_pairs={{0,8},{1,25},{2,42},{3,59},{4,76},{5,93},{6,110},{7,127},{8,16},{9... | collective-permute-start | bytes 1544 | tf_op jit(solution)/shard_map/ppermute | solution.py:514
  40.8 3.1 %partial.5.own = f32[256,1024]{1,0:T(8,128)S(1)} custom-call(s32[4]{0:T(128)S(1)} %pad_add_fusion.where, bf16[256,1024]{1,0:T(8,128)(2,1)S(1)} %copy-done.3, bf16[8192,1024]{1,0:T(8,128)(2,1)} %refs_8_.1, bf16[256,1024]{1,0:T(8,128)(2,1)S(1)} %collective-permute-done.4.refs_0_), custom_call_target="tpu_custom_call" | custom-call | flops 536870912 | bytes 2097152 | tf_op jit(solution)/shard_map/partial/pallas_call | solution.py:89
  44.5 0.9 collective-permute-start.10
  45.4 0.8 collective-permute-done.10
  46.2 1.7 %collective-permute-start.11 = (f32[8,256]{1,0:T(8,128)S(1)}, f32[8,256]{1,0:T(8,128)S(1)}, u32[]{:S(2)}, u32[]{:S(2)}) collective-permute-start(f32[8,256]{1,0:T(8,128)S(1)} %add.23.s0), channel_id=1, source_target_pairs={{0,4},{1,5},{2,6},{3,7},{4,0},{5,1},{6,2},{7,3},{8,12},{9,13},{10,... | collective-permute-start | bytes 24584 | tf_op jit(solution)/shard_map/ppermute | solution.py:524
  47.9 1.7 %collective-permute-start.12 = (f32[8,256]{1,0:T(8,128)S(1)}, f32[8,256]{1,0:T(8,128)S(1)}, u32[]{:S(2)}, u32[]{:S(2)}) collective-permute-start(f32[8,256]{1,0:T(8,128)S(1)} %add.23.s0), channel_id=1, source_target_pairs={{0,2},{1,3},{2,4},{3,5},{4,6},{5,7},{6,0},{7,1},{8,10},{9,11},{10,... | collective-permute-start | bytes 24584 | tf_op jit(solution)/shard_map/ppermute | solution.py:524
  49.6 0.9 collective-permute-start.13
  50.6 1.4 %collective-permute-done.12.s2 = f32[8,256]{1,0:T(8,128)S(1)} collective-permute-done((f32[8,256]{1,0:T(8,128)S(1)}, f32[8,256]{1,0:T(8,128)S(1)}, u32[]{:S(2)}, u32[]{:S(2)}) %collective-permute-start.12) | collective-permute-done | bytes 8224 | tf_op jit(solution)/shard_map/ppermute | solution.py:524
  52.5 1.5 %grad.1 = (bf16[256,1024]{1,0:T(8,128)(2,1)}, bf16[256,1024]{1,0:T(8,128)(2,1)S(1)}, f32[1,1024]{1,0:T(1,128)S(1)}) custom-call(f32[256,1024]{1,0:T(8,128)S(1)} %get-tuple-element.54.hidden, bf16[256,1024]{1,0:T(8,128)(2,1)S(1)} %copy-done.4, bf16[1,1024]{1,0:T(2,128)(2,1)S(1)} %broadcast_in_dim.40.gain, f32[8,256]{1,0:T(8,128)S(1)} %add.23.s0, ...), custom_call_target="tpu_custom_call" | custom-call | flops 3145728 | bytes 2097152 | tf_op jit(solution)/shard_map/grad/pallas_call | solution.py:258
  54.0 2.7 %collective-permute-start.18 = (bf16[256,1024]{1,0:T(8,128)(2,1)S(1)}, bf16[256,1024]{1,0:T(8,128)(2,1)S(1)}, u32[]{:S(2)}, u32[]{:S(2)}) collective-permute-start(bf16[256,1024]{1,0:T(8,128)(2,1)S(1)} %get-tuple-element.57.refs_0_), channel_id=1, source_target_pairs={{0,6},{1,7},{2,0},{3,1},{4,2},{5,3},{6,4},{7,5},{8,14},{9,15},{10,... | collective-permute-start | bytes 1572872 | tf_op jit(solution)/shard_map/ppermute | solution.py:530
  56.7 10.4 %collective-permute-done.15.refs_2_ = bf16[256,1024]{1,0:T(8,128)(2,1)S(1)} collective-permute-done((bf16[256,1024]{1,0:T(8,128)(2,1)S(1)}, bf16[256,1024]{1,0:T(8,128)(2,1)S(1)}, u32[]{:S(2)}, u32[]{:S(2)}) %collective-permute-start.15) | collective-permute-done | bytes 524320 | tf_op jit(solution)/shard_map/ppermute | solution.py:530
  67.2 2.7 %collective-permute-start.19 = (bf16[128,1024]{1,0:T(8,128)(2,1)S(1)}, bf16[128,1024]{1,0:T(8,128)(2,1)S(1)}, u32[]{:S(2)}, u32[]{:S(2)}) collective-permute-start(bf16[128,1024]{1,0:T(8,128)(2,1)S(1)} %slice.41), channel_id=1, source_target_pairs={{0,6},{1,7},{2,0},{3,1},{4,2},{5,3},{6,4},{7,5},{8,14},{9,15},{10,... | collective-permute-start | bytes 786440 | tf_op jit(solution)/shard_map/ppermute | solution.py:532
  69.9 3.0 %collective-permute-start.14 = (bf16[256,1024]{1,0:T(8,128)(2,1)S(1)}, bf16[256,1024]{1,0:T(8,128)(2,1)S(1)}, u32[]{:S(2)}, u32[]{:S(2)}) collective-permute-start(bf16[256,1024]{1,0:T(8,128)(2,1)S(1)} %get-tuple-element.57.refs_0_), channel_id=1, source_target_pairs={{0,1},{1,0},{2,3},{3,2},{4,5},{5,4},{6,7},{7,6},{8,9},{9,8},{10,11... | collective-permute-start | bytes 1572872 | tf_op jit(solution)/shard_map/ppermute | solution.py:41
  74.0 3.3 %collective-permute-start.20 = (bf16[256,1024]{1,0:T(8,128)(2,1)S(1)}, bf16[256,1024]{1,0:T(8,128)(2,1)S(1)}, u32[]{:S(2)}, u32[]{:S(2)}) collective-permute-start(bf16[256,1024]{1,0:T(8,128)(2,1)S(1)} %joined.1.refs_4_), channel_id=1, source_target_pairs={{0,1},{1,0},{2,3},{3,2},{4,5},{5,4},{6,7},{7,6},{8,9},{9,8},{10,11... | collective-permute-start | bytes 1572872 | tf_op jit(solution)/shard_map/ppermute | solution.py:41
  77.3 1.5 %collective-permute-done.20.refs_5_ = bf16[256,1024]{1,0:T(8,128)(2,1)S(1)} collective-permute-done((bf16[256,1024]{1,0:T(8,128)(2,1)S(1)}, bf16[256,1024]{1,0:T(8,128)(2,1)S(1)}, u32[]{:S(2)}, u32[]{:S(2)}) %collective-permute-start.20) | collective-permute-done | bytes 524320 | tf_op jit(solution)/shard_map/ppermute | solution.py:41
  78.9 1.5 %first_pack.1 = (bf16[4,272,256]{2,1,0:T(8,128)(2,1)S(1)}, bf16[4,272,256]{2,1,0:T(8,128)(2,1)S(1)}, bf16[4,272,256]{2,1,0:T(8,128)(2,1)S(1)}, bf16[4,272,256]{2,1,0:T(8,128)(2,1)S(1)}) custom-call(s32[4]{0:T(128)S(1)} %pad_add_fusion.where, bf16[256,1024]{1,0:T(8,128)(2,1)S(1)} %get-tuple-element.57.refs_0_, ...), custom_call_target="tpu_custom_call" | custom-call | bytes 4194304 | tf_op jit(solution)/shard_map/first_pack/pallas_call | solution.py:368
  80.4 1.4 %collective-permute-start.22 = (bf16[4,272,256]{2,1,0:T(8,128)(2,1)S(1)}, bf16[4,272,256]{2,1,0:T(8,128)(2,1)S(1)}, u32[]{:S(2)}, u32[]{:S(2)}) collective-permute-start(bf16[4,272,256]{2,1,0:T(8,128)(2,1)S(1)} %get-tuple-element.60), channel_id=1, source_target_pairs={{0,32},{1,9},{2,34},{3,11},{4,36},{5,13},{6,38},{7,15},{8,40},{9,1... | collective-permute-start | bytes 1671176 | tf_op jit(solution)/shard_map/ppermute | solution.py:541
  81.8 2.6 %collective-permute-start.23 = (bf16[4,272,256]{2,1,0:T(8,128)(2,1)S(1)}, bf16[4,272,256]{2,1,0:T(8,128)(2,1)S(1)}, u32[]{:S(2)}, u32[]{:S(2)}) collective-permute-start(bf16[4,272,256]{2,1,0:T(8,128)(2,1)S(1)} %get-tuple-element.61), channel_id=1, source_target_pairs={{0,64},{1,17},{2,66},{3,19},{4,68},{5,21},{6,70},{7,23},{8,72},{9,... | collective-permute-start | bytes 1671176 | tf_op jit(solution)/shard_map/ppermute | solution.py:541
  84.4 1.1 collective-permute-start.24
  85.5 8.0 %attention_grad.1 = bf16[256,1024]{1,0:T(8,128)(2,1)} custom-call(s32[4]{0:T(128)S(1)} %pad_add_fusion.where, bf16[256,1024]{1,0:T(8,128)(2,1)S(1)} %get-tuple-element.57.refs_0_, bf16[256,1024]{1,0:T(8,128)(2,1)S(1)} %collective-permute-done.14.refs_1_, bf16[256,1024]{1,0:T(8,128)(2,1)S(1)} %collective-permute-done.15.refs_2_, ...), custom_call_target="tpu_custom_call" | custom-call | flops 4294967296 | bytes 16777216 | tf_op jit(solution)/shard_map/attention_grad/pallas_call | solution.py:301
  93.5 4.1 %collective-permute-done.23.refs_2_ = bf16[4,272,256]{2,1,0:T(8,128)(2,1)S(1)} collective-permute-done((bf16[4,272,256]{2,1,0:T(8,128)(2,1)S(1)}, bf16[4,272,256]{2,1,0:T(8,128)(2,1)S(1)}, u32[]{:S(2)}, u32[]{:S(2)}) %collective-permute-start.23) | collective-permute-done | bytes 557088 | tf_op jit(solution)/shard_map/ppermute | solution.py:541
  97.6 1.8 %second_pack.1 = (bf16[4,272,256]{2,1,0:T(8,128)(2,1)S(1)}, bf16[4,272,256]{2,1,0:T(8,128)(2,1)}, bf16[4,272,256]{2,1,0:T(8,128)(2,1)}, bf16[4,272,256]{2,1,0:T(8,128)(2,1)}) custom-call(s32[4]{0:T(128)S(1)} %pad_add_fusion.where, bf16[4,272,256]{2,1,0:T(8,128)(2,1)S(1)} %get-tuple-element.59.refs_0_, ...), custom_call_target="tpu_custom_call" | custom-call | bytes 4194304 | tf_op jit(solution)/shard_map/second_pack/pallas_call | solution.py:368
  99.4 2.3 %collective-permute-start.27 = (bf16[4,272,256]{2,1,0:T(8,128)(2,1)S(1)}, bf16[4,272,256]{2,1,0:T(8,128)(2,1)S(1)}, u32[]{:S(2)}, u32[]{:S(2)}) collective-permute-start(bf16[4,272,256]{2,1,0:T(8,128)(2,1)S(1)} %get-tuple-element.67.refs_0_), channel_id=1, source_target_pairs={{0,1},{1,0},{2,3},{3,2},{4,5},{5,4},{6,7},{7,6},{8,9},{9,8},{10,11... | collective-permute-start | bytes 1671176 | tf_op jit(solution)/shard_map/ppermute | solution.py:41
  101.7 1.2 collective-permute-start.26
  103.0 1.4 %collective-permute-start.28 = (bf16[4,272,256]{2,1,0:T(8,128)(2,1)}, bf16[4,272,256]{2,1,0:T(8,128)(2,1)S(1)}, u32[]{:S(2)}, u32[]{:S(2)}) collective-permute-start(bf16[4,272,256]{2,1,0:T(8,128)(2,1)} %get-tuple-element.69), channel_id=1, source_target_pairs={{0,24},{1,97},{2,26},{3,99},{4,28},{5,101},{6,30},{7,103},{8,0},{9... | collective-permute-start | bytes 1671176 | tf_op jit(solution)/shard_map/ppermute | solution.py:549
  104.4 1.1 collective-permute-start.25
  105.5 3.4 %copy-done = bf16[4096,1024]{1,0:T(8,128)(2,1)S(1)} copy-done((bf16[4096,1024]{1,0:T(8,128)(2,1)S(1)}, bf16[4096,1024]{1,0:T(8,128)(2,1)}, u32[]{:S(2)}) %copy-start) | copy-done | bytes 8388632
  108.8 1.8 %projection_grad.4.refs_2_ = f32[2,256,1024]{2,1,0:T(8,128)S(1)} custom-call(s32[4]{0:T(128)S(1)} %pad_add_fusion.where, bf16[4096,1024]{1,0:T(8,128)(2,1)S(1)} %copy-done, bf16[4,272,256]{2,1,0:T(8,128)(2,1)S(1)} %get-tuple-element.67.refs_0_, bf16[4,272,256]{2,1,0:T(8,128)(2,1)S(1)} %collective-permute-done.27.refs_1_), custom_call_target="tpu_custom_call" | custom-call | flops 1073741824 | bytes 5242880 | tf_op jit(solution)/shard_map/projection_grad/pallas_call | solution.py:425
  110.7 1.2 collective-permute-done.26.refs_0_
  111.8 1.2 collective-permute-start.31
  113.0 1.8 %projection_grad.5.refs_3_ = f32[2,256,1024]{2,1,0:T(8,128)S(1)} custom-call(s32[4]{0:T(128)S(1)} %pad_add_fusion.where, bf16[4096,1024]{1,0:T(8,128)(2,1)S(1)} %copy-done.1, bf16[4,272,256]{2,1,0:T(8,128)(2,1)S(1)} %collective-permute-done.26.refs_0_, bf16[4,272,256]{2,1,0:T(8,128)(2,1)S(1)} %collective-permute-done.28.refs_1_, ...), custom_call_target="tpu_custom_call" | custom-call | flops 1073741824 | bytes 5242880 | tf_op jit(solution)/shard_map/projection_grad/pallas_call | solution.py:425
  114.9 3.3 %collective-permute-done.25.refs_0_ = bf16[4,272,256]{2,1,0:T(8,128)(2,1)S(1)} collective-permute-done((bf16[4,272,256]{2,1,0:T(8,128)(2,1)}, bf16[4,272,256]{2,1,0:T(8,128)(2,1)S(1)}, u32[]{:S(2)}, u32[]{:S(2)}) %collective-permute-start.25) | collective-permute-done | bytes 557088 | tf_op jit(solution)/shard_map/ppermute | solution.py:549
  118.2 1.6 %collective-permute-start.29 = (bf16[4,272,256]{2,1,0:T(8,128)(2,1)S(1)}, bf16[4,272,256]{2,1,0:T(8,128)(2,1)S(1)}, u32[]{:S(2)}, u32[]{:S(2)}) collective-permute-start(bf16[4,272,256]{2,1,0:T(8,128)(2,1)S(1)} %collective-permute-done.25.refs_0_), channel_id=1, source_target_pairs={{0,1},{1,0},{2,3},{3,2},{4,5},{5,4},{6,7},{7,6},{8,9},{9,8},{10,11... | collective-permute-start | bytes 1671176 | tf_op jit(solution)/shard_map/ppermute | solution.py:41
  119.9 2.3 %projection_grad.6.refs_1_ = f32[2,256,1024]{2,1,0:T(8,128)S(1)} custom-call(s32[4]{0:T(128)S(1)} %pad_add_fusion.where, bf16[4096,1024]{1,0:T(8,128)(2,1)S(1)} %copy-done.1, bf16[4,272,256]{2,1,0:T(8,128)(2,1)S(1)} %collective-permute-done.25.refs_0_, bf16[4,272,256]{2,1,0:T(8,128)(2,1)S(1)} %collective-permute-done.30.refs_1_, ...), custom_call_target="tpu_custom_call" | custom-call | flops 1610612736 | bytes 7864320 | tf_op jit(solution)/shard_map/projection_grad/pallas_call | solution.py:425
  122.2 2.2 %projection_grad.7 = (bf16[512,1024]{1,0:T(8,128)(2,1)}, f32[1,1024]{1,0:T(1,128)}) custom-call(s32[4]{0:T(128)S(1)} %pad_add_fusion.where, bf16[4096,1024]{1,0:T(8,128)(2,1)S(1)} %copy-done.1, bf16[4,272,256]{2,1,0:T(8,128)(2,1)S(1)} %collective-permute-done.29.refs_0_, f32[2,256,1024]{2,1,0:T(8,128)S(1)} %projection_grad.6.refs_1_, ...), custom_call_target="tpu_custom_call" | custom-call | flops 536870912 | bytes 2621440 | tf_op jit(solution)/shard_map/projection_grad/pallas_call | solution.py:425
  (77 shorter events, 4.1 us)
Async XLA Ops:
  7.2 98.3 %all-gather.2.cloned.1.call-start = ((), (), s32[]{:S(2)}) async-start(), calls=%async_computation | async-start | bytes 8912896 | tf_op jit(solution)/shard_map/all_gather | solution.py:487
  8.0 1.0 copy-start.2
  9.1 8.8 %copy-start.9 = (s32[4]{0:T(128)S(1)}, s32[4]{0:T(128)}, u32[]{:S(2)}) copy-start(s32[4]{0:T(128)} %param.16) | copy-start | bytes 52
  9.1 8.8 %copy-start.10 = (s32[1,4]{1,0:T(1,128)S(1)}, s32[1,4]{1,0:T(1,128)}, u32[]{:S(2)}) copy-start(s32[1,4]{1,0:T(1,128)} %param.17) | copy-start | bytes 52
  9.1 9.0 %copy-start.8 = (s32[4]{0:T(128)S(1)}, s32[4]{0:T(128)}, u32[]{:S(2)}) copy-start(s32[4]{0:T(128)} %param.15) | copy-start | bytes 52
  9.1 12.9 %copy-start.7 = (f32[4]{0:T(128)S(1)}, f32[4]{0:T(128)}, u32[]{:S(2)}) copy-start(f32[4]{0:T(128)} %param.14) | copy-start | bytes 52
  9.1 13.0 %copy-start.3 = (bf16[256,1024]{1,0:T(8,128)(2,1)S(1)}, bf16[256,1024]{1,0:T(8,128)(2,1)}, u32[]{:S(2)}) copy-start(bf16[256,1024]{1,0:T(8,128)(2,1)} %att.5) | copy-start | bytes 1572868
  15.9 3.2 %collective-permute-start = (bf16[256,1024]{1,0:T(8,128)(2,1)}, bf16[256,1024]{1,0:T(8,128)(2,1)S(1)}, u32[]{:S(2)}, u32[]{:S(2)}) collective-permute-start(bf16[256,1024]{1,0:T(8,128)(2,1)} %get-tuple-element.42), channel_id=1, source_target_pairs={{0,1},{1,0},{2,3},{3,2},{4,5},{5,4},{6,7},{7,6},{8,9},{9,8},{10,11... | collective-permute-start | bytes 1572872 | tf_op jit(solution)/shard_map/ppermute | solution.py:41
  17.4 4.7 %collective-permute-start.1 = (bf16[256,1024]{1,0:T(8,128)(2,1)}, bf16[256,1024]{1,0:T(8,128)(2,1)S(1)}, u32[]{:S(2)}, u32[]{:S(2)}) collective-permute-start(bf16[256,1024]{1,0:T(8,128)(2,1)} %get-tuple-element.46), channel_id=1, source_target_pairs={{0,1},{1,0},{2,3},{3,2},{4,5},{5,4},{6,7},{7,6},{8,9},{9,8},{10,11... | collective-permute-start | bytes 1572872 | tf_op jit(solution)/shard_map/ppermute | solution.py:41
  17.5 4.6 %collective-permute-start.2 = (bf16[256,1024]{1,0:T(8,128)(2,1)}, bf16[256,1024]{1,0:T(8,128)(2,1)S(1)}, u32[]{:S(2)}, u32[]{:S(2)}) collective-permute-start(bf16[256,1024]{1,0:T(8,128)(2,1)} %get-tuple-element.47), channel_id=1, source_target_pairs={{0,1},{1,0},{2,3},{3,2},{4,5},{5,4},{6,7},{7,6},{8,9},{9,8},{10,11... | collective-permute-start | bytes 1572872 | tf_op jit(solution)/shard_map/ppermute | solution.py:41
  19.2 9.8 %collective-permute-start.5 = (bf16[128,1024]{1,0:T(8,128)(2,1)S(1)}, bf16[128,1024]{1,0:T(8,128)(2,1)S(1)}, u32[]{:S(2)}, u32[]{:S(2)}) collective-permute-start(bf16[128,1024]{1,0:T(8,128)(2,1)S(1)} %get-tuple-element.43), channel_id=1, source_target_pairs={{0,2},{1,3},{2,4},{3,5},{4,6},{5,7},{6,0},{7,1},{8,10},{9,11},{10,... | collective-permute-start | bytes 786440 | tf_op jit(solution)/shard_map/ppermute | solution.py:493
  20.6 8.7 %collective-permute-start.3 = (bf16[128,1024]{1,0:T(8,128)(2,1)S(1)}, bf16[128,1024]{1,0:T(8,128)(2,1)S(1)}, u32[]{:S(2)}, u32[]{:S(2)}) collective-permute-start(bf16[128,1024]{1,0:T(8,128)(2,1)S(1)} %get-tuple-element.44), channel_id=1, source_target_pairs={{0,6},{1,7},{2,0},{3,1},{4,2},{5,3},{6,4},{7,5},{8,14},{9,15},{10,... | collective-permute-start | bytes 786440 | tf_op jit(solution)/shard_map/ppermute | solution.py:494
  28.0 4.0 %copy-start.6 = (bf16[1024]{0:T(1024)(128)(2,1)S(1)}, bf16[1024]{0:T(1024)(128)(2,1)}, u32[]{:S(2)}) copy-start(bf16[1024]{0:T(1024)(128)(2,1)} %param.12) | copy-start | bytes 6148
  28.1 12.7 %collective-permute-start.4 = (bf16[256,1024]{1,0:T(8,128)(2,1)}, bf16[256,1024]{1,0:T(8,128)(2,1)S(1)}, u32[]{:S(2)}, u32[]{:S(2)}) collective-permute-start(bf16[256,1024]{1,0:T(8,128)(2,1)} %get-tuple-element.50), channel_id=1, source_target_pairs={{0,1},{1,0},{2,3},{3,2},{4,5},{5,4},{6,7},{7,6},{8,9},{9,8},{10,11... | collective-permute-start | bytes 1572872 | tf_op jit(solution)/shard_map/ppermute | solution.py:41
  29.1 14.7 %collective-permute-start.6 = (bf16[256,1024]{1,0:T(8,128)(2,1)S(1)}, bf16[256,1024]{1,0:T(8,128)(2,1)S(1)}, u32[]{:S(2)}, u32[]{:S(2)}) collective-permute-start(bf16[256,1024]{1,0:T(8,128)(2,1)S(1)} %passed.3), channel_id=1, source_target_pairs={{0,2},{1,3},{2,4},{3,5},{4,6},{5,7},{6,0},{7,1},{8,10},{9,11},{10,... | collective-permute-start | bytes 1572872 | tf_op jit(solution)/shard_map/ppermute | solution.py:505
  29.4 14.5 %collective-permute-start.7 = (bf16[256,1024]{1,0:T(8,128)(2,1)S(1)}, bf16[256,1024]{1,0:T(8,128)(2,1)S(1)}, u32[]{:S(2)}, u32[]{:S(2)}) collective-permute-start(bf16[256,1024]{1,0:T(8,128)(2,1)S(1)} %passed.2), channel_id=1, source_target_pairs={{0,6},{1,7},{2,0},{3,1},{4,2},{5,3},{6,4},{7,5},{8,14},{9,15},{10,... | collective-permute-start | bytes 1572872 | tf_op jit(solution)/shard_map/ppermute | solution.py:509
  33.6 10.3 %copy-start.4 = (bf16[256,1024]{1,0:T(8,128)(2,1)S(1)}, bf16[256,1024]{1,0:T(8,128)(2,1)}, u32[]{:S(2)}) copy-start(bf16[256,1024]{1,0:T(8,128)(2,1)} %cot.3) | copy-start | bytes 1572868
  33.6 10.3 %copy-start.5 = (bf16[256,1024]{1,0:T(8,128)(2,1)S(1)}, bf16[256,1024]{1,0:T(8,128)(2,1)}, u32[]{:S(2)}) copy-start(bf16[256,1024]{1,0:T(8,128)(2,1)} %residual) | copy-start | bytes 1572868
  33.6 10.3 %collective-permute-start.8 = (f32[1,128]{1,0:T(1,128)S(1)}, f32[1,128]{1,0:T(1,128)S(1)}, u32[]{:S(2)}, u32[]{:S(2)}) collective-permute-start(f32[1,128]{1,0:T(1,128)S(1)} %bitcast.28), channel_id=1, source_target_pairs={{0,0},{1,17},{2,34},{3,51},{4,68},{5,85},{6,102},{7,119},{8,8},{9,... | collective-permute-start | bytes 1544 | tf_op jit(solution)/shard_map/ppermute | solution.py:514
  38.6 5.3 %collective-permute-start.9 = (f32[1,128]{1,0:T(1,128)S(1)}, f32[1,128]{1,0:T(1,128)S(1)}, u32[]{:S(2)}, u32[]{:S(2)}) collective-permute-start(f32[1,128]{1,0:T(1,128)S(1)} %bitcast.29), channel_id=1, source_target_pairs={{0,8},{1,25},{2,42},{3,59},{4,76},{5,93},{6,110},{7,127},{8,16},{9... | collective-permute-start | bytes 1544 | tf_op jit(solution)/shard_map/ppermute | solution.py:514
  44.5 1.8 %collective-permute-start.10 = (f32[8,256]{1,0:T(8,128)S(1)}, f32[8,256]{1,0:T(8,128)S(1)}, u32[]{:S(2)}, u32[]{:S(2)}) collective-permute-start(f32[8,256]{1,0:T(8,128)S(1)} %get-tuple-element.55), channel_id=1, source_target_pairs={{0,1},{1,0},{2,3},{3,2},{4,5},{5,4},{6,7},{7,6},{8,9},{9,8},{10,11... | collective-permute-start | bytes 24584 | tf_op jit(solution)/shard_map/ppermute | solution.py:41
  46.2 4.3 %collective-permute-start.11 = (f32[8,256]{1,0:T(8,128)S(1)}, f32[8,256]{1,0:T(8,128)S(1)}, u32[]{:S(2)}, u32[]{:S(2)}) collective-permute-start(f32[8,256]{1,0:T(8,128)S(1)} %add.23.s0), channel_id=1, source_target_pairs={{0,4},{1,5},{2,6},{3,7},{4,0},{5,1},{6,2},{7,3},{8,12},{9,13},{10,... | collective-permute-start | bytes 24584 | tf_op jit(solution)/shard_map/ppermute | solution.py:524
  47.9 4.1 %collective-permute-start.12 = (f32[8,256]{1,0:T(8,128)S(1)}, f32[8,256]{1,0:T(8,128)S(1)}, u32[]{:S(2)}, u32[]{:S(2)}) collective-permute-start(f32[8,256]{1,0:T(8,128)S(1)} %add.23.s0), channel_id=1, source_target_pairs={{0,2},{1,3},{2,4},{3,5},{4,6},{5,7},{6,0},{7,1},{8,10},{9,11},{10,... | collective-permute-start | bytes 24584 | tf_op jit(solution)/shard_map/ppermute | solution.py:524
  49.6 2.9 %collective-permute-start.13 = (f32[8,256]{1,0:T(8,128)S(1)}, f32[8,256]{1,0:T(8,128)S(1)}, u32[]{:S(2)}, u32[]{:S(2)}) collective-permute-start(f32[8,256]{1,0:T(8,128)S(1)} %add.23.s0), channel_id=1, source_target_pairs={{0,6},{1,7},{2,0},{3,1},{4,2},{5,3},{6,4},{7,5},{8,14},{9,15},{10,... | collective-permute-start | bytes 24584 | tf_op jit(solution)/shard_map/ppermute | solution.py:524
  54.0 13.1 %collective-permute-start.15 = (bf16[256,1024]{1,0:T(8,128)(2,1)S(1)}, bf16[256,1024]{1,0:T(8,128)(2,1)S(1)}, u32[]{:S(2)}, u32[]{:S(2)}) collective-permute-start(bf16[256,1024]{1,0:T(8,128)(2,1)S(1)} %get-tuple-element.57.refs_0_), channel_id=1, source_target_pairs={{0,2},{1,3},{2,4},{3,5},{4,6},{5,7},{6,0},{7,1},{8,10},{9,11},{10,... | collective-permute-start | bytes 1572872 | tf_op jit(solution)/shard_map/ppermute | solution.py:530
  54.0 13.2 %collective-permute-start.18 = (bf16[256,1024]{1,0:T(8,128)(2,1)S(1)}, bf16[256,1024]{1,0:T(8,128)(2,1)S(1)}, u32[]{:S(2)}, u32[]{:S(2)}) collective-permute-start(bf16[256,1024]{1,0:T(8,128)(2,1)S(1)} %get-tuple-element.57.refs_0_), channel_id=1, source_target_pairs={{0,6},{1,7},{2,0},{3,1},{4,2},{5,3},{6,4},{7,5},{8,14},{9,15},{10,... | collective-permute-start | bytes 1572872 | tf_op jit(solution)/shard_map/ppermute | solution.py:530
  67.1 6.9 %collective-permute-start.17 = (bf16[128,1024]{1,0:T(8,128)(2,1)S(1)}, bf16[128,1024]{1,0:T(8,128)(2,1)S(1)}, u32[]{:S(2)}, u32[]{:S(2)}) collective-permute-start(bf16[128,1024]{1,0:T(8,128)(2,1)S(1)} %slice.40), channel_id=1, source_target_pairs={{0,2},{1,3},{2,4},{3,5},{4,6},{5,7},{6,0},{7,1},{8,10},{9,11},{10,... | collective-permute-start | bytes 786440 | tf_op jit(solution)/shard_map/ppermute | solution.py:531
  67.2 6.8 %collective-permute-start.19 = (bf16[128,1024]{1,0:T(8,128)(2,1)S(1)}, bf16[128,1024]{1,0:T(8,128)(2,1)S(1)}, u32[]{:S(2)}, u32[]{:S(2)}) collective-permute-start(bf16[128,1024]{1,0:T(8,128)(2,1)S(1)} %slice.41), channel_id=1, source_target_pairs={{0,6},{1,7},{2,0},{3,1},{4,2},{5,3},{6,4},{7,5},{8,14},{9,15},{10,... | collective-permute-start | bytes 786440 | tf_op jit(solution)/shard_map/ppermute | solution.py:532
  69.9 7.4 %collective-permute-start.14 = (bf16[256,1024]{1,0:T(8,128)(2,1)S(1)}, bf16[256,1024]{1,0:T(8,128)(2,1)S(1)}, u32[]{:S(2)}, u32[]{:S(2)}) collective-permute-start(bf16[256,1024]{1,0:T(8,128)(2,1)S(1)} %get-tuple-element.57.refs_0_), channel_id=1, source_target_pairs={{0,1},{1,0},{2,3},{3,2},{4,5},{5,4},{6,7},{7,6},{8,9},{9,8},{10,11... | collective-permute-start | bytes 1572872 | tf_op jit(solution)/shard_map/ppermute | solution.py:41
  73.0 4.4 %collective-permute-start.16 = (bf16[256,1024]{1,0:T(8,128)(2,1)S(1)}, bf16[256,1024]{1,0:T(8,128)(2,1)S(1)}, u32[]{:S(2)}, u32[]{:S(2)}) collective-permute-start(bf16[256,1024]{1,0:T(8,128)(2,1)S(1)} %collective-permute-done.15.refs_2_), channel_id=1, source_target_pairs={{0,1},{1,0},{2,3},{3,2},{4,5},{5,4},{6,7},{7,6},{8,9},{9,8},{10,11... | collective-permute-start | bytes 1572872 | tf_op jit(solution)/shard_map/ppermute | solution.py:41
  73.0 4.4 %collective-permute-start.21 = (bf16[256,1024]{1,0:T(8,128)(2,1)S(1)}, bf16[256,1024]{1,0:T(8,128)(2,1)S(1)}, u32[]{:S(2)}, u32[]{:S(2)}) collective-permute-start(bf16[256,1024]{1,0:T(8,128)(2,1)S(1)} %collective-permute-done.18.refs_6_), channel_id=1, source_target_pairs={{0,1},{1,0},{2,3},{3,2},{4,5},{5,4},{6,7},{7,6},{8,9},{9,8},{10,11... | collective-permute-start | bytes 1572872 | tf_op jit(solution)/shard_map/ppermute | solution.py:41
  74.0 4.8 %collective-permute-start.20 = (bf16[256,1024]{1,0:T(8,128)(2,1)S(1)}, bf16[256,1024]{1,0:T(8,128)(2,1)S(1)}, u32[]{:S(2)}, u32[]{:S(2)}) collective-permute-start(bf16[256,1024]{1,0:T(8,128)(2,1)S(1)} %joined.1.refs_4_), channel_id=1, source_target_pairs={{0,1},{1,0},{2,3},{3,2},{4,5},{5,4},{6,7},{7,6},{8,9},{9,8},{10,11... | collective-permute-start | bytes 1572872 | tf_op jit(solution)/shard_map/ppermute | solution.py:41
  80.4 13.1 %collective-permute-start.22 = (bf16[4,272,256]{2,1,0:T(8,128)(2,1)S(1)}, bf16[4,272,256]{2,1,0:T(8,128)(2,1)S(1)}, u32[]{:S(2)}, u32[]{:S(2)}) collective-permute-start(bf16[4,272,256]{2,1,0:T(8,128)(2,1)S(1)} %get-tuple-element.60), channel_id=1, source_target_pairs={{0,32},{1,9},{2,34},{3,11},{4,36},{5,13},{6,38},{7,15},{8,40},{9,1... | collective-permute-start | bytes 1671176 | tf_op jit(solution)/shard_map/ppermute | solution.py:541
  81.8 15.8 %collective-permute-start.23 = (bf16[4,272,256]{2,1,0:T(8,128)(2,1)S(1)}, bf16[4,272,256]{2,1,0:T(8,128)(2,1)S(1)}, u32[]{:S(2)}, u32[]{:S(2)}) collective-permute-start(bf16[4,272,256]{2,1,0:T(8,128)(2,1)S(1)} %get-tuple-element.61), channel_id=1, source_target_pairs={{0,64},{1,17},{2,66},{3,19},{4,68},{5,21},{6,70},{7,23},{8,72},{9,... | collective-permute-start | bytes 1671176 | tf_op jit(solution)/shard_map/ppermute | solution.py:541
  84.4 13.2 %collective-permute-start.24 = (bf16[4,272,256]{2,1,0:T(8,128)(2,1)S(1)}, bf16[4,272,256]{2,1,0:T(8,128)(2,1)S(1)}, u32[]{:S(2)}, u32[]{:S(2)}) collective-permute-start(bf16[4,272,256]{2,1,0:T(8,128)(2,1)S(1)} %get-tuple-element.62), channel_id=1, source_target_pairs={{0,96},{1,25},{2,98},{3,27},{4,100},{5,29},{6,102},{7,31},{8,104},... | collective-permute-start | bytes 1671176 | tf_op jit(solution)/shard_map/ppermute | solution.py:541
  99.4 6.0 %collective-permute-start.27 = (bf16[4,272,256]{2,1,0:T(8,128)(2,1)S(1)}, bf16[4,272,256]{2,1,0:T(8,128)(2,1)S(1)}, u32[]{:S(2)}, u32[]{:S(2)}) collective-permute-start(bf16[4,272,256]{2,1,0:T(8,128)(2,1)S(1)} %get-tuple-element.67.refs_0_), channel_id=1, source_target_pairs={{0,1},{1,0},{2,3},{3,2},{4,5},{5,4},{6,7},{7,6},{8,9},{9,8},{10,11... | collective-permute-start | bytes 1671176 | tf_op jit(solution)/shard_map/ppermute | solution.py:41
  101.7 10.1 %collective-permute-start.26 = (bf16[4,272,256]{2,1,0:T(8,128)(2,1)}, bf16[4,272,256]{2,1,0:T(8,128)(2,1)S(1)}, u32[]{:S(2)}, u32[]{:S(2)}) collective-permute-start(bf16[4,272,256]{2,1,0:T(8,128)(2,1)} %get-tuple-element.66), channel_id=1, source_target_pairs={{0,8},{1,33},{2,10},{3,35},{4,12},{5,37},{6,14},{7,39},{8,16},{9,4... | collective-permute-start | bytes 1671176 | tf_op jit(solution)/shard_map/ppermute | solution.py:549
  103.0 8.9 %collective-permute-start.28 = (bf16[4,272,256]{2,1,0:T(8,128)(2,1)}, bf16[4,272,256]{2,1,0:T(8,128)(2,1)S(1)}, u32[]{:S(2)}, u32[]{:S(2)}) collective-permute-start(bf16[4,272,256]{2,1,0:T(8,128)(2,1)} %get-tuple-element.69), channel_id=1, source_target_pairs={{0,24},{1,97},{2,26},{3,99},{4,28},{5,101},{6,30},{7,103},{8,0},{9... | collective-permute-start | bytes 1671176 | tf_op jit(solution)/shard_map/ppermute | solution.py:549
  104.4 13.8 %collective-permute-start.25 = (bf16[4,272,256]{2,1,0:T(8,128)(2,1)}, bf16[4,272,256]{2,1,0:T(8,128)(2,1)S(1)}, u32[]{:S(2)}, u32[]{:S(2)}) collective-permute-start(bf16[4,272,256]{2,1,0:T(8,128)(2,1)} %get-tuple-element.65), channel_id=1, source_target_pairs={{0,16},{1,65},{2,18},{3,67},{4,20},{5,69},{6,22},{7,71},{8,24},{9,... | collective-permute-start | bytes 1671176 | tf_op jit(solution)/shard_map/ppermute | solution.py:549
  105.5 3.4 %copy-start = (bf16[4096,1024]{1,0:T(8,128)(2,1)S(1)}, bf16[4096,1024]{1,0:T(8,128)(2,1)}, u32[]{:S(2)}) copy-start(bf16[4096,1024]{1,0:T(8,128)(2,1)} %all-gather.2.cloned.1.call-done.gathered) | copy-start | bytes 25165828
  108.8 4.2 %copy-start.1 = (bf16[4096,1024]{1,0:T(8,128)(2,1)S(1)}, bf16[4096,1024]{1,0:T(8,128)(2,1)}, u32[]{:S(2)}) copy-start(bf16[4096,1024]{1,0:T(8,128)(2,1)} %all-gather.2.cloned.1.call-done.gathered) | copy-start | bytes 25165828
  111.8 8.0 %collective-permute-start.31 = (bf16[4,272,256]{2,1,0:T(8,128)(2,1)S(1)}, bf16[4,272,256]{2,1,0:T(8,128)(2,1)S(1)}, u32[]{:S(2)}, u32[]{:S(2)}) collective-permute-start(bf16[4,272,256]{2,1,0:T(8,128)(2,1)S(1)} %collective-permute-done.28.refs_1_), channel_id=1, source_target_pairs={{0,1},{1,0},{2,3},{3,2},{4,5},{5,4},{6,7},{7,6},{8,9},{9,8},{10,11... | collective-permute-start | bytes 1671176 | tf_op jit(solution)/shard_map/ppermute | solution.py:41
  113.0 6.8 %collective-permute-start.30 = (bf16[4,272,256]{2,1,0:T(8,128)(2,1)S(1)}, bf16[4,272,256]{2,1,0:T(8,128)(2,1)S(1)}, u32[]{:S(2)}, u32[]{:S(2)}) collective-permute-start(bf16[4,272,256]{2,1,0:T(8,128)(2,1)S(1)} %collective-permute-done.26.refs_0_), channel_id=1, source_target_pairs={{0,1},{1,0},{2,3},{3,2},{4,5},{5,4},{6,7},{7,6},{8,9},{9,8},{10,11... | collective-permute-start | bytes 1671176 | tf_op jit(solution)/shard_map/ppermute | solution.py:41
  118.2 4.1 %collective-permute-start.29 = (bf16[4,272,256]{2,1,0:T(8,128)(2,1)S(1)}, bf16[4,272,256]{2,1,0:T(8,128)(2,1)S(1)}, u32[]{:S(2)}, u32[]{:S(2)}) collective-permute-start(bf16[4,272,256]{2,1,0:T(8,128)(2,1)S(1)} %collective-permute-done.25.refs_0_), channel_id=1, source_target_pairs={{0,1},{1,0},{2,3},{3,2},{4,5},{5,4},{6,7},{7,6},{8,9},{9,8},{10,11... | collective-permute-start | bytes 1671176 | tf_op jit(solution)/shard_map/ppermute | solution.py:41
Sparse Core Ops, SparseCore 0:
  10.1 74.1 all-gather.1
